TPU v7x, 32 devices: a whole 2x2x4 slice. The times are simulated.
32 devices in a mesh: dp: 4 (over y, core), tm: 8 (over z, x).
Axes of the slice: x: 2, y: 2, z: 4, core: 2. Of those that a mesh axis runs over, the one named last changes fastest.
Arguments:
- frames: bfloat16 [8192, 1536], P(('dp', 'tm')), may hold values from -28 to 28, as said below
- seg: int32 [4, 2048], P('dp'), may hold values from 0 to 3, never falling along the last dimension, each value on 1 to 1024 neighbouring positions
- look_back: int32 [4, 8], P('dp'), may hold values 0 or 1
- w_dw: float32 [5, 1536], replicated, may hold values from -2.5 to 2.5
- w_qkv: bfloat16 [1536, 4608], P(None, 'dp'), may hold values from -0.15625 to 0.15625
- w_o: bfloat16 [1536, 1536], replicated, may hold values from -1.5 to 1.5
- cotangent: bfloat16 [8192, 1536], P(('dp', 'tm')), may hold values from -0.23925781 to 0.23925781
Outputs:
- mixed: bfloat16 [8192, 1536], P(('dp', 'tm'))
- weight_grad: float32 [1536, 1536], P('tm', 'dp')
Inputs may be any that keep to these rules, and one draw needn't show every extreme that they name: Float features; a few short runs of frames may be several times larger than the rest. `seg`: recording numbers never fall along a replica's frames; each recording has 1 to 1024 frames, one exactly 1024.
All inputs are finite; a program needn't handle non-finite values. No bound on the sum of `look_back` on one device may be relied on, other than what follows from the above.
Results may differ from a plain program's by a relative error of at most 0.012.
The roundings to bfloat16 on the way count: a program that leaves them out, or rounds other values in their place, can miss the bound.
Values may be sent and summed in bfloat16 or wider, within the bound.
No kernel may reach another device: no remote copies, remote signals or barrier semaphores. Data moves between devices by JAX's collectives and lax.ppermute only.
A program may use at most 128 MiB of HBM per device.

v0:
```python
import math

import jax
import jax.numpy as jnp
from jax import lax
from jax.sharding import PartitionSpec as P

KER = 5
HDIM = 96
STRETCH = 256


def extended(block, sides, width):
    for axis, dim in sides:
        count = lax.axis_size(axis)
        forward = [(i, i + 1) for i in range(count - 1)]
        backward = [(target, source) for source, target in forward]
        low = lax.ppermute(
            lax.slice_in_dim(block, block.shape[dim] - width, None, axis=dim), axis, forward
        )
        high = lax.ppermute(lax.slice_in_dim(block, 0, width, axis=dim), axis, backward)
        block = jnp.concatenate([low, block, high], axis=dim)
    return block


def swapped(block, axis, distance):
    count = lax.axis_size(axis)
    route = []
    for low in range(count):
        high = low | 1 << distance
        if high != low and high < count:
            route += [(low, high), (high, low)]
    return lax.ppermute(block, axis, route)


def stretch_attention(queries, keys, values, seg_row, look_row, stretch):
    frame_count, heads_here, head_dim = queries.shape
    value_dim = values.shape[2]
    blocks = frame_count // stretch
    query_blocks = queries.reshape(blocks, stretch, heads_here, head_dim)
    key_blocks = keys.reshape(blocks, stretch, heads_here, head_dim)
    value_blocks = values.reshape(blocks, stretch, heads_here, value_dim)
    key_pairs = jnp.concatenate(
        [jnp.concatenate([jnp.zeros_like(key_blocks[:1]), key_blocks[:-1]], 0), key_blocks], 1
    )
    value_pairs = jnp.concatenate(
        [jnp.concatenate([jnp.zeros_like(value_blocks[:1]), value_blocks[:-1]], 0), value_blocks], 1
    )
    seg_blocks = seg_row.reshape(blocks, stretch)
    seg_pairs = jnp.concatenate(
        [jnp.concatenate([jnp.full((1, stretch), -1, jnp.int32), seg_blocks[:-1]], 0), seg_blocks],
        1,
    )
    allow_prev = look_row == 1
    per_step = math.gcd(blocks, max(1, 512 // stretch))
    current = jnp.arange(2 * stretch) >= stretch
    scale = 1.0 / math.sqrt(head_dim)

    def block_step(block_index):
        start = block_index * per_step

        def pick_rows(array):
            return lax.dynamic_slice_in_dim(array, start, per_step, 0)

        scores = (
            jnp.einsum(
                "gqhd,gkhd->ghqk",
                pick_rows(query_blocks),
                pick_rows(key_pairs),
                preferred_element_type=jnp.float32,
            )
            * scale
        )
        same_rec = pick_rows(seg_pairs)[:, None, :] == pick_rows(seg_blocks)[:, :, None]
        allowed = same_rec & (current[None, None, :] | pick_rows(allow_prev)[:, None, None])
        scores = jnp.where(allowed[:, None], scores, -1e30)
        row_max = jnp.max(scores, axis=-1, keepdims=True)
        raw_weights = jnp.exp(scores - row_max)
        probs = (raw_weights / jnp.sum(raw_weights, axis=-1, keepdims=True)).astype(jnp.bfloat16)
        outputs = jnp.einsum(
            "ghqk,gkhv->gqhv", probs, pick_rows(value_pairs), preferred_element_type=jnp.float32
        )
        return outputs.astype(jnp.bfloat16).reshape(per_step * stretch, heads_here * value_dim)

    mixed = lax.map(block_step, jnp.arange(blocks // per_step, dtype=jnp.int32))
    return mixed.reshape(frame_count, heads_here * value_dim)


def local(frames, seg, look_back, w_dw, w_qkv, w_o, cotangent):
    rows = frames.shape[0]
    width = frames.shape[1]
    tm_count = lax.axis_size("tm")
    piece = width // tm_count
    half = KER // 2
    padded = extended(frames, (("tm", 0),), half)
    seg_row = seg[0]
    look_row = look_back[0]
    seg_padded = jnp.pad(seg_row, (half, half), constant_values=-1)
    local_seg = lax.dynamic_slice_in_dim(
        seg_padded, lax.axis_index("tm") * rows, rows + 2 * half, 0
    )
    own_seg = local_seg[half : half + rows]
    total = jnp.zeros((rows, width), jnp.float32)
    for offset in range(KER):
        same_rec = (local_seg[offset : offset + rows] == own_seg).astype(jnp.float32)
        total = (
            total
            + w_dw[offset] * padded[offset : offset + rows].astype(jnp.float32) * same_rec[:, None]
        )
    activ = jax.nn.silu(total).astype(jnp.bfloat16)
    qkv = jnp.dot(
        activ, lax.all_gather(w_qkv, "dp", axis=1, tiled=True), preferred_element_type=jnp.float32
    ).astype(jnp.bfloat16)
    arranged = qkv.reshape(rows, 3, tm_count, piece)
    arrived = lax.all_to_all(arranged, "tm", split_axis=2, concat_axis=0, tiled=True)
    frame_count = arrived.shape[0]
    if piece < HDIM:
        lower = lax.axis_index("tm") % 2 == 0
        own_pair = arrived[:, 0:2, 0, :]
        other_pair = swapped(own_pair, "tm", 0)
        joined = jnp.where(
            lower,
            jnp.concatenate([own_pair, other_pair], -1),
            jnp.concatenate([other_pair, own_pair], -1),
        )
        queries = joined[:, 0][:, None, :]
        keys = joined[:, 1][:, None, :]
        values = arrived[:, 2, 0, :][:, None, :]
        attended = stretch_attention(queries, keys, values, seg_row, look_row, STRETCH)
    else:
        heads_here = piece // HDIM
        queries = arrived[:, 0, 0, :].reshape(frame_count, heads_here, HDIM)
        keys = arrived[:, 1, 0, :].reshape(frame_count, heads_here, HDIM)
        values = arrived[:, 2, 0, :].reshape(frame_count, heads_here, HDIM)
        attended = stretch_attention(queries, keys, values, seg_row, look_row, STRETCH)
    returned = lax.all_to_all(
        attended.reshape(frame_count, 1, piece), "tm", split_axis=0, concat_axis=1, tiled=True
    )
    attn = returned.reshape(rows, width)
    mixed = jnp.dot(attn, w_o, preferred_element_type=jnp.float32).astype(jnp.bfloat16)
    grad_term = lax.dot_general(
        attn, cotangent, (((0,), (0,)), ((), ())), preferred_element_type=jnp.float32
    )
    row_share = lax.psum_scatter(grad_term, "tm", scatter_dimension=0, tiled=True)
    weight_grad = lax.psum_scatter(row_share, "dp", scatter_dimension=1, tiled=True)
    return (mixed, weight_grad)


def solution(mesh):
    placed = (
        P(("dp", "tm"), None),
        P("dp", None),
        P("dp", None),
        P(),
        P(None, "dp"),
        P(),
        P(("dp", "tm"), None),
    )
    return jax.shard_map(
        local,
        mesh=mesh,
        in_specs=placed,
        out_specs=(P(("dp", "tm"), None), P("tm", "dp")),
        check_vma=False,
    )
```

profile of v0, /device:TPU:0, one launch (start us, length us, event | category | flops | bytes accessed | tf_op | source)
XLA Modules:
  0.0 499.9 jit_solution(6617299900685329578)
XLA Ops:
  9.7 5.5 %collective-permute-start = (bf16[2,1536]{1,0:T(2,128)(2,1)S(1)}, bf16[2,1536]{1,0:T(2,128)(2,1)S(1)}, u32[]{:S(2)}, u32[]{:S(2)}) collective-permute-start(bf16[2,1536]{1,0:T(2,128)(2,1)S(1)} %get-tuple-element.135), channel_id=1, source_target_pairs={{0,1},{1,2},{2,3},{3,4},{4,5},{5,6},{6,7},{8,9},{9,10},{10,11},{11... | collective-permute-start | bytes 18440 | tf_op jit(solution)/shard_map/ppermute | solution.py:18
  16.5 86.8 %all-gather.2.cloned.1.call-done = bf16[1536,4608]{1,0:T(8,128)(2,1)} async-done(((bf16[1536,1152]{1,0:T(8,128)(2,1)}), bf16[1536,4608]{1,0:T(8,128)(2,1)}) %all-gather.2.cloned.1.call-update) | async-done | bytes 14155792 | tf_op jit(solution)/shard_map/all_gather | solution.py:112
  103.3 11.5 %convolution_convert_fusion.1 = bf16[256,4608]{1,0:T(8,128)(2,1)} fusion(bf16[1536,4608]{1,0:T(8,128)(2,1)} %all-gather.2.cloned.1.call-done, bf16[256,1536]{1,0:T(8,128)(2,1)S(1)} %copy-done.3, bf16[2,1536]{1,0:T(2,128)(2,1)S(1)} %collective-permute-done, bf16[258,1536]{1,0:T(8,128)(2,1)S(1)} %constant_dynamic-update-slice_fusion.1, ...), kind=kOutput, calls=%fused_computation.26 | convolution fusion | flops 3636461568 | bytes 18925568 | tf_op jit(solution)/shard_map/dot_general | solution.py:111
  114.8 2.8 copy.24
  119.2 5.6 %all-to-all-start = ((bf16[256,3,8,192]{0,3,1,2:T(8,128)(2,1)}), bf16[256,3,8,192]{0,3,1,2:T(8,128)(2,1)S(1)}, u32[]{:S(2)}, u32[]{:S(2)}) async-start(bf16[256,3,8,192]{0,3,1,2:T(8,128)(2,1)} %copy.25), calls=%async_computation | async-start | bytes 4718592 | tf_op jit(solution)/shard_map/all_to_all | solution.py:115
  126.4 52.8 %all-to-all-done = bf16[256,3,8,192]{0,3,1,2:T(8,128)(2,1)S(1)} async-done(((bf16[256,3,8,192]{0,3,1,2:T(8,128)(2,1)}), bf16[256,3,8,192]{0,3,1,2:T(8,128)(2,1)S(1)}, u32[]{:S(2)}, u32[]{:S(2)}) %all-to-all-start) | async-done | bytes 2359328 | tf_op jit(solution)/shard_map/all_to_all | solution.py:115
  182.2 2.5 slice.105
  184.7 2.5 slice.99
  188.9 2.8 fusion.28
  191.7 49.4 %while.11 = (s32[]{:T(128)}, bf16[4,512,192]{1,2,0:T(8,128)(2,1)}, s32[4]{0:T(128)S(1)}, bf16[8,512,2,96]{1,0,3,2:T(8,128)(2,1)S(1)}, s32[8,512]{1,0:T(8,128)S(1...) while((s32[]{:T(128)}, bf16[4,512,192]{1,2,0:T(8,128)(2,1)}, ...), condition=%wide.region_3.4_spmd.clone, body=%wide.region_0.3_spmd.clone.sunk | while | flops 205096960 | bytes 9074385 | solution.py:85
  193.4 2.2 constant_dynamic-slice_fusion.11
  197.6 3.2 fusion.69
  205.7 2.2 constant_dynamic-slice_fusion.11
  210.0 3.2 fusion.69
  213.2 2.1 fusion.70
  218.1 2.2 constant_dynamic-slice_fusion.11
  222.4 3.2 fusion.69
  225.6 2.1 fusion.70
  230.5 2.2 constant_dynamic-slice_fusion.11
  234.7 3.2 fusion.69
  238.0 2.1 fusion.70
  241.1 2.2 copy.34
  243.4 6.1 %reshape.60 = bf16[2048,1,192]{2,1,0:T(2,128)(2,1)S(1)} reshape(bf16[4,512,192]{2,1,0:T(8,128)(2,1)} %copy.34) | data formatting | bytes 1572864 | tf_op jit(solution)/shard_map/reshape;reshape | solution.py:137
  250.0 12.6 %reduce.16 = bf16[2048,192]{1,0:T(8,128)(2,1)} reduce(bf16[2048,1,192]{2,1,0:T(2,128)(2,1)S(1)} %reshape.60, bf16[]{:T(256)} %broadcast.95), dimensions={1}, to_apply=%reshape.60.reduce_sub_computation | reduce | bytes 1572866 | tf_op jit(solution)/shard_map/reshape;reshape | solution.py:137
  262.6 2.8 reshape.76
  265.4 23.8 %all_to_all.33 = bf16[8,2,24576]{2,1,0:T(2,128)(2,1)} all-to-all(bf16[8,2,24576]{2,1,0:T(2,128)(2,1)S(1)} %reshape.76), channel_id=1, replica_groups=mesh['dp'=4,'tm'=8] {'tm'}, dimensions={0} | all-to-all | bytes 1572864 | tf_op jit(solution)/shard_map/all_to_all | solution.py:136
  289.3 4.5 reshape.77
  293.8 3.3 copy.32
  298.6 5.0 %fusion.55 = f32[1536,1536]{1,0:T(8,128)} fusion(bf16[256,1536]{0,1:T(8,128)(2,1)S(1)} %bitcast.66, bf16[256,1536]{1,0:T(8,128)(2,1)S(1)} %copy-done), kind=kOutput, calls=%fused_computation.73 | convolution fusion | flops 1207959552 | bytes 11010048 | tf_op jit(solution)/shard_map/dot_general | solution.py:141
  303.7 161.7 %reduce-scatter.3.cloned.1.call-done = f32[192,1536]{1,0:T(8,128)} async-done(((f32[1536,1536]{1,0:T(8,128)}), f32[192,1536]{1,0:T(8,128)}) %reduce-scatter.3.cloned.1.call-update) | async-done | bytes 1179664 | tf_op jit(solution)/shard_map/reduce_scatter | solution.py:144
  465.4 4.6 convolution_convert_fusion.2
  470.0 23.4 %reduce-scatter.5.cloned.1.call-done = f32[192,384]{1,0:T(8,128)} async-done(((f32[192,1536]{1,0:T(8,128)}), f32[192,384]{1,0:T(8,128)}) %reduce-scatter.5.cloned.1.call-update) | async-done | bytes 294928 | tf_op jit(solution)/shard_map/reduce_scatter | solution.py:145
  (93 shorter events, 31.8 us)
Async XLA Ops:
  7.2 291.4 %copy-start = (bf16[256,1536]{1,0:T(8,128)(2,1)S(1)}, bf16[256,1536]{1,0:T(8,128)(2,1)}, u32[]{:S(2)}) copy-start(bf16[256,1536]{1,0:T(8,128)(2,1)} %param.15) | copy-start | bytes 2359300
  7.2 1.2 copy-start.3
  7.2 8.0 %copy-start.4 = (s32[1,2048]{1,0:T(1,128)S(1)}, s32[1,2048]{1,0:T(1,128)}, u32[]{:S(2)}) copy-start(s32[1,2048]{1,0:T(1,128)} %param.10) | copy-start | bytes 24580
  7.2 96.1 %all-gather.2.cloned.1.call-start = ((), (), s32[]{:S(2)}) async-start(), calls=%async_computation.4 | async-start | bytes 17694720 | tf_op jit(solution)/shard_map/all_gather | solution.py:112
  8.4 7.0 %copy-start.5 = (f32[5,1536]{1,0:T(8,128)S(1)}, f32[5,1536]{1,0:T(8,128)}, u32[]{:S(2)}) copy-start(f32[5,1536]{1,0:T(8,128)} %param.12) | copy-start | bytes 92164
  8.4 7.1 %collective-permute-start.1 = (bf16[2,1536]{1,0:T(2,128)(2,1)S(1)}, bf16[2,1536]{1,0:T(2,128)(2,1)S(1)}, u32[]{:S(2)}, u32[]{:S(2)}) collective-permute-start(bf16[2,1536]{1,0:T(2,128)(2,1)S(1)} %get-tuple-element.134), channel_id=1, source_target_pairs={{1,0},{2,1},{3,2},{4,3},{5,4},{6,5},{7,6},{9,8},{10,9},{11,10},{12... | collective-permute-start | bytes 18440 | tf_op jit(solution)/shard_map/ppermute | solution.py:21
  9.7 6.8 %collective-permute-start = (bf16[2,1536]{1,0:T(2,128)(2,1)S(1)}, bf16[2,1536]{1,0:T(2,128)(2,1)S(1)}, u32[]{:S(2)}, u32[]{:S(2)}) collective-permute-start(bf16[2,1536]{1,0:T(2,128)(2,1)S(1)} %get-tuple-element.135), channel_id=1, source_target_pairs={{0,1},{1,2},{2,3},{3,4},{4,5},{5,6},{6,7},{8,9},{9,10},{10,11},{11... | collective-permute-start | bytes 18440 | tf_op jit(solution)/shard_map/ppermute | solution.py:18
  119.2 7.1 %copy-start.6 = (s32[1,8]{1,0:T(1,128)S(1)}, s32[1,8]{1,0:T(1,128)}, u32[]{:S(2)}) copy-start(s32[1,8]{1,0:T(1,128)} %param.11) | copy-start | bytes 100
  119.2 59.9 %all-to-all-start = ((bf16[256,3,8,192]{0,3,1,2:T(8,128)(2,1)}), bf16[256,3,8,192]{0,3,1,2:T(8,128)(2,1)S(1)}, u32[]{:S(2)}, u32[]{:S(2)}) async-start(bf16[256,3,8,192]{0,3,1,2:T(8,128)(2,1)} %copy.25), calls=%async_computation | async-start | bytes 4718592 | tf_op jit(solution)/shard_map/all_to_all | solution.py:115
  124.9 340.5 %reduce-scatter.3.cloned.1.call-start = ((), (), s32[]{:S(2)}) async-start(), calls=%async_computation.5 | async-start | bytes 10616832 | tf_op jit(solution)/shard_map/reduce_scatter | solution.py:144
  187.2 1.2 copy-start.1
  187.2 1.7 copy-start.2
  303.6 189.8 %reduce-scatter.5.cloned.1.call-start = ((), (), s32[]{:S(2)}) async-start(), calls=%async_computation.6 | async-start | bytes 1474560 | tf_op jit(solution)/shard_map/reduce_scatter | solution.py:145
Sparse Core Ops, SparseCore 0:
  9.6 93.6 all-gather.1
  303.8 161.5 reduce-scatter.2
  468.5 24.8 reduce-scatter.4
where the time goes:
time: 501 us; the launch traced here: 500 us
  waiting for transfers between devices  326 us (65%)
  local copies, waits for them, and re-layouts  60.2 us (12%)
  matrix products  42.7 us (9%)
  blocking collectives  23.8 us (5%)
  other arithmetic  17.5 us (3%)
  between operations  14 us (3%)
  starting transfers between devices  12.7 us (3%)
    reduce_scatter x1, waiting for transfers between devices, local(): lax.psum_scatter(grad_term, 'tm', scatter_dimension=0, tiled=True)  162 us
    all_gather x1, waiting for transfers between devices, local(): lax.all_gather(w_qkv, 'dp', axis=1, tiled=True)  86.8 us
    all_to_all x1, waiting for transfers between devices, local(): lax.all_to_all(arranged, 'tm', split_axis=2, concat_axis=0, tiled=True)  52.8 us
    all_to_all x1, blocking collectives, local(): lax.all_to_all(attended.reshape(frame_count, 1, piece), 'tm', split_axis=...  23.8 us
    reduce_scatter x1, waiting for transfers between devices, local(): lax.psum_scatter(row_share, 'dp', scatter_dimension=1, tiled=True)  23.4 us
    dynamic_slice x20, local copies, waits for them, and re-layouts, pick_rows(): return lax.dynamic_slice_in_dim(array, start, per_step, 0)  17.4 us
    sub x4, matrix products, block_step(): raw_weights = jnp.exp(scores - row_max)  13 us
    unnamed x22, local copies, waits for them, and re-layouts  12.6 us
  transfers between devices with their start and end apart: 6, of which 5 were waited for; matrix products, arithmetic and copies ran while one was open for 1% of the time, Pallas kernels for 0%

commit v1 on v0

v1 whole, which is shorter than its diff:
```python
import math

import jax
import jax.numpy as jnp
from jax import lax
from jax.experimental import pallas as pl
from jax.experimental.pallas import tpu as pltpu
from jax.sharding import PartitionSpec as P

KER = 5
HDIM = 96
STRETCH = 256
GROUP = 4
COLS = GROUP * HDIM
EDGE = 16
MIB = 1 << 20
LITTLE = pl.CostEstimate(flops=10**6, bytes_accessed=10**4, transcendentals=0)

ORDERS = (
    ((0, 1, 2), (1, 2, 0), (2, 0, 1), (0, 1, 2)),
    ((2, 0, 1), (0, 1, 2), (0, 1, 2), (1, 2, 0)),
)
SENT_SLOT = [
    sum(ORDERS[f][d][r] << 2 * (4 * f + d) for f in range(2) for d in range(4)) for r in range(3)
]
SENT_ROUND = [
    sum(ORDERS[f][d].index(s) << 2 * (4 * f + d) for f in range(2) for d in range(4))
    for s in range(3)
]


def in_hbm(block):
    return pltpu.with_memory_space_constraint(block, pltpu.HBM)


def shifted(block, axis, step):
    count = lax.axis_size(axis)
    route = [(i, i + step) for i in range(count) if 0 <= i + step < count]
    return lax.ppermute(block, axis, route)


def crossed(block, axis, bits):
    count = lax.axis_size(axis)
    return lax.ppermute(block, axis, [(i, i ^ bits) for i in range(count)])


def after(block, *earlier):
    return lax.optimization_barrier((block, *earlier))[0]


def picked(packed, first, owner):
    return (packed >> (2 * (4 * first + owner))) & 3


def place_bits():
    at, place = lax.axis_index("tm"), lax.axis_index("dp")
    return at, place, 1 - at // 4, (at ^ (at >> 1)) & 1


def masks_kernel(look_ref, seg_ref, same_ref, bias_ref, segs):
    rows = bias_ref.shape[0]
    at = lax.axis_index("tm")
    half = KER // 2
    segs[...] = jnp.full(segs.shape, -1.0, jnp.float32)
    segs[:, rows + 128 : rows + 128 + seg_ref.shape[1]] = seg_ref[...].astype(jnp.float32)
    window = segs[:, pl.ds(pl.multiple_of(at * rows, 128), 2 * rows + 256)]
    mid = window[:, 128 : 128 + 2 * rows]
    lines = jnp.broadcast_to(mid, (128, 2 * rows))
    line = lax.broadcasted_iota(jnp.int32, (128, 2 * rows), 0)
    for o in range(KER):
        start = 128 + o - half
        equal = (window[:, start : start + 2 * rows] == mid).astype(jnp.float32)
        lines = jnp.where(line == o, jnp.broadcast_to(equal, lines.shape), lines)
    columns = lines.T
    same_ref[...] = columns
    col = lax.broadcasted_iota(jnp.int32, (rows, 2 * rows), 1)
    kept = (columns[rows:, KER : KER + 1] == mid) & ((col >= rows) | (look_ref[0, at] == 1))
    bias_ref[...] = jnp.where(kept, 0.0, -1e30)


def masks(look_back, seg, rows):
    vmem = pl.BlockSpec(memory_space=pltpu.VMEM)
    return pl.pallas_call(
        masks_kernel,
        out_shape=(
            jax.ShapeDtypeStruct((2 * rows, 128), jnp.float32),
            jax.ShapeDtypeStruct((rows, 2 * rows), jnp.float32),
        ),
        in_specs=[pl.BlockSpec(memory_space=pltpu.SMEM), vmem],
        out_specs=(vmem, vmem),
        scratch_shapes=[pltpu.VMEM((1, seg.shape[1] + 2 * rows + 256), jnp.float32)],
        compiler_params=pltpu.CompilerParams(vmem_limit_bytes=8 * MIB),
        cost_estimate=LITTLE,
        name="masks",
    )(look_back, seg)


def conv_kernel(far_ref, prev_ref, own_ref, next_ref, same_ref, taps_ref, act_ref, wide):
    rows = own_ref.shape[0]
    width = own_ref.shape[1]
    wide[0:EDGE] = far_ref[...].astype(jnp.float32)
    wide[EDGE : EDGE + rows] = prev_ref[...].astype(jnp.float32)
    wide[EDGE + rows : EDGE + 2 * rows] = own_ref[...].astype(jnp.float32)
    wide[EDGE + 2 * rows : 2 * EDGE + 2 * rows] = next_ref[...].astype(jnp.float32)
    part = 64
    half = KER // 2

    for start in range(0, 2 * rows, part):
        same = [
            jnp.broadcast_to(same_ref[start : start + part, o : o + 1], (part, 128))
            for o in range(KER)
        ]
        for col in range(0, width, 128):
            total = None
            for o in range(KER):
                first = EDGE + start + o - half
                term = (
                    taps_ref[o : o + 1, col : col + 128]
                    * wide[first : first + part, col : col + 128]
                )
                if o != half:
                    term = term * same[o]
                total = term if total is None else total + term
            total = 0.5 * total
            act_ref[start : start + part, col : col + 128] = (
                total + total * jnp.tanh(total)
            ).astype(jnp.bfloat16)


def conv_silu(far, prev, own, following, same, taps):
    rows, width = own.shape
    return pl.pallas_call(
        conv_kernel,
        out_shape=jax.ShapeDtypeStruct((2 * rows, width), jnp.bfloat16),
        scratch_shapes=[pltpu.VMEM((2 * EDGE + 2 * rows, width), jnp.float32)],
        compiler_params=pltpu.CompilerParams(vmem_limit_bytes=16 * MIB),
        cost_estimate=LITTLE,
        name="conv_silu",
    )(far, prev, own, following, same, taps)


def copies(pairs, sems):
    moves = [pltpu.make_async_copy(a, b, sems.at[i]) for i, (a, b) in enumerate(pairs)]
    for move in moves:
        move.start()
    for move in moves:
        move.wait()


def block_of(w_ref, turn):
    place, first, flip = place_bits()[1:]
    rows = w_ref.shape[0] // 2
    slot = picked(SENT_SLOT[turn], first, place)
    return w_ref.at[
        pl.ds(pl.multiple_of(flip * rows, rows), rows),
        pl.ds(pl.multiple_of(slot * COLS, 128), COLS),
    ]


def first_slice(w_ref, out_ref, sems):
    copies([(block_of(w_ref, turn), out_ref.at[turn]) for turn in range(2)], sems)


def later_slices(w_ref, cot_ref, _, *refs):
    place = lax.axis_index("dp")
    last, cot_own, cot_side, cot_two, sems = refs
    cots = (cot_own, cot_side, cot_two.at[0], cot_two.at[1])
    part = cot_ref.shape[1] // 4
    pairs = [(block_of(w_ref, 2), last)]
    for bits, ref in enumerate(cots):
        cols = pl.ds(pl.multiple_of((place ^ bits) * part, 128), part)
        pairs.append((cot_ref.at[:, cols], ref))
    copies(pairs, sems)


def sliced(kernel, name, out_shape, *blocks):
    anywhere = pl.BlockSpec(memory_space=pl.ANY)
    return pl.pallas_call(
        kernel,
        out_shape=out_shape,
        in_specs=[anywhere] * len(blocks),
        out_specs=[anywhere] * len(out_shape),
        scratch_shapes=[pltpu.SemaphoreType.DMA((8,))],
        compiler_params=pltpu.CompilerParams(vmem_limit_bytes=MIB),
        cost_estimate=LITTLE,
        name=name,
    )(*[in_hbm(block) for block in blocks[:2]], *blocks[2:])


def heads_kernel(sources, turn_in_order, act_ref, bias_ref, *refs):
    weight_refs, (own_ref, out_ref, held, sems) = refs[:-4], refs[-4:]
    rows = own_ref.shape[0]
    weight_refs, ahead_ref = weight_refs[:-1], weight_refs[-1]
    if ahead_ref is not None:
        out_ref[:, :COLS] = ahead_ref[...]
    width = act_ref.shape[1]
    half = width // 2
    scale = math.log2(math.e) / math.sqrt(HDIM)
    place, first, flip = place_bits()[1:]
    ring = len(sources) > 1
    if ring:
        group = 2 * (first ^ (turn_in_order // 2)) + turn_in_order % 2
    else:
        group, flip = turn_in_order, 0
    low_half = pl.ds(pl.multiple_of(flip * half, half), half)
    high_half = pl.ds(pl.multiple_of((1 - flip) * half, half), half)

    def fetch(kind):
        block = 4 * kind + group
        sem = sems.at[kind]
        target = held.at[kind]
        if ring:
            owner = (block * 11) >> 5
            slot = block - 3 * owner
            distance = owner ^ place
            code = jnp.where(
                slot == 0, SENT_ROUND[0], jnp.where(slot == 1, SENT_ROUND[1], SENT_ROUND[2])
            )
            sent_in = picked(code, first, owner)
        else:
            slot, distance = block, 0
        for form, which, refs_here in sources:
            wanted = distance == which
            if form == "first":
                wanted = wanted & (sent_in < 2)
            elif form == "last":
                wanted = wanted & (sent_in == 2)

            @pl.when(wanted)
            def _():
                if form == "whole":
                    ref = weight_refs[refs_here[0]]
                    cols = pl.ds(pl.multiple_of(slot * COLS, 128), COLS)
                    pltpu.make_async_copy(ref.at[low_half, cols], target.at[0:half], sem).start()
                    pltpu.make_async_copy(
                        ref.at[high_half, cols], target.at[half:width], sem
                    ).start()
                else:
                    start = 0
                    for index in refs_here:
                        ref = weight_refs[index]
                        if form == "first":
                            ref = ref.at[jnp.minimum(sent_in, 1)]
                        stop = start + ref.shape[0]
                        pltpu.make_async_copy(ref, target.at[start:stop], sem).start()
                        start = stop

    def project(kind, first_row):
        pltpu.make_async_copy(held.at[kind], held.at[kind], sems.at[kind]).wait()
        total = jnp.dot(
            act_ref[first_row:, low_half], held[kind, 0:half], preferred_element_type=jnp.float32
        ) + jnp.dot(
            act_ref[first_row:, high_half],
            held[kind, half:width],
            preferred_element_type=jnp.float32,
        )
        return total.astype(jnp.bfloat16)

    for kind in range(3):
        fetch(kind)
    queries = project(0, rows)
    keys = project(1, 0)
    values = project(2, 0)
    pieces = [None] * (COLS // 128)
    for head in range(GROUP):
        low, high = head * HDIM, (head + 1) * HDIM
        first_tile, last_tile = low // 128, -(-high // 128)
        window = slice(first_tile * 128, last_tile * 128)
        lanes = (rows, (last_tile - first_tile) * 128)
        lane = lax.broadcasted_iota(jnp.int32, lanes, 1) + first_tile * 128
        mine = (lane >= low) & (lane < high)
        one = jnp.where(mine, queries[:, window], jnp.zeros((), jnp.bfloat16))
        scores = lax.dot_general(
            one, keys[:, window], (((1,), (1,)), ((), ())), preferred_element_type=jnp.float32
        )
        scores = scores * scale + bias_ref[...]
        raw = jnp.exp2(scores - jnp.max(scores, axis=1, keepdims=True))
        mixed = jnp.dot(
            raw.astype(jnp.bfloat16), values[:, window], preferred_element_type=jnp.float32
        ) * (1.0 / jnp.sum(raw, axis=1, keepdims=True))
        for tile in range(first_tile, last_tile):
            here = slice((tile - first_tile) * 128, (tile - first_tile + 1) * 128)
            if pieces[tile] is None:
                pieces[tile] = mixed[:, here]
            else:
                pieces[tile] = jnp.where(mine[:, here], mixed[:, here], pieces[tile])
    for tile, piece in enumerate(pieces):
        block = piece.astype(jnp.bfloat16)
        own_ref[:, tile * 128 : (tile + 1) * 128] = block
        if ahead_ref is not None:
            out_ref[:, COLS + tile * 128 : COLS + (tile + 1) * 128] = block


def attend(sources, turn_in_order, weights, act, bias, *ahead):
    rows, width = act.shape[0] // 2, act.shape[1]
    vmem = pl.BlockSpec(memory_space=pltpu.VMEM)
    anywhere = pl.BlockSpec(memory_space=pl.ANY)

    def kernel(act_ref, bias_ref, *refs):
        if not ahead:
            refs = refs[:-3] + (None, refs[-3], None) + refs[-2:]
        heads_kernel(sources, turn_in_order, act_ref, bias_ref, *refs)

    outs = [jax.ShapeDtypeStruct((rows, COLS * n), jnp.bfloat16) for n in range(1, 2 + len(ahead))]
    return pl.pallas_call(
        kernel,
        out_shape=outs,
        in_specs=[vmem, vmem] + [anywhere] * len(weights) + [vmem] * len(ahead),
        out_specs=[vmem] * len(outs),
        scratch_shapes=[
            pltpu.VMEM((3, width, COLS), jnp.bfloat16),
            pltpu.SemaphoreType.DMA((3,)),
        ],
        compiler_params=pltpu.CompilerParams(vmem_limit_bytes=16 * MIB),
        cost_estimate=LITTLE,
        name=f"attention_{turn_in_order}",
    )(act, bias, in_hbm(weights[0]), *weights[1:], *ahead)


def mixed_kernel(far_ref, near_ref, w_ref, out_ref):
    depth = far_ref.shape[1]
    first = place_bits()[2]
    far_rows, near_rows = (
        pl.ds(pl.multiple_of(pair * depth, depth), depth) for pair in (first, 1 - first)
    )
    total = jnp.dot(
        far_ref[...], w_ref[far_rows], preferred_element_type=jnp.float32
    ) + jnp.dot(near_ref[...], w_ref[near_rows], preferred_element_type=jnp.float32)
    out_ref[...] = total.astype(jnp.bfloat16)


def project_out(attns, w_o):
    rows, width = attns[0].shape[0], w_o.shape[1]
    cols = 512
    return pl.pallas_call(
        mixed_kernel,
        grid=(width // cols,),
        out_shape=jax.ShapeDtypeStruct((rows, width), jnp.bfloat16),
        in_specs=[pl.BlockSpec(attn.shape, lambda i: (0, 0)) for attn in attns]
        + [pl.BlockSpec((width, cols), lambda i: (0, i))],
        out_specs=pl.BlockSpec((rows, cols), lambda i: (0, i)),
        compiler_params=pltpu.CompilerParams(
            dimension_semantics=("arbitrary",), vmem_limit_bytes=16 * MIB
        ),
        cost_estimate=LITTLE,
        name="mixed",
    )(*attns, in_hbm(w_o))


def product(attn, cot):
    return lax.dot_general(attn, cot, (((0,), (0,)), ((), ())), preferred_element_type=jnp.float32)


def grad_kernel(*refs):
    *attn_refs, cot_0, cot_1, cot_2, cot_3, keep_ref, send_1, send_2, send_3, total = refs
    size = keep_ref.shape[0]
    low = lax.axis_index("tm") & 3
    for half in range(2):
        cols = slice(half * COLS, (half + 1) * COLS)
        blocks = [ref[:, cols] for ref in attn_refs if ref.shape[1] > COLS]
        blocks += [ref[...] for ref in attn_refs[len(blocks) + half :: 2]]
        cots = (cot_0[...], cot_1[...], cot_2[0], cot_3[1])
        total[cols] = sum(product(block, cot) for block, cot in zip(blocks, cots))
    keep_ref[...] = total[pl.ds(pl.multiple_of(low * size, size), size)]
    for bits, ref in enumerate((send_1, send_2, send_3), 1):
        ref[...] = total[pl.ds(pl.multiple_of((low ^ bits) * size, size), size)].astype(
            jnp.bfloat16
        )


def grad_part(attns, cots, name):
    cols = cots[0].shape[1]
    size = COLS // 2
    return pl.pallas_call(
        grad_kernel,
        out_shape=[jax.ShapeDtypeStruct((size, cols), jnp.float32)]
        + [jax.ShapeDtypeStruct((size, cols), jnp.bfloat16)] * 3,
        scratch_shapes=[pltpu.VMEM((2 * COLS, cols), jnp.float32)],
        compiler_params=pltpu.CompilerParams(vmem_limit_bytes=16 * MIB),
        cost_estimate=LITTLE,
        name=name,
    )(*attns, *cots)


def local(frames, seg, look_back, w_dw, w_qkv, w_o, cotangent):
    rows, width = frames.shape
    assert rows == STRETCH
    dp_count = lax.axis_size("dp")
    tm_count = lax.axis_size("tm")
    ring = dp_count == 4 and tm_count == 8
    part = width // dp_count

    far = shifted(frames[rows - EDGE :], "tm", 2)
    following = shifted(frames[:EDGE], "tm", -1)
    prev = shifted(frames, "tm", 1)
    same, bias = masks(look_back, seg, rows)


    if not ring:
        gathered = lax.all_gather(w_qkv, "dp", axis=1, tiled=True)
        act = conv_silu(far, prev, frames, following, same, w_dw)
        sources = [("whole", 0, (0,))]
        attn = jnp.concatenate(
            [
                attend(sources, group, [gathered], act, bias)[0]
                for group in range(width // COLS)
            ],
            1,
        )
        mixed = jnp.dot(attn, w_o, preferred_element_type=jnp.float32).astype(jnp.bfloat16)
        place = lax.axis_index("dp")
        cots = [
            lax.dynamic_slice_in_dim(cotangent, (place ^ bits) * part, part, 1)
            for bits in range(dp_count)
        ]
        cot = jnp.concatenate(
            [crossed(c, "dp", bits) if bits else c for bits, c in enumerate(cots)], 0
        )
        blocks = [attn]
        bits = 1
        while bits < dp_count:
            blocks += [crossed(block, "dp", bits) for block in blocks]
            bits *= 2
        grad = lax.dot_general(
            jnp.concatenate(blocks, 0),
            cot,
            (((0,), (0,)), ((), ())),
            preferred_element_type=jnp.float32,
        )
        return mixed, lax.psum_scatter(grad, "tm", scatter_dimension=0, tiled=True)

    mid_rows = width // 2

    sent_shape = jax.ShapeDtypeStruct((mid_rows, COLS), jnp.bfloat16)
    cot_shape = jax.ShapeDtypeStruct((rows, part), jnp.bfloat16)
    pair_shape = jax.ShapeDtypeStruct((2, mid_rows, COLS), jnp.bfloat16)
    two_shape = jax.ShapeDtypeStruct((2, rows, part), jnp.bfloat16)
    sent = sliced(first_slice, "first_slice", [pair_shape], w_qkv)[0]
    later_shapes = [sent_shape] + [cot_shape] * 2 + [two_shape]
    last, cot_own, cot_side, cot_two = sliced(
        later_slices, "later_slices", later_shapes, w_qkv, cotangent, sent
    )
    first_over = crossed(sent, "dp", 2)
    last_over = crossed(after(last, first_over), "dp", 2)
    cot_side = crossed(cot_side, "dp", 1)
    frames_here = after(frames, cot_side, last)
    act = conv_silu(far, prev, frames_here, following, same, w_dw)
    sibling = crossed(w_qkv, "dp", 1)

    def spread(block, earlier=(), relay_after=()):
        block = after(block, *earlier)
        side = crossed(block[..., : mid_rows // 2, :], "tm", 1)
        deep = crossed(block[..., mid_rows // 2 :, :], "tm", 2)
        relays = [crossed(after(b, *relay_after), "dp", 1) for b in (block, side, deep)]
        return [block, side, deep] + relays

    first_sources = [
        ("whole", 0, (0,)),
        ("whole", 1, (1,)),
        ("first", 2, (2, 3, 4)),
        ("first", 3, (5, 6, 7)),
    ]
    weights = [w_qkv, sibling] + spread(first_over, (act,))
    first_attn = attend(first_sources, 0, weights, act, bias)[0]
    far_attn = attend(first_sources, 1, weights, after(act, first_attn), bias, first_attn)[1]

    sources = first_sources + [("last", 2, (8, 9, 10)), ("last", 3, (11, 12, 13))]
    weights = weights + spread(last_over, (), (first_attn,))
    cot_over = crossed(after(cot_two, first_over), "dp", 2)
    cots = [cot_own, cot_side, cot_over, crossed(cot_over, "dp", 1)]

    def attention(turn, *earlier, ahead=()):
        return attend(sources, turn, weights, after(act, *earlier), bias, *ahead)

    far_side = crossed(far_attn, "dp", 1)
    third_attn = attention(2, far_attn, far_side)[0]
    fourth_attn, near_attn = attention(3, third_attn, ahead=(third_attn,))
    mixed = project_out([far_attn, near_attn], w_o)

    def traded(sums, *sent):
        for bits, block in enumerate(sent, 1):
            sums = sums + crossed(block, "tm", bits).astype(jnp.float32)
        return sums

    far_over = crossed(after(far_attn, cot_over), "dp", 2)
    far_relay = crossed(after(far_over, near_attn), "dp", 1)
    far_sums = traded(*grad_part([far_attn, far_side, far_over, far_relay], cots, "far"))
    far_term = crossed(far_sums.astype(jnp.bfloat16), "tm", 4)
    near_over = crossed(near_attn, "dp", 2)
    near_blocks = [near_attn, crossed(near_attn, "dp", 1), near_over, crossed(near_over, "dp", 1)]
    weight_grad = traded(*grad_part(near_blocks, cots, "near")) + far_term.astype(jnp.float32)
    return mixed, weight_grad


def solution(mesh):
    placed = (
        P(("dp", "tm"), None),
        P("dp", None),
        P("dp", None),
        P(),
        P(None, "dp"),
        P(),
        P(("dp", "tm"), None),
    )
    return jax.shard_map(
        local,
        mesh=mesh,
        in_specs=placed,
        out_specs=(P(("dp", "tm"), None), P("tm", "dp")),
        check_vma=False,
    )
```

time: 501 us -> 106 us (0.21)
  waiting for transfers between devices: 326 us -> 37.4 us
  local copies, waits for them, and re-layouts: 60.2 us -> 0.21 us
  matrix products: 42.7 us -> 0 us
  Pallas kernels: 0 us -> 34.5 us
  blocking collectives: 23.8 us -> 0 us
  starting transfers between devices: 12.7 us -> 31.3 us
  other arithmetic: 17.5 us -> 0.86 us
  between operations: 14 us -> 0.89 us
    reduce_scatter x2 -> x0, waiting for transfers between devices: 185 us -> none  [the longest x1 162 us: local(): lax.psum_scatter(grad_term, 'tm', scatter_dimension=0, tiled=True)]
    all_gather x1 -> x0, waiting for transfers between devices: 86.8 us -> none  [local(): lax.all_gather(w_qkv, 'dp', axis=1, tiled=True)]
    all_to_all x1 -> x0, waiting for transfers between devices: 52.8 us -> none  [local(): lax.all_to_all(arranged, 'tm', split_axis=2, concat_axis=0, tiled=True)]
    ppermute x2 -> x32, waiting for transfers between devices: 0.97 us -> 37.4 us  [the longest x29 26.6 us: crossed(): return lax.ppermute(block, axis, [(i, i ^ bits) for i in range(count)])]
    pallas_call x0 -> x11, Pallas kernels: none -> 34.5 us  [the longest x4 19.8 us: attend(): pl.pallas_call(kernel, out_shape=outs, in_specs=[vmem, vmem] + [anywhere]...]
    dot_general x7 -> x0, matrix products: 29.7 us -> none  [the longest x1 11.5 us: local(): jnp.dot(activ, lax.all_gather(w_qkv, 'dp', axis=1, tiled=True), preferred...]
    ppermute x2 -> x32, starting transfers between devices: 6.76 us -> 31.3 us  [the longest x29 23.2 us: crossed(): return lax.ppermute(block, axis, [(i, i ^ bits) for i in range(count)])]
    all_to_all x1 -> x0, blocking collectives: 23.8 us -> none  [local(): lax.all_to_all(attended.reshape(frame_count, 1, piece), 'tm', split_axis=...]
  transfers between devices with their start and end apart: 6 -> 32, of which waited for: 5 -> 13; matrix products, arithmetic and copies ran while one was open for 1% -> 0% of each run, Pallas kernels for 0% -> 33%
where the time goes in v1:
time: 106 us; the launch traced here: 105 us
  waiting for transfers between devices  37.4 us (35%)
  Pallas kernels  34.5 us (33%)
  starting transfers between devices  31.3 us (30%)
    ppermute x29, waiting for transfers between devices, crossed(): return lax.ppermute(block, axis, [(i, i ^ bits) for i in range(count)])  26.6 us
    ppermute x29, starting transfers between devices, crossed(): return lax.ppermute(block, axis, [(i, i ^ bits) for i in range(count)])  23.2 us
    pallas_call x4, Pallas kernels, attend(): pl.pallas_call(kernel, out_shape=outs, in_specs=[vmem, vmem] + [anywhere]...  19.8 us
    ppermute x3, waiting for transfers between devices, shifted(): return lax.ppermute(block, axis, route)  10.8 us
    ppermute x3, starting transfers between devices, shifted(): return lax.ppermute(block, axis, route)  8.16 us
    pallas_call x1, Pallas kernels, project_out(): pl.pallas_call(mixed_kernel, grid=(width // cols,), out_shape=jax.ShapeDt...  4.77 us
    pallas_call x1, Pallas kernels, conv_silu(): pl.pallas_call(conv_kernel, out_shape=jax.ShapeDtypeStruct((2 * rows, wid...  4.07 us
    pallas_call x2, Pallas kernels, sliced(): pl.pallas_call(kernel, out_shape=out_shape, in_specs=[anywhere] * len(blo...  2.71 us
  transfers between devices with their start and end apart: 32, of which 13 were waited for; matrix products, arithmetic and copies ran while one was open for 0% of the time, Pallas kernels for 33%

profile of v1, /device:TPU:0, one launch (start us, length us, event | category | flops | bytes accessed | tf_op | source)
XLA Modules:
  0.0 105.3 jit_solution(16453367742163237306)
XLA Ops:
  1.2 1.3 %first_slice.1._ = bf16[2,768,384]{2,1,0:T(8,128)(2,1)S(1)} custom-call(bf16[1536,1152]{1,0:T(8,128)(2,1)} %refs_0_.7), custom_call_target="tpu_custom_call" | custom-call | flops 1000000 | bytes 10000 | tf_op jit(solution)/shard_map/first_slice/pallas_call | solution.py:178
  2.5 2.7 %collective-permute-start.5 = (bf16[2,768,384]{2,1,0:T(8,128)(2,1)S(1)}, bf16[2,768,384]{2,1,0:T(8,128)(2,1)S(1)}, u32[]{:S(2)}, u32[]{:S(2)}) collective-permute-start(bf16[2,768,384]{2,1,0:T(8,128)(2,1)S(1)} %first_slice.1._), channel_id=1, source_target_pairs={{0,16},{8,24},{16,0},{24,8},{1,17},{9,25},{17,1},{25,9},{2,18},{10... | collective-permute-start | bytes 3538952 | tf_op jit(solution)/shard_map/ppermute | solution.py:44
  5.2 3.4 %collective-permute-start.1 = (bf16[256,1536]{1,0:T(8,128)(2,1)S(1)}, bf16[256,1536]{1,0:T(8,128)(2,1)S(1)}, u32[]{:S(2)}, u32[]{:S(2)}) collective-permute-start(bf16[256,1536]{1,0:T(8,128)(2,1)S(1)} %copy-done), channel_id=1, source_target_pairs={{0,1},{1,2},{2,3},{3,4},{4,5},{5,6},{6,7},{8,9},{9,10},{10,11},{11... | collective-permute-start | bytes 2359304 | tf_op jit(solution)/shard_map/ppermute | solution.py:39
  8.6 1.4 %later_slices.1 = (bf16[768,384]{1,0:T(8,128)(2,1)S(1)}, bf16[256,384]{1,0:T(8,128)(2,1)S(1)}, bf16[256,384]{1,0:T(8,128)(2,1)S(1)}, bf16[2,256,384]{2,1,0:T(8,128)(2,1)S(1)}) custom-call(bf16[1536,1152]{1,0:T(8,128)(2,1)} %refs_0_.7, bf16[256,1536]{1,0:T(8,128)(2,1)} %cot_ref.1, bf16[2,768,384]{2,1,0:T(8,128)(2,1)S(1)} %first_slice.1._), custom_call_target="tpu_custom_call" | custom-call | flops 1000000 | bytes 10000 | tf_op jit(solution)/shard_map/later_slices/pallas_call | solution.py:178
  10.1 3.4 %collective-permute-start = (bf16[16,1536]{1,0:T(8,128)(2,1)S(1)}, bf16[16,1536]{1,0:T(8,128)(2,1)S(1)}, u32[]{:S(2)}, u32[]{:S(2)}) collective-permute-start(bf16[16,1536]{1,0:T(8,128)(2,1)S(1)} %get-tuple-element.61), channel_id=1, source_target_pairs={{0,2},{1,3},{2,4},{3,5},{4,6},{5,7},{8,10},{9,11},{10,12},{11,13},... | collective-permute-start | bytes 147464 | tf_op jit(solution)/shard_map/ppermute | solution.py:39
  13.6 1.3 %collective-permute-start.3 = (bf16[16,1536]{1,0:T(8,128)(2,1)S(1)}, bf16[16,1536]{1,0:T(8,128)(2,1)S(1)}, u32[]{:S(2)}, u32[]{:S(2)}) collective-permute-start(bf16[16,1536]{1,0:T(8,128)(2,1)S(1)} %get-tuple-element.60), channel_id=1, source_target_pairs={{1,0},{2,1},{3,2},{4,3},{5,4},{6,5},{7,6},{9,8},{10,9},{11,10},{12... | collective-permute-start | bytes 147464 | tf_op jit(solution)/shard_map/ppermute | solution.py:39
  14.9 1.0 masks.1
  16.0 3.6 %collective-permute-done.3.next_ref = bf16[16,1536]{1,0:T(8,128)(2,1)S(1)} collective-permute-done((bf16[16,1536]{1,0:T(8,128)(2,1)S(1)}, bf16[16,1536]{1,0:T(8,128)(2,1)S(1)}, u32[]{:S(2)}, u32[]{:S(2)}) %collective-permute-start.3) | collective-permute-done | bytes 49184 | tf_op jit(solution)/shard_map/ppermute | solution.py:39
  19.6 7.2 %collective-permute-done.1.prev_ref = bf16[256,1536]{1,0:T(8,128)(2,1)S(1)} collective-permute-done((bf16[256,1536]{1,0:T(8,128)(2,1)S(1)}, bf16[256,1536]{1,0:T(8,128)(2,1)S(1)}, u32[]{:S(2)}, u32[]{:S(2)}) %collective-permute-start.1) | collective-permute-done | bytes 786464 | tf_op jit(solution)/shard_map/ppermute | solution.py:39
  26.7 4.1 %conv_silu.1.act_ref = bf16[512,1536]{1,0:T(8,128)(2,1)S(1)} custom-call(bf16[16,1536]{1,0:T(8,128)(2,1)S(1)} %collective-permute-done.far_ref, bf16[256,1536]{1,0:T(8,128)(2,1)S(1)} %collective-permute-done.1.prev_ref, bf16[256,1536]{1,0:T(8,128)(2,1)S(1)} %copy-done, bf16[16,1536]{1,0:T(8,128)(2,1)S(1)} %collective-permute-done.3.next_ref, ...), custom_call_target="tpu_custom_call" | custom-call | flops 1000000 | bytes 10000 | tf_op jit(solution)/shard_map/conv_silu/pallas_call | solution.py:132
  31.9 2.6 %collective-permute-start.7 = (bf16[2,384,384]{2,1,0:T(8,128)(2,1)S(1)}, bf16[2,384,384]{2,1,0:T(8,128)(2,1)S(1)}, u32[]{:S(2)}, u32[]{:S(2)}) collective-permute-start(bf16[2,384,384]{2,1,0:T(8,128)(2,1)S(1)} %get-tuple-element.58), channel_id=1, source_target_pairs={{0,2},{1,3},{2,0},{3,1},{4,6},{5,7},{6,4},{7,5},{8,10},{9,11},{10,... | collective-permute-start | bytes 1769480 | tf_op jit(solution)/shard_map/ppermute | solution.py:44
  35.2 1.5 %collective-permute-start.12 = (bf16[768,384]{1,0:T(8,128)(2,1)S(1)}, bf16[768,384]{1,0:T(8,128)(2,1)S(1)}, u32[]{:S(2)}, u32[]{:S(2)}) collective-permute-start(bf16[768,384]{1,0:T(8,128)(2,1)S(1)} %get-tuple-element.39), channel_id=1, source_target_pairs={{0,16},{8,24},{16,0},{24,8},{1,17},{9,25},{17,1},{25,9},{2,18},{10... | collective-permute-start | bytes 1769480 | tf_op jit(solution)/shard_map/ppermute | solution.py:44
  36.8 11.3 %collective-permute-done.7.refs_4_ = bf16[2,384,384]{2,1,0:T(8,128)(2,1)S(1)} collective-permute-done((bf16[2,384,384]{2,1,0:T(8,128)(2,1)S(1)}, bf16[2,384,384]{2,1,0:T(8,128)(2,1)S(1)}, u32[]{:S(2)}, u32[]{:S(2)}) %collective-permute-start.7) | collective-permute-done | bytes 589856 | tf_op jit(solution)/shard_map/ppermute | solution.py:44
  48.0 1.5 %collective-permute-done.6.refs_3_ = bf16[2,384,384]{2,1,0:T(8,128)(2,1)S(1)} collective-permute-done((bf16[2,384,384]{2,1,0:T(8,128)(2,1)S(1)}, bf16[2,384,384]{2,1,0:T(8,128)(2,1)S(1)}, u32[]{:S(2)}, u32[]{:S(2)}) %collective-permute-start.6) | collective-permute-done | bytes 589856 | tf_op jit(solution)/shard_map/ppermute | solution.py:44
  49.5 1.5 %collective-permute-done.12.refs_8_ = bf16[768,384]{1,0:T(8,128)(2,1)S(1)} collective-permute-done((bf16[768,384]{1,0:T(8,128)(2,1)S(1)}, bf16[768,384]{1,0:T(8,128)(2,1)S(1)}, u32[]{:S(2)}, u32[]{:S(2)}) %collective-permute-start.12) | collective-permute-done | bytes 589856 | tf_op jit(solution)/shard_map/ppermute | solution.py:44
  51.0 1.5 %collective-permute-start.21 = (bf16[2,256,384]{2,1,0:T(8,128)(2,1)S(1)}, bf16[2,256,384]{2,1,0:T(8,128)(2,1)S(1)}, u32[]{:S(2)}, u32[]{:S(2)}) collective-permute-start(bf16[2,256,384]{2,1,0:T(8,128)(2,1)S(1)} %get-tuple-element.47), channel_id=1, source_target_pairs={{0,16},{8,24},{16,0},{24,8},{1,17},{9,25},{17,1},{25,9},{2,18},{10... | collective-permute-start | bytes 1179656 | tf_op jit(solution)/shard_map/ppermute | solution.py:44
  53.6 4.7 %attention_0.1.refs_8_ = bf16[256,384]{1,0:T(8,128)(2,1)S(1)} custom-call(bf16[512,1536]{1,0:T(8,128)(2,1)S(1)} %conv_silu.1.act_ref, f32[256,512]{1,0:T(8,128)S(1)} %get-tuple-element.34.bias_ref, bf16[1536,1152]{1,0:T(8,128)(2,1)} %refs_0_.7, bf16[1536,1152]{1,0:T(8,128)(2,1)S(1)} %collective-permute-done.4.refs_1_, ...), custom_call_target="tpu_custom_call" | custom-call | flops 1000000 | bytes 10000 | tf_op jit(solution)/shard_map/attention_0/pallas_call | solution.py:305
  58.4 5.0 %attention_1.1 = (bf16[256,384]{1,0:T(8,128)(2,1)}, bf16[256,768]{1,0:T(8,128)(2,1)S(1)}) custom-call(bf16[512,1536]{1,0:T(8,128)(2,1)S(1)} %conv_silu.1.act_ref, f32[256,512]{1,0:T(8,128)S(1)} %get-tuple-element.34.bias_ref, bf16[1536,1152]{1,0:T(8,128)(2,1)} %refs_0_.7, bf16[1536,1152]{1,0:T(8,128)(2,1)S(1)} %collective-permute-done.4.refs_1_, ...), custom_call_target="tpu_custom_call" | custom-call | flops 1000000 | bytes 10000 | tf_op jit(solution)/shard_map/attention_1/pallas_call | solution.py:305
  66.6 4.7 %attention_2.1.refs_14_ = bf16[256,384]{1,0:T(8,128)(2,1)S(1)} custom-call(bf16[512,1536]{1,0:T(8,128)(2,1)S(1)} %conv_silu.1.act_ref, f32[256,512]{1,0:T(8,128)S(1)} %get-tuple-element.34.bias_ref, bf16[1536,1152]{1,0:T(8,128)(2,1)} %refs_0_.7, bf16[1536,1152]{1,0:T(8,128)(2,1)S(1)} %collective-permute-done.4.refs_1_, ...), custom_call_target="tpu_custom_call" | custom-call | flops 1000000 | bytes 10000 | tf_op jit(solution)/shard_map/attention_2/pallas_call | solution.py:305
  71.3 5.4 %attention_3.1 = (bf16[256,384]{1,0:T(8,128)(2,1)}, bf16[256,768]{1,0:T(8,128)(2,1)S(1)}) custom-call(bf16[512,1536]{1,0:T(8,128)(2,1)S(1)} %conv_silu.1.act_ref, f32[256,512]{1,0:T(8,128)S(1)} %get-tuple-element.34.bias_ref, bf16[1536,1152]{1,0:T(8,128)(2,1)} %refs_0_.7, bf16[1536,1152]{1,0:T(8,128)(2,1)S(1)} %collective-permute-done.4.refs_1_, ...), custom_call_target="tpu_custom_call" | custom-call | flops 1000000 | bytes 10000 | tf_op jit(solution)/shard_map/attention_3/pallas_call | solution.py:305
  76.8 1.0 collective-permute-start.19
  78.5 1.1 %far.1 = (f32[192,384]{1,0:T(8,128)S(1)}, bf16[192,384]{1,0:T(8,128)(2,1)S(1)}, bf16[192,384]{1,0:T(8,128)(2,1)S(1)}, bf16[192,384]{1,0:T(8,128)(2,1)S(1)}) custom-call(bf16[256,768]{1,0:T(8,128)(2,1)S(1)} %get-tuple-element.52.far_ref.refs_0_, bf16[256,768]{1,0:T(8,128)(2,1)S(1)} %collective-permute-done.11.refs_1_, ...), custom_call_target="tpu_custom_call" | custom-call | flops 1000000 | bytes 10000 | tf_op jit(solution)/shard_map/far/pallas_call | solution.py:374
  79.6 1.6 %collective-permute-start.28 = (bf16[192,384]{1,0:T(8,128)(2,1)S(1)}, bf16[192,384]{1,0:T(8,128)(2,1)S(1)}, u32[]{:S(2)}, u32[]{:S(2)}) collective-permute-start(bf16[192,384]{1,0:T(8,128)(2,1)S(1)} %get-tuple-element.55), channel_id=1, source_target_pairs={{0,1},{1,0},{2,3},{3,2},{4,5},{5,4},{6,7},{7,6},{8,9},{9,8},{10,11... | collective-permute-start | bytes 442376 | tf_op jit(solution)/shard_map/ppermute | solution.py:44
  81.2 1.6 %collective-permute-start.29 = (bf16[192,384]{1,0:T(8,128)(2,1)S(1)}, bf16[192,384]{1,0:T(8,128)(2,1)S(1)}, u32[]{:S(2)}, u32[]{:S(2)}) collective-permute-start(bf16[192,384]{1,0:T(8,128)(2,1)S(1)} %get-tuple-element.56), channel_id=1, source_target_pairs={{0,2},{1,3},{2,0},{3,1},{4,6},{5,7},{6,4},{7,5},{8,10},{9,11},{10,... | collective-permute-start | bytes 442376 | tf_op jit(solution)/shard_map/ppermute | solution.py:44
  83.1 5.2 %collective-permute-done.19.refs_2_ = bf16[256,768]{1,0:T(8,128)(2,1)S(1)} collective-permute-done((bf16[256,768]{1,0:T(8,128)(2,1)S(1)}, bf16[256,768]{1,0:T(8,128)(2,1)S(1)}, u32[]{:S(2)}, u32[]{:S(2)}) %collective-permute-start.19) | collective-permute-done | bytes 393248 | tf_op jit(solution)/shard_map/ppermute | solution.py:44
  88.3 1.6 %collective-permute-done.30 = bf16[192,384]{1,0:T(8,128)(2,1)S(1)} collective-permute-done((bf16[192,384]{1,0:T(8,128)(2,1)S(1)}, bf16[192,384]{1,0:T(8,128)(2,1)S(1)}, u32[]{:S(2)}, u32[]{:S(2)}) %collective-permute-start.30) | collective-permute-done | bytes 147488 | tf_op jit(solution)/shard_map/ppermute | solution.py:44
  89.9 2.3 %collective-permute-start.31 = (bf16[192,384]{1,0:T(8,128)(2,1)S(1)}, bf16[192,384]{1,0:T(8,128)(2,1)S(1)}, u32[]{:S(2)}, u32[]{:S(2)}) collective-permute-start(bf16[192,384]{1,0:T(8,128)(2,1)S(1)} %add_convert_fusion), channel_id=1, source_target_pairs={{0,4},{1,5},{2,6},{3,7},{4,0},{5,1},{6,2},{7,3},{8,12},{9,13},{10,... | collective-permute-start | bytes 442376 | tf_op jit(solution)/shard_map/ppermute | solution.py:44
  92.2 1.1 %near.1 = (f32[192,384]{1,0:T(8,128)S(1)}, bf16[192,384]{1,0:T(8,128)(2,1)S(1)}, bf16[192,384]{1,0:T(8,128)(2,1)S(1)}, bf16[192,384]{1,0:T(8,128)(2,1)S(1)}) custom-call(bf16[256,768]{1,0:T(8,128)(2,1)S(1)} %get-tuple-element.44.near_ref.refs_0_, bf16[256,768]{1,0:T(8,128)(2,1)S(1)} %collective-permute-done.18.refs_1_, ...), custom_call_target="tpu_custom_call" | custom-call | flops 1000000 | bytes 10000 | tf_op jit(solution)/shard_map/near/pallas_call | solution.py:374
  93.3 1.6 %collective-permute-start.23 = (bf16[192,384]{1,0:T(8,128)(2,1)S(1)}, bf16[192,384]{1,0:T(8,128)(2,1)S(1)}, u32[]{:S(2)}, u32[]{:S(2)}) collective-permute-start(bf16[192,384]{1,0:T(8,128)(2,1)S(1)} %get-tuple-element.49), channel_id=1, source_target_pairs={{0,1},{1,0},{2,3},{3,2},{4,5},{5,4},{6,7},{7,6},{8,9},{9,8},{10,11... | collective-permute-start | bytes 442376 | tf_op jit(solution)/shard_map/ppermute | solution.py:44
  94.9 1.6 %collective-permute-start.24 = (bf16[192,384]{1,0:T(8,128)(2,1)S(1)}, bf16[192,384]{1,0:T(8,128)(2,1)S(1)}, u32[]{:S(2)}, u32[]{:S(2)}) collective-permute-start(bf16[192,384]{1,0:T(8,128)(2,1)S(1)} %get-tuple-element.50), channel_id=1, source_target_pairs={{0,2},{1,3},{2,0},{3,1},{4,6},{5,7},{6,4},{7,5},{8,10},{9,11},{10,... | collective-permute-start | bytes 442376 | tf_op jit(solution)/shard_map/ppermute | solution.py:44
  96.9 4.8 %mixed.1 = bf16[256,1536]{1,0:T(8,128)(2,1)} custom-call(bf16[256,768]{1,0:T(8,128)(2,1)S(1)} %get-tuple-element.52.far_ref.refs_0_, bf16[256,768]{1,0:T(8,128)(2,1)S(1)} %get-tuple-element.44.near_ref.refs_0_, bf16[1536,1536]{1,0:T(8,128)(2,1)} %w_ref.5), custom_call_target="tpu_custom_call" | custom-call | flops 1000000 | bytes 10000 | tf_op jit(solution)/shard_map/mixed/pallas_call | solution.py:335
  102.4 2.1 %collective-permute-done.25 = bf16[192,384]{1,0:T(8,128)(2,1)S(1)} collective-permute-done((bf16[192,384]{1,0:T(8,128)(2,1)S(1)}, bf16[192,384]{1,0:T(8,128)(2,1)S(1)}, u32[]{:S(2)}, u32[]{:S(2)}) %collective-permute-start.25) | collective-permute-done | bytes 147488 | tf_op jit(solution)/shard_map/ppermute | solution.py:44
  (56 shorter events, 9.8 us)
Async XLA Ops:
  0.6 53.0 %collective-permute-start.4 = (bf16[1536,1152]{1,0:T(8,128)(2,1)}, bf16[1536,1152]{1,0:T(8,128)(2,1)S(1)}, u32[]{:S(2)}, u32[]{:S(2)}) collective-permute-start(bf16[1536,1152]{1,0:T(8,128)(2,1)} %refs_0_.7), channel_id=1, source_target_pairs={{0,8},{8,0},{16,24},{24,16},{1,9},{9,1},{17,25},{25,17},{2,10},{10... | collective-permute-start | bytes 10616840 | tf_op jit(solution)/shard_map/ppermute | solution.py:44
  2.5 29.2 %collective-permute-start.5 = (bf16[2,768,384]{2,1,0:T(8,128)(2,1)S(1)}, bf16[2,768,384]{2,1,0:T(8,128)(2,1)S(1)}, u32[]{:S(2)}, u32[]{:S(2)}) collective-permute-start(bf16[2,768,384]{2,1,0:T(8,128)(2,1)S(1)} %first_slice.1._), channel_id=1, source_target_pairs={{0,16},{8,24},{16,0},{24,8},{1,17},{9,25},{17,1},{25,9},{2,18},{10... | collective-permute-start | bytes 3538952 | tf_op jit(solution)/shard_map/ppermute | solution.py:44
  5.2 21.5 %collective-permute-start.1 = (bf16[256,1536]{1,0:T(8,128)(2,1)S(1)}, bf16[256,1536]{1,0:T(8,128)(2,1)S(1)}, u32[]{:S(2)}, u32[]{:S(2)}) collective-permute-start(bf16[256,1536]{1,0:T(8,128)(2,1)S(1)} %copy-done), channel_id=1, source_target_pairs={{0,1},{1,2},{2,3},{3,4},{4,5},{5,6},{6,7},{8,9},{9,10},{10,11},{11... | collective-permute-start | bytes 2359304 | tf_op jit(solution)/shard_map/ppermute | solution.py:39
  10.0 3.5 %collective-permute-start.2 = (bf16[256,384]{1,0:T(8,128)(2,1)S(1)}, bf16[256,384]{1,0:T(8,128)(2,1)S(1)}, u32[]{:S(2)}, u32[]{:S(2)}) collective-permute-start(bf16[256,384]{1,0:T(8,128)(2,1)S(1)} %get-tuple-element.30), channel_id=1, source_target_pairs={{0,8},{8,0},{16,24},{24,16},{1,9},{9,1},{17,25},{25,17},{2,10},{10... | collective-permute-start | bytes 589832 | tf_op jit(solution)/shard_map/ppermute | solution.py:44
  10.1 5.8 %collective-permute-start = (bf16[16,1536]{1,0:T(8,128)(2,1)S(1)}, bf16[16,1536]{1,0:T(8,128)(2,1)S(1)}, u32[]{:S(2)}, u32[]{:S(2)}) collective-permute-start(bf16[16,1536]{1,0:T(8,128)(2,1)S(1)} %get-tuple-element.61), channel_id=1, source_target_pairs={{0,2},{1,3},{2,4},{3,5},{4,6},{5,7},{8,10},{9,11},{10,12},{11,13},... | collective-permute-start | bytes 147464 | tf_op jit(solution)/shard_map/ppermute | solution.py:39
  13.6 6.0 %collective-permute-start.3 = (bf16[16,1536]{1,0:T(8,128)(2,1)S(1)}, bf16[16,1536]{1,0:T(8,128)(2,1)S(1)}, u32[]{:S(2)}, u32[]{:S(2)}) collective-permute-start(bf16[16,1536]{1,0:T(8,128)(2,1)S(1)} %get-tuple-element.60), channel_id=1, source_target_pairs={{1,0},{2,1},{3,2},{4,3},{5,4},{6,5},{7,6},{9,8},{10,9},{11,10},{12... | collective-permute-start | bytes 147464 | tf_op jit(solution)/shard_map/ppermute | solution.py:39
  31.9 16.2 %collective-permute-start.7 = (bf16[2,384,384]{2,1,0:T(8,128)(2,1)S(1)}, bf16[2,384,384]{2,1,0:T(8,128)(2,1)S(1)}, u32[]{:S(2)}, u32[]{:S(2)}) collective-permute-start(bf16[2,384,384]{2,1,0:T(8,128)(2,1)S(1)} %get-tuple-element.58), channel_id=1, source_target_pairs={{0,2},{1,3},{2,0},{3,1},{4,6},{5,7},{6,4},{7,5},{8,10},{9,11},{10,... | collective-permute-start | bytes 1769480 | tf_op jit(solution)/shard_map/ppermute | solution.py:44
  34.5 15.0 %collective-permute-start.6 = (bf16[2,384,384]{2,1,0:T(8,128)(2,1)S(1)}, bf16[2,384,384]{2,1,0:T(8,128)(2,1)S(1)}, u32[]{:S(2)}, u32[]{:S(2)}) collective-permute-start(bf16[2,384,384]{2,1,0:T(8,128)(2,1)S(1)} %get-tuple-element.59), channel_id=1, source_target_pairs={{0,1},{1,0},{2,3},{3,2},{4,5},{5,4},{6,7},{7,6},{8,9},{9,8},{10,11... | collective-permute-start | bytes 1769480 | tf_op jit(solution)/shard_map/ppermute | solution.py:44
  35.2 18.4 %collective-permute-start.8 = (bf16[2,768,384]{2,1,0:T(8,128)(2,1)S(1)}, bf16[2,768,384]{2,1,0:T(8,128)(2,1)S(1)}, u32[]{:S(2)}, u32[]{:S(2)}) collective-permute-start(bf16[2,768,384]{2,1,0:T(8,128)(2,1)S(1)} %collective-permute-done.5.refs_2_), channel_id=1, source_target_pairs={{0,8},{8,0},{16,24},{24,16},{1,9},{9,1},{17,25},{25,17},{2,10},{10... | collective-permute-start | bytes 3538952 | tf_op jit(solution)/shard_map/ppermute | solution.py:44
  35.2 15.7 %collective-permute-start.12 = (bf16[768,384]{1,0:T(8,128)(2,1)S(1)}, bf16[768,384]{1,0:T(8,128)(2,1)S(1)}, u32[]{:S(2)}, u32[]{:S(2)}) collective-permute-start(bf16[768,384]{1,0:T(8,128)(2,1)S(1)} %get-tuple-element.39), channel_id=1, source_target_pairs={{0,16},{8,24},{16,0},{24,8},{1,17},{9,25},{17,1},{25,9},{2,18},{10... | collective-permute-start | bytes 1769480 | tf_op jit(solution)/shard_map/ppermute | solution.py:44
  48.0 4.5 %collective-permute-start.10 = (bf16[2,384,384]{2,1,0:T(8,128)(2,1)S(1)}, bf16[2,384,384]{2,1,0:T(8,128)(2,1)S(1)}, u32[]{:S(2)}, u32[]{:S(2)}) collective-permute-start(bf16[2,384,384]{2,1,0:T(8,128)(2,1)S(1)} %collective-permute-done.7.refs_4_), channel_id=1, source_target_pairs={{0,8},{8,0},{16,24},{24,16},{1,9},{9,1},{17,25},{25,17},{2,10},{10... | collective-permute-start | bytes 1769480 | tf_op jit(solution)/shard_map/ppermute | solution.py:44
  49.5 3.6 %collective-permute-start.9 = (bf16[2,384,384]{2,1,0:T(8,128)(2,1)S(1)}, bf16[2,384,384]{2,1,0:T(8,128)(2,1)S(1)}, u32[]{:S(2)}, u32[]{:S(2)}) collective-permute-start(bf16[2,384,384]{2,1,0:T(8,128)(2,1)S(1)} %collective-permute-done.6.refs_3_), channel_id=1, source_target_pairs={{0,8},{8,0},{16,24},{24,16},{1,9},{9,1},{17,25},{25,17},{2,10},{10... | collective-permute-start | bytes 1769480 | tf_op jit(solution)/shard_map/ppermute | solution.py:44
  51.0 13.4 %collective-permute-start.21 = (bf16[2,256,384]{2,1,0:T(8,128)(2,1)S(1)}, bf16[2,256,384]{2,1,0:T(8,128)(2,1)S(1)}, u32[]{:S(2)}, u32[]{:S(2)}) collective-permute-start(bf16[2,256,384]{2,1,0:T(8,128)(2,1)S(1)} %get-tuple-element.47), channel_id=1, source_target_pairs={{0,16},{8,24},{16,0},{24,8},{1,17},{9,25},{17,1},{25,9},{2,18},{10... | collective-permute-start | bytes 1179656 | tf_op jit(solution)/shard_map/ppermute | solution.py:44
  52.6 11.8 %collective-permute-start.14 = (bf16[384,384]{1,0:T(8,128)(2,1)S(1)}, bf16[384,384]{1,0:T(8,128)(2,1)S(1)}, u32[]{:S(2)}, u32[]{:S(2)}) collective-permute-start(bf16[384,384]{1,0:T(8,128)(2,1)S(1)} %get-tuple-element.62), channel_id=1, source_target_pairs={{0,2},{1,3},{2,0},{3,1},{4,6},{5,7},{6,4},{7,5},{8,10},{9,11},{10,... | collective-permute-start | bytes 884744 | tf_op jit(solution)/shard_map/ppermute | solution.py:44
  53.1 11.5 %collective-permute-start.13 = (bf16[384,384]{1,0:T(8,128)(2,1)S(1)}, bf16[384,384]{1,0:T(8,128)(2,1)S(1)}, u32[]{:S(2)}, u32[]{:S(2)}) collective-permute-start(bf16[384,384]{1,0:T(8,128)(2,1)S(1)} %get-tuple-element.63), channel_id=1, source_target_pairs={{0,1},{1,0},{2,3},{3,2},{4,5},{5,4},{6,7},{7,6},{8,9},{9,8},{10,11... | collective-permute-start | bytes 884744 | tf_op jit(solution)/shard_map/ppermute | solution.py:44
  58.3 8.2 %collective-permute-start.15 = (bf16[768,384]{1,0:T(8,128)(2,1)S(1)}, bf16[768,384]{1,0:T(8,128)(2,1)S(1)}, u32[]{:S(2)}, u32[]{:S(2)}) collective-permute-start(bf16[768,384]{1,0:T(8,128)(2,1)S(1)} %collective-permute-done.12.refs_8_), channel_id=1, source_target_pairs={{0,8},{8,0},{16,24},{24,16},{1,9},{9,1},{17,25},{25,17},{2,10},{10... | collective-permute-start | bytes 1769480 | tf_op jit(solution)/shard_map/ppermute | solution.py:44
  63.4 2.3 %collective-permute-start.11 = (bf16[256,768]{1,0:T(8,128)(2,1)S(1)}, bf16[256,768]{1,0:T(8,128)(2,1)S(1)}, u32[]{:S(2)}, u32[]{:S(2)}) collective-permute-start(bf16[256,768]{1,0:T(8,128)(2,1)S(1)} %get-tuple-element.52.far_ref.refs_0_), channel_id=1, source_target_pairs={{0,8},{8,0},{16,24},{24,16},{1,9},{9,1},{17,25},{25,17},{2,10},{10... | collective-permute-start | bytes 1179656 | tf_op jit(solution)/shard_map/ppermute | solution.py:44
  64.4 12.3 %collective-permute-start.26 = (bf16[256,768]{1,0:T(8,128)(2,1)S(1)}, bf16[256,768]{1,0:T(8,128)(2,1)S(1)}, u32[]{:S(2)}, u32[]{:S(2)}) collective-permute-start(bf16[256,768]{1,0:T(8,128)(2,1)S(1)} %get-tuple-element.52.far_ref.refs_0_), channel_id=1, source_target_pairs={{0,16},{8,24},{16,0},{24,8},{1,17},{9,25},{17,1},{25,9},{2,18},{10... | collective-permute-start | bytes 1179656 | tf_op jit(solution)/shard_map/ppermute | solution.py:44
  64.4 1.8 %collective-permute-start.17 = (bf16[384,384]{1,0:T(8,128)(2,1)S(1)}, bf16[384,384]{1,0:T(8,128)(2,1)S(1)}, u32[]{:S(2)}, u32[]{:S(2)}) collective-permute-start(bf16[384,384]{1,0:T(8,128)(2,1)S(1)} %collective-permute-done.14.refs_10_), channel_id=1, source_target_pairs={{0,8},{8,0},{16,24},{24,16},{1,9},{9,1},{17,25},{25,17},{2,10},{10... | collective-permute-start | bytes 884744 | tf_op jit(solution)/shard_map/ppermute | solution.py:44
  64.6 2.0 %collective-permute-start.16 = (bf16[384,384]{1,0:T(8,128)(2,1)S(1)}, bf16[384,384]{1,0:T(8,128)(2,1)S(1)}, u32[]{:S(2)}, u32[]{:S(2)}) collective-permute-start(bf16[384,384]{1,0:T(8,128)(2,1)S(1)} %collective-permute-done.13.refs_9_), channel_id=1, source_target_pairs={{0,8},{8,0},{16,24},{24,16},{1,9},{9,1},{17,25},{25,17},{2,10},{10... | collective-permute-start | bytes 884744 | tf_op jit(solution)/shard_map/ppermute | solution.py:44
  65.7 12.1 %collective-permute-start.22 = (bf16[2,256,384]{2,1,0:T(8,128)(2,1)S(1)}, bf16[2,256,384]{2,1,0:T(8,128)(2,1)S(1)}, u32[]{:S(2)}, u32[]{:S(2)}) collective-permute-start(bf16[2,256,384]{2,1,0:T(8,128)(2,1)S(1)} %collective-permute-done.21.refs_6_), channel_id=1, source_target_pairs={{0,8},{8,0},{16,24},{24,16},{1,9},{9,1},{17,25},{25,17},{2,10},{10... | collective-permute-start | bytes 1179656 | tf_op jit(solution)/shard_map/ppermute | solution.py:44
  76.7 1.8 %collective-permute-start.27 = (bf16[256,768]{1,0:T(8,128)(2,1)S(1)}, bf16[256,768]{1,0:T(8,128)(2,1)S(1)}, u32[]{:S(2)}, u32[]{:S(2)}) collective-permute-start(bf16[256,768]{1,0:T(8,128)(2,1)S(1)} %collective-permute-done.26.refs_2_), channel_id=1, source_target_pairs={{0,8},{8,0},{16,24},{24,16},{1,9},{9,1},{17,25},{25,17},{2,10},{10... | collective-permute-start | bytes 1179656 | tf_op jit(solution)/shard_map/ppermute | solution.py:44
  76.8 11.5 %collective-permute-start.19 = (bf16[256,768]{1,0:T(8,128)(2,1)S(1)}, bf16[256,768]{1,0:T(8,128)(2,1)S(1)}, u32[]{:S(2)}, u32[]{:S(2)}) collective-permute-start(bf16[256,768]{1,0:T(8,128)(2,1)S(1)} %get-tuple-element.44.near_ref.refs_0_), channel_id=1, source_target_pairs={{0,16},{8,24},{16,0},{24,8},{1,17},{9,25},{17,1},{25,9},{2,18},{10... | collective-permute-start | bytes 1179656 | tf_op jit(solution)/shard_map/ppermute | solution.py:44
  79.6 8.7 %collective-permute-start.28 = (bf16[192,384]{1,0:T(8,128)(2,1)S(1)}, bf16[192,384]{1,0:T(8,128)(2,1)S(1)}, u32[]{:S(2)}, u32[]{:S(2)}) collective-permute-start(bf16[192,384]{1,0:T(8,128)(2,1)S(1)} %get-tuple-element.55), channel_id=1, source_target_pairs={{0,1},{1,0},{2,3},{3,2},{4,5},{5,4},{6,7},{7,6},{8,9},{9,8},{10,11... | collective-permute-start | bytes 442376 | tf_op jit(solution)/shard_map/ppermute | solution.py:44
  81.2 7.1 %collective-permute-start.29 = (bf16[192,384]{1,0:T(8,128)(2,1)S(1)}, bf16[192,384]{1,0:T(8,128)(2,1)S(1)}, u32[]{:S(2)}, u32[]{:S(2)}) collective-permute-start(bf16[192,384]{1,0:T(8,128)(2,1)S(1)} %get-tuple-element.56), channel_id=1, source_target_pairs={{0,2},{1,3},{2,0},{3,1},{4,6},{5,7},{6,4},{7,5},{8,10},{9,11},{10,... | collective-permute-start | bytes 442376 | tf_op jit(solution)/shard_map/ppermute | solution.py:44
  82.7 7.1 %collective-permute-start.30 = (bf16[192,384]{1,0:T(8,128)(2,1)S(1)}, bf16[192,384]{1,0:T(8,128)(2,1)S(1)}, u32[]{:S(2)}, u32[]{:S(2)}) collective-permute-start(bf16[192,384]{1,0:T(8,128)(2,1)S(1)} %get-tuple-element.57), channel_id=1, source_target_pairs={{0,3},{1,2},{2,1},{3,0},{4,7},{5,6},{6,5},{7,4},{8,11},{9,10},{10,... | collective-permute-start | bytes 442376 | tf_op jit(solution)/shard_map/ppermute | solution.py:44
  83.1 9.1 %collective-permute-start.18 = (bf16[256,768]{1,0:T(8,128)(2,1)S(1)}, bf16[256,768]{1,0:T(8,128)(2,1)S(1)}, u32[]{:S(2)}, u32[]{:S(2)}) collective-permute-start(bf16[256,768]{1,0:T(8,128)(2,1)S(1)} %get-tuple-element.44.near_ref.refs_0_), channel_id=1, source_target_pairs={{0,8},{8,0},{16,24},{24,16},{1,9},{9,1},{17,25},{25,17},{2,10},{10... | collective-permute-start | bytes 1179656 | tf_op jit(solution)/shard_map/ppermute | solution.py:44
  88.3 3.9 %collective-permute-start.20 = (bf16[256,768]{1,0:T(8,128)(2,1)S(1)}, bf16[256,768]{1,0:T(8,128)(2,1)S(1)}, u32[]{:S(2)}, u32[]{:S(2)}) collective-permute-start(bf16[256,768]{1,0:T(8,128)(2,1)S(1)} %collective-permute-done.19.refs_2_), channel_id=1, source_target_pairs={{0,8},{8,0},{16,24},{24,16},{1,9},{9,1},{17,25},{25,17},{2,10},{10... | collective-permute-start | bytes 1179656 | tf_op jit(solution)/shard_map/ppermute | solution.py:44
  89.9 11.7 %collective-permute-start.31 = (bf16[192,384]{1,0:T(8,128)(2,1)S(1)}, bf16[192,384]{1,0:T(8,128)(2,1)S(1)}, u32[]{:S(2)}, u32[]{:S(2)}) collective-permute-start(bf16[192,384]{1,0:T(8,128)(2,1)S(1)} %add_convert_fusion), channel_id=1, source_target_pairs={{0,4},{1,5},{2,6},{3,7},{4,0},{5,1},{6,2},{7,3},{8,12},{9,13},{10,... | collective-permute-start | bytes 442376 | tf_op jit(solution)/shard_map/ppermute | solution.py:44
  93.3 8.3 %collective-permute-start.23 = (bf16[192,384]{1,0:T(8,128)(2,1)S(1)}, bf16[192,384]{1,0:T(8,128)(2,1)S(1)}, u32[]{:S(2)}, u32[]{:S(2)}) collective-permute-start(bf16[192,384]{1,0:T(8,128)(2,1)S(1)} %get-tuple-element.49), channel_id=1, source_target_pairs={{0,1},{1,0},{2,3},{3,2},{4,5},{5,4},{6,7},{7,6},{8,9},{9,8},{10,11... | collective-permute-start | bytes 442376 | tf_op jit(solution)/shard_map/ppermute | solution.py:44
  94.9 7.5 %collective-permute-start.24 = (bf16[192,384]{1,0:T(8,128)(2,1)S(1)}, bf16[192,384]{1,0:T(8,128)(2,1)S(1)}, u32[]{:S(2)}, u32[]{:S(2)}) collective-permute-start(bf16[192,384]{1,0:T(8,128)(2,1)S(1)} %get-tuple-element.50), channel_id=1, source_target_pairs={{0,2},{1,3},{2,0},{3,1},{4,6},{5,7},{6,4},{7,5},{8,10},{9,11},{10,... | collective-permute-start | bytes 442376 | tf_op jit(solution)/shard_map/ppermute | solution.py:44
  96.5 8.0 %collective-permute-start.25 = (bf16[192,384]{1,0:T(8,128)(2,1)S(1)}, bf16[192,384]{1,0:T(8,128)(2,1)S(1)}, u32[]{:S(2)}, u32[]{:S(2)}) collective-permute-start(bf16[192,384]{1,0:T(8,128)(2,1)S(1)} %get-tuple-element.51), channel_id=1, source_target_pairs={{0,3},{1,2},{2,1},{3,0},{4,7},{5,6},{6,5},{7,4},{8,11},{9,10},{10,... | collective-permute-start | bytes 442376 | tf_op jit(solution)/shard_map/ppermute | solution.py:44
  (4 other events, 53.6 us)

commit v2 on v1

--- a/solution.py
+++ b/solution.py
@@ -187,28 +187,25 @@
     )(*[in_hbm(block) for block in blocks[:2]], *blocks[2:])
 
 
-def heads_kernel(sources, turn_in_order, act_ref, bias_ref, *refs):
-    weight_refs, (own_ref, out_ref, held, sems) = refs[:-4], refs[-4:]
-    rows = own_ref.shape[0]
-    weight_refs, ahead_ref = weight_refs[:-1], weight_refs[-1]
-    if ahead_ref is not None:
-        out_ref[:, :COLS] = ahead_ref[...]
+def heads_kernel(sources, turn, act_ref, bias_ref, *refs):
+    weight_refs, (out_ref, held, sems) = refs[:-3], refs[-3:]
+    rows = out_ref.shape[0]
     width = act_ref.shape[1]
     half = width // 2
     scale = math.log2(math.e) / math.sqrt(HDIM)
     place, first, flip = place_bits()[1:]
     ring = len(sources) > 1
     if ring:
-        group = 2 * (first ^ (turn_in_order // 2)) + turn_in_order % 2
+        pair = first ^ turn
     else:
-        group, flip = turn_in_order, 0
+        pair, flip = turn, 0
     low_half = pl.ds(pl.multiple_of(flip * half, half), half)
     high_half = pl.ds(pl.multiple_of((1 - flip) * half, half), half)
 
-    def fetch(kind):
-        block = 4 * kind + group
-        sem = sems.at[kind]
-        target = held.at[kind]
+    def fetch(at):
+        block = 4 * (at % 3) + 2 * pair + at // 3
+        sem = sems.at[at]
+        target = held.at[at]
         if ring:
             owner = (block * 11) >> 5
             slot = block - 3 * owner
@@ -245,76 +242,81 @@
                         pltpu.make_async_copy(ref, target.at[start:stop], sem).start()
                         start = stop
 
-    def project(kind, first_row):
-        pltpu.make_async_copy(held.at[kind], held.at[kind], sems.at[kind]).wait()
+    def wait(at):
+        pltpu.make_async_copy(held.at[at], held.at[at], sems.at[at]).wait()
+
+    def project(at, first_row):
         total = jnp.dot(
-            act_ref[first_row:, low_half], held[kind, 0:half], preferred_element_type=jnp.float32
+            act_ref[first_row:, low_half], held[at, 0:half], preferred_element_type=jnp.float32
         ) + jnp.dot(
-            act_ref[first_row:, high_half],
-            held[kind, half:width],
-            preferred_element_type=jnp.float32,
+            act_ref[first_row:, high_half], held[at, half:width], preferred_element_type=jnp.float32
         )
         return total.astype(jnp.bfloat16)
 
-    for kind in range(3):
-        fetch(kind)
-    queries = project(0, rows)
-    keys = project(1, 0)
-    values = project(2, 0)
-    pieces = [None] * (COLS // 128)
-    for head in range(GROUP):
-        low, high = head * HDIM, (head + 1) * HDIM
-        first_tile, last_tile = low // 128, -(-high // 128)
-        window = slice(first_tile * 128, last_tile * 128)
-        lanes = (rows, (last_tile - first_tile) * 128)
-        lane = lax.broadcasted_iota(jnp.int32, lanes, 1) + first_tile * 128
-        mine = (lane >= low) & (lane < high)
-        one = jnp.where(mine, queries[:, window], jnp.zeros((), jnp.bfloat16))
-        scores = lax.dot_general(
-            one, keys[:, window], (((1,), (1,)), ((), ())), preferred_element_type=jnp.float32
-        )
-        scores = scores * scale + bias_ref[...]
-        raw = jnp.exp2(scores - jnp.max(scores, axis=1, keepdims=True))
-        mixed = jnp.dot(
-            raw.astype(jnp.bfloat16), values[:, window], preferred_element_type=jnp.float32
-        ) * (1.0 / jnp.sum(raw, axis=1, keepdims=True))
-        for tile in range(first_tile, last_tile):
-            here = slice((tile - first_tile) * 128, (tile - first_tile + 1) * 128)
-            if pieces[tile] is None:
-                pieces[tile] = mixed[:, here]
-            else:
-                pieces[tile] = jnp.where(mine[:, here], mixed[:, here], pieces[tile])
-    for tile, piece in enumerate(pieces):
-        block = piece.astype(jnp.bfloat16)
-        own_ref[:, tile * 128 : (tile + 1) * 128] = block
-        if ahead_ref is not None:
-            out_ref[:, COLS + tile * 128 : COLS + (tile + 1) * 128] = block
-
-
-def attend(sources, turn_in_order, weights, act, bias, *ahead):
+    def attend_group(group, queries, keys, values):
+        pieces = [None] * (COLS // 128)
+        for head in range(GROUP):
+            low, high = head * HDIM, (head + 1) * HDIM
+            first_tile, last_tile = low // 128, -(-high // 128)
+            window = slice(first_tile * 128, last_tile * 128)
+            base = first_tile * 128
+            lane = lax.broadcasted_iota(jnp.int32, (rows, last_tile * 128 - base), 1) + base
+            mine = (lane >= low) & (lane < high)
+            one = jnp.where(mine, queries[:, window], jnp.zeros((), jnp.bfloat16))
+            scores = lax.dot_general(
+                one, keys[:, window], (((1,), (1,)), ((), ())), preferred_element_type=jnp.float32
+            )
+            scores = scores * scale + bias_ref[...]
+            raw = jnp.exp2(scores - jnp.max(scores, axis=1, keepdims=True)).astype(jnp.bfloat16)
+            spare = high if high < last_tile * 128 else low - 1
+            value = values[:, window]
+            at = lax.broadcasted_iota(jnp.int32, value.shape, 1) + base
+            value = jnp.where(at == spare, jnp.ones((), jnp.bfloat16), value)
+            mixed = jnp.dot(raw, value, preferred_element_type=jnp.float32)
+            mixed = mixed * (1.0 / mixed[:, spare - base : spare - base + 1])
+            for tile in range(first_tile, last_tile):
+                here = slice(tile * 128 - base, (tile + 1) * 128 - base)
+                if pieces[tile] is None:
+                    pieces[tile] = mixed[:, here]
+                else:
+                    pieces[tile] = jnp.where(mine[:, here], mixed[:, here], pieces[tile])
+        for tile, piece in enumerate(pieces):
+            start = group * COLS + tile * 128
+            out_ref[:, start : start + 128] = piece.astype(jnp.bfloat16)
+
+    for at in range(6):
+        fetch(at)
+    ready = []
+    for at in range(3):
+        wait(at)
+        ready.append(project(at, rows if at == 0 else 0))
+    for at in range(3, 6):
+        wait(at)
+    attend_group(0, *ready)
+    attend_group(1, *(project(at, rows if at == 3 else 0) for at in range(3, 6)))
+
+
+def attend(sources, turn, weights, act, bias):
     rows, width = act.shape[0] // 2, act.shape[1]
     vmem = pl.BlockSpec(memory_space=pltpu.VMEM)
     anywhere = pl.BlockSpec(memory_space=pl.ANY)
 
-    def kernel(act_ref, bias_ref, *refs):
-        if not ahead:
-            refs = refs[:-3] + (None, refs[-3], None) + refs[-2:]
-        heads_kernel(sources, turn_in_order, act_ref, bias_ref, *refs)
-
-    outs = [jax.ShapeDtypeStruct((rows, COLS * n), jnp.bfloat16) for n in range(1, 2 + len(ahead))]
+    def kernel(*refs):
+        heads_kernel(sources, turn, *refs)
+
     return pl.pallas_call(
         kernel,
-        out_shape=outs,
-        in_specs=[vmem, vmem] + [anywhere] * len(weights) + [vmem] * len(ahead),
-        out_specs=[vmem] * len(outs),
+        out_shape=jax.ShapeDtypeStruct((rows, 2 * COLS), jnp.bfloat16),
+        in_specs=[vmem, vmem] + [anywhere] * len(weights),
+        out_specs=vmem,
         scratch_shapes=[
-            pltpu.VMEM((3, width, COLS), jnp.bfloat16),
-            pltpu.SemaphoreType.DMA((3,)),
+            pltpu.VMEM((6, width, COLS), jnp.bfloat16),
+            pltpu.SemaphoreType.DMA((6,)),
         ],
-        compiler_params=pltpu.CompilerParams(vmem_limit_bytes=16 * MIB),
+        compiler_params=pltpu.CompilerParams(vmem_limit_bytes=20 * MIB),
         cost_estimate=LITTLE,
-        name=f"attention_{turn_in_order}",
-    )(act, bias, in_hbm(weights[0]), *weights[1:], *ahead)
+        name=f"attention_{turn}",
+    )(act, bias, in_hbm(weights[0]), *weights[1:])
 
 
 def mixed_kernel(far_ref, near_ref, w_ref, out_ref):
@@ -355,12 +357,8 @@
     *attn_refs, cot_0, cot_1, cot_2, cot_3, keep_ref, send_1, send_2, send_3, total = refs
     size = keep_ref.shape[0]
     low = lax.axis_index("tm") & 3
-    for half in range(2):
-        cols = slice(half * COLS, (half + 1) * COLS)
-        blocks = [ref[:, cols] for ref in attn_refs if ref.shape[1] > COLS]
-        blocks += [ref[...] for ref in attn_refs[len(blocks) + half :: 2]]
-        cots = (cot_0[...], cot_1[...], cot_2[0], cot_3[1])
-        total[cols] = sum(product(block, cot) for block, cot in zip(blocks, cots))
+    cots = (cot_0[...], cot_1[...], cot_2[0], cot_3[1])
+    total[...] = sum(product(ref[...], cot) for ref, cot in zip(attn_refs, cots))
     keep_ref[...] = total[pl.ds(pl.multiple_of(low * size, size), size)]
     for bits, ref in enumerate((send_1, send_2, send_3), 1):
         ref[...] = total[pl.ds(pl.multiple_of((low ^ bits) * size, size), size)].astype(
@@ -402,8 +400,8 @@
         sources = [("whole", 0, (0,))]
         attn = jnp.concatenate(
             [
-                attend(sources, group, [gathered], act, bias)[0]
-                for group in range(width // COLS)
+                attend(sources, pair, [gathered], act, bias)
+                for pair in range(width // COLS // 2)
             ],
             1,
         )
@@ -451,7 +449,8 @@
         block = after(block, *earlier)
         side = crossed(block[..., : mid_rows // 2, :], "tm", 1)
         deep = crossed(block[..., mid_rows // 2 :, :], "tm", 2)
-        relays = [crossed(after(b, *relay_after), "dp", 1) for b in (block, side, deep)]
+        relays = [crossed(block, "dp", 1)]
+        relays += [crossed(after(b, *relay_after), "dp", 1) for b in (side, deep)]
         return [block, side, deep] + relays
 
     first_sources = [
@@ -461,25 +460,19 @@
         ("first", 3, (5, 6, 7)),
     ]
     weights = [w_qkv, sibling] + spread(first_over, (act,))
-    first_attn = attend(first_sources, 0, weights, act, bias)[0]
-    far_attn = attend(first_sources, 1, weights, after(act, first_attn), bias, first_attn)[1]
+    far_attn = attend(first_sources, 0, weights, act, bias)
+    far_side = crossed(far_attn, "dp", 1)
 
     sources = first_sources + [("last", 2, (8, 9, 10)), ("last", 3, (11, 12, 13))]
-    weights = weights + spread(last_over, (), (first_attn,))
-    cot_over = crossed(after(cot_two, first_over), "dp", 2)
-    cots = [cot_own, cot_side, cot_over, crossed(cot_over, "dp", 1)]
-
-    def attention(turn, *earlier, ahead=()):
-        return attend(sources, turn, weights, after(act, *earlier), bias, *ahead)
-
-    far_side = crossed(far_attn, "dp", 1)
-    third_attn = attention(2, far_attn, far_side)[0]
-    fourth_attn, near_attn = attention(3, third_attn, ahead=(third_attn,))
+    weights = weights + spread(last_over, (), (far_attn,))
+    cot_over = crossed(after(cot_two, last_over), "dp", 2)
+    near_attn = attend(sources, 1, weights, after(act, far_attn), bias)
+    cots = [cot_own, cot_side, cot_over, crossed(after(cot_over, near_attn), "dp", 1)]
     mixed = project_out([far_attn, near_attn], w_o)
 
     def traded(sums, *sent):
-        for bits, block in enumerate(sent, 1):
-            sums = sums + crossed(block, "tm", bits).astype(jnp.float32)
+        for bits in (3, 2, 1):
+            sums = sums + crossed(sent[bits - 1], "tm", bits).astype(jnp.float32)
         return sums
 
     far_over = crossed(after(far_attn, cot_over), "dp", 2)

time: 106 us -> 103 us (0.972)
  Pallas kernels: 34.5 us -> 30.9 us
  starting transfers between devices: 31.3 us -> 34.5 us
  waiting for transfers between devices: 37.4 us -> 35.3 us
    pallas_call x4 -> x2, Pallas kernels: 19.8 us -> 16.1 us  [attend(): pl.pallas_call(kernel, out_shape=jax.ShapeDtypeStruct((rows, 2 * COLS), j...]
    ppermute x3, waiting for transfers between devices: 10.8 us -> 8.73 us  [shifted(): return lax.ppermute(block, axis, route)]
    ppermute x3, starting transfers between devices: 8.16 us -> 10.1 us  [shifted(): return lax.ppermute(block, axis, route)]
    ppermute x29, starting transfers between devices: 23.2 us -> 24.4 us  [crossed(): return lax.ppermute(block, axis, [(i, i ^ bits) for i in range(count)])]
  transfers between devices with their start and end apart: 32 -> 32, of which waited for: 13 -> 16; matrix products, arithmetic and copies ran while one was open for 0% -> 0% of each run, Pallas kernels for 33% -> 30%
where the time goes in v2:
time: 103 us
  waiting for transfers between devices  35.3 us (34%)
  starting transfers between devices  34.5 us (33%)
  Pallas kernels  30.9 us (30%)
    ppermute x29, waiting for transfers between devices, crossed(): return lax.ppermute(block, axis, [(i, i ^ bits) for i in range(count)])  26.5 us
    ppermute x29, starting transfers between devices, crossed(): return lax.ppermute(block, axis, [(i, i ^ bits) for i in range(count)])  24.4 us
    pallas_call x2, Pallas kernels, attend(): pl.pallas_call(kernel, out_shape=jax.ShapeDtypeStruct((rows, 2 * COLS), j...  16.1 us
    ppermute x3, starting transfers between devices, shifted(): return lax.ppermute(block, axis, route)  10.1 us
    ppermute x3, waiting for transfers between devices, shifted(): return lax.ppermute(block, axis, route)  8.73 us
    pallas_call x1, Pallas kernels, project_out(): pl.pallas_call(mixed_kernel, grid=(width // cols,), out_shape=jax.ShapeDt...  4.77 us
    pallas_call x1, Pallas kernels, conv_silu(): pl.pallas_call(conv_kernel, out_shape=jax.ShapeDtypeStruct((2 * rows, wid...  4.07 us
    pallas_call x2, Pallas kernels, sliced(): pl.pallas_call(kernel, out_shape=out_shape, in_specs=[anywhere] * len(blo...  2.71 us
  transfers between devices with their start and end apart: 32, of which 16 were waited for; matrix products, arithmetic and copies ran while one was open for 0% of the time, Pallas kernels for 30%

profile of v2, /device:TPU:0, one launch (start us, length us, event | category | flops | bytes accessed | tf_op | source)
XLA Modules:
  0.0 102.5 jit_solution(11185546419680771025)
XLA Ops:
  1.2 1.3 %first_slice.1._ = bf16[2,768,384]{2,1,0:T(8,128)(2,1)S(1)} custom-call(bf16[1536,1152]{1,0:T(8,128)(2,1)} %refs_2_.3), custom_call_target="tpu_custom_call" | custom-call | flops 1000000 | bytes 10000 | tf_op jit(solution)/shard_map/first_slice/pallas_call | solution.py:178
  2.5 2.7 %collective-permute-start.5 = (bf16[2,768,384]{2,1,0:T(8,128)(2,1)S(1)}, bf16[2,768,384]{2,1,0:T(8,128)(2,1)S(1)}, u32[]{:S(2)}, u32[]{:S(2)}) collective-permute-start(bf16[2,768,384]{2,1,0:T(8,128)(2,1)S(1)} %first_slice.1._), channel_id=1, source_target_pairs={{0,16},{8,24},{16,0},{24,8},{1,17},{9,25},{17,1},{25,9},{2,18},{10... | collective-permute-start | bytes 3538952 | tf_op jit(solution)/shard_map/ppermute | solution.py:44
  5.2 3.4 %collective-permute-start.1 = (bf16[256,1536]{1,0:T(8,128)(2,1)S(1)}, bf16[256,1536]{1,0:T(8,128)(2,1)S(1)}, u32[]{:S(2)}, u32[]{:S(2)}) collective-permute-start(bf16[256,1536]{1,0:T(8,128)(2,1)S(1)} %copy-done), channel_id=1, source_target_pairs={{0,1},{1,2},{2,3},{3,4},{4,5},{5,6},{6,7},{8,9},{9,10},{10,11},{11... | collective-permute-start | bytes 2359304 | tf_op jit(solution)/shard_map/ppermute | solution.py:39
  8.6 1.4 %later_slices.1 = (bf16[768,384]{1,0:T(8,128)(2,1)S(1)}, bf16[256,384]{1,0:T(8,128)(2,1)S(1)}, bf16[256,384]{1,0:T(8,128)(2,1)S(1)}, bf16[2,256,384]{2,1,0:T(8,128)(2,1)S(1)}) custom-call(bf16[1536,1152]{1,0:T(8,128)(2,1)} %refs_2_.3, bf16[256,1536]{1,0:T(8,128)(2,1)} %cot_ref.1, bf16[2,768,384]{2,1,0:T(8,128)(2,1)S(1)} %first_slice.1._), custom_call_target="tpu_custom_call" | custom-call | flops 1000000 | bytes 10000 | tf_op jit(solution)/shard_map/later_slices/pallas_call | solution.py:178
  10.1 1.3 %collective-permute-start.3 = (bf16[16,1536]{1,0:T(8,128)(2,1)S(1)}, bf16[16,1536]{1,0:T(8,128)(2,1)S(1)}, u32[]{:S(2)}, u32[]{:S(2)}) collective-permute-start(bf16[16,1536]{1,0:T(8,128)(2,1)S(1)} %get-tuple-element.52), channel_id=1, source_target_pairs={{1,0},{2,1},{3,2},{4,3},{5,4},{6,5},{7,6},{9,8},{10,9},{11,10},{12... | collective-permute-start | bytes 147464 | tf_op jit(solution)/shard_map/ppermute | solution.py:39
  11.5 5.4 %collective-permute-start = (bf16[16,1536]{1,0:T(8,128)(2,1)S(1)}, bf16[16,1536]{1,0:T(8,128)(2,1)S(1)}, u32[]{:S(2)}, u32[]{:S(2)}) collective-permute-start(bf16[16,1536]{1,0:T(8,128)(2,1)S(1)} %get-tuple-element.53), channel_id=1, source_target_pairs={{0,2},{1,3},{2,4},{3,5},{4,6},{5,7},{8,10},{9,11},{10,12},{11,13},... | collective-permute-start | bytes 147464 | tf_op jit(solution)/shard_map/ppermute | solution.py:39
  17.0 1.0 %masks.1 = (f32[512,128]{1,0:T(8,128)S(1)}, f32[256,512]{1,0:T(8,128)S(1)}) custom-call(s32[1,8]{1,0:T(1,128)S(1)} %copy-done.3, s32[1,2048]{1,0:T(1,128)S(1)} %copy-done.2), custom_call_target="tpu_custom_call" | custom-call | flops 1000000 | bytes 10000 | tf_op jit(solution)/shard_map/masks/pallas_call | solution.py:83
  18.7 8.1 %collective-permute-done.1.prev_ref = bf16[256,1536]{1,0:T(8,128)(2,1)S(1)} collective-permute-done((bf16[256,1536]{1,0:T(8,128)(2,1)S(1)}, bf16[256,1536]{1,0:T(8,128)(2,1)S(1)}, u32[]{:S(2)}, u32[]{:S(2)}) %collective-permute-start.1) | collective-permute-done | bytes 786464 | tf_op jit(solution)/shard_map/ppermute | solution.py:39
  26.7 4.1 %conv_silu.1.refs_0_ = bf16[512,1536]{1,0:T(8,128)(2,1)S(1)} custom-call(bf16[16,1536]{1,0:T(8,128)(2,1)S(1)} %collective-permute-done.far_ref, bf16[256,1536]{1,0:T(8,128)(2,1)S(1)} %collective-permute-done.1.prev_ref, bf16[256,1536]{1,0:T(8,128)(2,1)S(1)} %copy-done, bf16[16,1536]{1,0:T(8,128)(2,1)S(1)} %collective-permute-done.3.next_ref, ...), custom_call_target="tpu_custom_call" | custom-call | flops 1000000 | bytes 10000 | tf_op jit(solution)/shard_map/conv_silu/pallas_call | solution.py:132
  30.8 0.9 collective-permute-done.5.refs_4_
  31.9 2.6 %collective-permute-start.7 = (bf16[2,384,384]{2,1,0:T(8,128)(2,1)S(1)}, bf16[2,384,384]{2,1,0:T(8,128)(2,1)S(1)}, u32[]{:S(2)}, u32[]{:S(2)}) collective-permute-start(bf16[2,384,384]{2,1,0:T(8,128)(2,1)S(1)} %get-tuple-element.50), channel_id=1, source_target_pairs={{0,2},{1,3},{2,0},{3,1},{4,6},{5,7},{6,4},{7,5},{8,10},{9,11},{10,... | collective-permute-start | bytes 1769480 | tf_op jit(solution)/shard_map/ppermute | solution.py:44
  35.2 1.5 %collective-permute-start.11 = (bf16[768,384]{1,0:T(8,128)(2,1)S(1)}, bf16[768,384]{1,0:T(8,128)(2,1)S(1)}, u32[]{:S(2)}, u32[]{:S(2)}) collective-permute-start(bf16[768,384]{1,0:T(8,128)(2,1)S(1)} %get-tuple-element.33), channel_id=1, source_target_pairs={{0,16},{8,24},{16,0},{24,8},{1,17},{9,25},{17,1},{25,9},{2,18},{10... | collective-permute-start | bytes 1769480 | tf_op jit(solution)/shard_map/ppermute | solution.py:44
  36.8 11.3 %collective-permute-done.7.refs_6_ = bf16[2,384,384]{2,1,0:T(8,128)(2,1)S(1)} collective-permute-done((bf16[2,384,384]{2,1,0:T(8,128)(2,1)S(1)}, bf16[2,384,384]{2,1,0:T(8,128)(2,1)S(1)}, u32[]{:S(2)}, u32[]{:S(2)}) %collective-permute-start.7) | collective-permute-done | bytes 589856 | tf_op jit(solution)/shard_map/ppermute | solution.py:44
  48.1 1.5 %collective-permute-done.6.refs_5_ = bf16[2,384,384]{2,1,0:T(8,128)(2,1)S(1)} collective-permute-done((bf16[2,384,384]{2,1,0:T(8,128)(2,1)S(1)}, bf16[2,384,384]{2,1,0:T(8,128)(2,1)S(1)}, u32[]{:S(2)}, u32[]{:S(2)}) %collective-permute-start.6) | collective-permute-done | bytes 589856 | tf_op jit(solution)/shard_map/ppermute | solution.py:44
  49.5 1.4 %collective-permute-done.11.refs_10_ = bf16[768,384]{1,0:T(8,128)(2,1)S(1)} collective-permute-done((bf16[768,384]{1,0:T(8,128)(2,1)S(1)}, bf16[768,384]{1,0:T(8,128)(2,1)S(1)}, u32[]{:S(2)}, u32[]{:S(2)}) %collective-permute-start.11) | collective-permute-done | bytes 589856 | tf_op jit(solution)/shard_map/ppermute | solution.py:44
  51.0 1.5 %collective-permute-start.20 = (bf16[2,256,384]{2,1,0:T(8,128)(2,1)S(1)}, bf16[2,256,384]{2,1,0:T(8,128)(2,1)S(1)}, u32[]{:S(2)}, u32[]{:S(2)}) collective-permute-start(bf16[2,256,384]{2,1,0:T(8,128)(2,1)S(1)} %get-tuple-element.38), channel_id=1, source_target_pairs={{0,16},{8,24},{16,0},{24,8},{1,17},{9,25},{17,1},{25,9},{2,18},{10... | collective-permute-start | bytes 1179656 | tf_op jit(solution)/shard_map/ppermute | solution.py:44
  53.6 8.2 %attention_0.1.far_ref.refs_0_ = bf16[256,768]{1,0:T(8,128)(2,1)S(1)} custom-call(bf16[512,1536]{1,0:T(8,128)(2,1)S(1)} %conv_silu.1.refs_0_, f32[256,512]{1,0:T(8,128)S(1)} %get-tuple-element.30.refs_1_, bf16[1536,1152]{1,0:T(8,128)(2,1)} %refs_2_.3, bf16[1536,1152]{1,0:T(8,128)(2,1)S(1)} %collective-permute-done.4.refs_3_, ...), custom_call_target="tpu_custom_call" | custom-call | flops 1000000 | bytes 10000 | tf_op jit(solution)/shard_map/attention_0/pallas_call | solution.py:307
  61.8 1.4 %collective-permute-start.26 = (bf16[256,768]{1,0:T(8,128)(2,1)S(1)}, bf16[256,768]{1,0:T(8,128)(2,1)S(1)}, u32[]{:S(2)}, u32[]{:S(2)}) collective-permute-start(bf16[256,768]{1,0:T(8,128)(2,1)S(1)} %attention_0.1.far_ref.refs_0_), channel_id=1, source_target_pairs={{0,16},{8,24},{16,0},{24,8},{1,17},{9,25},{17,1},{25,9},{2,18},{10... | collective-permute-start | bytes 1179656 | tf_op jit(solution)/shard_map/ppermute | solution.py:44
  63.8 1.0 collective-permute-done.15.refs_14_
  65.3 8.0 %attention_1.1.near_ref.refs_0_ = bf16[256,768]{1,0:T(8,128)(2,1)S(1)} custom-call(bf16[512,1536]{1,0:T(8,128)(2,1)S(1)} %conv_silu.1.refs_0_, f32[256,512]{1,0:T(8,128)S(1)} %get-tuple-element.30.refs_1_, bf16[1536,1152]{1,0:T(8,128)(2,1)} %refs_2_.3, bf16[1536,1152]{1,0:T(8,128)(2,1)S(1)} %collective-permute-done.4.refs_3_, ...), custom_call_target="tpu_custom_call" | custom-call | flops 1000000 | bytes 10000 | tf_op jit(solution)/shard_map/attention_1/pallas_call | solution.py:307
  73.8 1.0 collective-permute-start.18
  75.6 1.1 %far.1 = (f32[192,384]{1,0:T(8,128)S(1)}, bf16[192,384]{1,0:T(8,128)(2,1)S(1)}, bf16[192,384]{1,0:T(8,128)(2,1)S(1)}, bf16[192,384]{1,0:T(8,128)(2,1)S(1)}) custom-call(bf16[256,768]{1,0:T(8,128)(2,1)S(1)} %attention_0.1.far_ref.refs_0_, bf16[256,768]{1,0:T(8,128)(2,1)S(1)} %collective-permute-done.25.refs_1_, ...), custom_call_target="tpu_custom_call" | custom-call | flops 1000000 | bytes 10000 | tf_op jit(solution)/shard_map/far/pallas_call | solution.py:372
  76.7 2.1 %collective-permute-start.28 = (bf16[192,384]{1,0:T(8,128)(2,1)S(1)}, bf16[192,384]{1,0:T(8,128)(2,1)S(1)}, u32[]{:S(2)}, u32[]{:S(2)}) collective-permute-start(bf16[192,384]{1,0:T(8,128)(2,1)S(1)} %get-tuple-element.47), channel_id=1, source_target_pairs={{0,3},{1,2},{2,1},{3,0},{4,7},{5,6},{6,5},{7,4},{8,11},{9,10},{10,... | collective-permute-start | bytes 442376 | tf_op jit(solution)/shard_map/ppermute | solution.py:44
  79.2 1.0 collective-permute-start.30
  80.2 4.7 %collective-permute-done.18.refs_2_ = bf16[256,768]{1,0:T(8,128)(2,1)S(1)} collective-permute-done((bf16[256,768]{1,0:T(8,128)(2,1)S(1)}, bf16[256,768]{1,0:T(8,128)(2,1)S(1)}, u32[]{:S(2)}, u32[]{:S(2)}) %collective-permute-start.18) | collective-permute-done | bytes 393248 | tf_op jit(solution)/shard_map/ppermute | solution.py:44
  84.9 1.3 %collective-permute-done.29 = bf16[192,384]{1,0:T(8,128)(2,1)S(1)} collective-permute-done((bf16[192,384]{1,0:T(8,128)(2,1)S(1)}, bf16[192,384]{1,0:T(8,128)(2,1)S(1)}, u32[]{:S(2)}, u32[]{:S(2)}) %collective-permute-start.29) | collective-permute-done | bytes 147488 | tf_op jit(solution)/shard_map/ppermute | solution.py:44
  86.7 3.0 %collective-permute-start.31 = (bf16[192,384]{1,0:T(8,128)(2,1)S(1)}, bf16[192,384]{1,0:T(8,128)(2,1)S(1)}, u32[]{:S(2)}, u32[]{:S(2)}) collective-permute-start(bf16[192,384]{1,0:T(8,128)(2,1)S(1)} %add_convert_fusion), channel_id=1, source_target_pairs={{0,4},{1,5},{2,6},{3,7},{4,0},{5,1},{6,2},{7,3},{8,12},{9,13},{10,... | collective-permute-start | bytes 442376 | tf_op jit(solution)/shard_map/ppermute | solution.py:44
  89.7 1.1 %near.1 = (f32[192,384]{1,0:T(8,128)S(1)}, bf16[192,384]{1,0:T(8,128)(2,1)S(1)}, bf16[192,384]{1,0:T(8,128)(2,1)S(1)}, bf16[192,384]{1,0:T(8,128)(2,1)S(1)}) custom-call(bf16[256,768]{1,0:T(8,128)(2,1)S(1)} %attention_1.1.near_ref.refs_0_, bf16[256,768]{1,0:T(8,128)(2,1)S(1)} %collective-permute-done.17.refs_1_, ...), custom_call_target="tpu_custom_call" | custom-call | flops 1000000 | bytes 10000 | tf_op jit(solution)/shard_map/near/pallas_call | solution.py:372
  90.8 1.8 %collective-permute-start.22 = (bf16[192,384]{1,0:T(8,128)(2,1)S(1)}, bf16[192,384]{1,0:T(8,128)(2,1)S(1)}, u32[]{:S(2)}, u32[]{:S(2)}) collective-permute-start(bf16[192,384]{1,0:T(8,128)(2,1)S(1)} %get-tuple-element.41), channel_id=1, source_target_pairs={{0,3},{1,2},{2,1},{3,0},{4,7},{5,6},{6,5},{7,4},{8,11},{9,10},{10,... | collective-permute-start | bytes 442376 | tf_op jit(solution)/shard_map/ppermute | solution.py:44
  93.0 1.4 %collective-permute-start.24 = (bf16[192,384]{1,0:T(8,128)(2,1)S(1)}, bf16[192,384]{1,0:T(8,128)(2,1)S(1)}, u32[]{:S(2)}, u32[]{:S(2)}) collective-permute-start(bf16[192,384]{1,0:T(8,128)(2,1)S(1)} %get-tuple-element.43), channel_id=1, source_target_pairs={{0,1},{1,0},{2,3},{3,2},{4,5},{5,4},{6,7},{7,6},{8,9},{9,8},{10,11... | collective-permute-start | bytes 442376 | tf_op jit(solution)/shard_map/ppermute | solution.py:44
  94.4 4.8 %mixed.1 = bf16[256,1536]{1,0:T(8,128)(2,1)} custom-call(bf16[256,768]{1,0:T(8,128)(2,1)S(1)} %attention_0.1.far_ref.refs_0_, bf16[256,768]{1,0:T(8,128)(2,1)S(1)} %attention_1.1.near_ref.refs_0_, bf16[1536,1536]{1,0:T(8,128)(2,1)} %w_ref.5), custom_call_target="tpu_custom_call" | custom-call | flops 1000000 | bytes 10000 | tf_op jit(solution)/shard_map/mixed/pallas_call | solution.py:337
  100.0 1.7 %collective-permute-done.23 = bf16[192,384]{1,0:T(8,128)(2,1)S(1)} collective-permute-done((bf16[192,384]{1,0:T(8,128)(2,1)S(1)}, bf16[192,384]{1,0:T(8,128)(2,1)S(1)}, u32[]{:S(2)}, u32[]{:S(2)}) %collective-permute-start.23) | collective-permute-done | bytes 147488 | tf_op jit(solution)/shard_map/ppermute | solution.py:44
  (54 shorter events, 8.8 us)
Async XLA Ops:
  0.6 53.0 %collective-permute-start.4 = (bf16[1536,1152]{1,0:T(8,128)(2,1)}, bf16[1536,1152]{1,0:T(8,128)(2,1)S(1)}, u32[]{:S(2)}, u32[]{:S(2)}) collective-permute-start(bf16[1536,1152]{1,0:T(8,128)(2,1)} %refs_2_.3), channel_id=1, source_target_pairs={{0,8},{8,0},{16,24},{24,16},{1,9},{9,1},{17,25},{25,17},{2,10},{10... | collective-permute-start | bytes 10616840 | tf_op jit(solution)/shard_map/ppermute | solution.py:44
  2.5 29.2 %collective-permute-start.5 = (bf16[2,768,384]{2,1,0:T(8,128)(2,1)S(1)}, bf16[2,768,384]{2,1,0:T(8,128)(2,1)S(1)}, u32[]{:S(2)}, u32[]{:S(2)}) collective-permute-start(bf16[2,768,384]{2,1,0:T(8,128)(2,1)S(1)} %first_slice.1._), channel_id=1, source_target_pairs={{0,16},{8,24},{16,0},{24,8},{1,17},{9,25},{17,1},{25,9},{2,18},{10... | collective-permute-start | bytes 3538952 | tf_op jit(solution)/shard_map/ppermute | solution.py:44
  5.2 21.5 %collective-permute-start.1 = (bf16[256,1536]{1,0:T(8,128)(2,1)S(1)}, bf16[256,1536]{1,0:T(8,128)(2,1)S(1)}, u32[]{:S(2)}, u32[]{:S(2)}) collective-permute-start(bf16[256,1536]{1,0:T(8,128)(2,1)S(1)} %copy-done), channel_id=1, source_target_pairs={{0,1},{1,2},{2,3},{3,4},{4,5},{5,6},{6,7},{8,9},{9,10},{10,11},{11... | collective-permute-start | bytes 2359304 | tf_op jit(solution)/shard_map/ppermute | solution.py:39
  10.0 1.5 %collective-permute-start.2 = (bf16[256,384]{1,0:T(8,128)(2,1)S(1)}, bf16[256,384]{1,0:T(8,128)(2,1)S(1)}, u32[]{:S(2)}, u32[]{:S(2)}) collective-permute-start(bf16[256,384]{1,0:T(8,128)(2,1)S(1)} %get-tuple-element.26), channel_id=1, source_target_pairs={{0,8},{8,0},{16,24},{24,16},{1,9},{9,1},{17,25},{25,17},{2,10},{10... | collective-permute-start | bytes 589832 | tf_op jit(solution)/shard_map/ppermute | solution.py:44
  10.1 7.9 %collective-permute-start.3 = (bf16[16,1536]{1,0:T(8,128)(2,1)S(1)}, bf16[16,1536]{1,0:T(8,128)(2,1)S(1)}, u32[]{:S(2)}, u32[]{:S(2)}) collective-permute-start(bf16[16,1536]{1,0:T(8,128)(2,1)S(1)} %get-tuple-element.52), channel_id=1, source_target_pairs={{1,0},{2,1},{3,2},{4,3},{5,4},{6,5},{7,6},{9,8},{10,9},{11,10},{12... | collective-permute-start | bytes 147464 | tf_op jit(solution)/shard_map/ppermute | solution.py:39
  11.5 7.1 %collective-permute-start = (bf16[16,1536]{1,0:T(8,128)(2,1)S(1)}, bf16[16,1536]{1,0:T(8,128)(2,1)S(1)}, u32[]{:S(2)}, u32[]{:S(2)}) collective-permute-start(bf16[16,1536]{1,0:T(8,128)(2,1)S(1)} %get-tuple-element.53), channel_id=1, source_target_pairs={{0,2},{1,3},{2,4},{3,5},{4,6},{5,7},{8,10},{9,11},{10,12},{11,13},... | collective-permute-start | bytes 147464 | tf_op jit(solution)/shard_map/ppermute | solution.py:39
  31.9 16.2 %collective-permute-start.7 = (bf16[2,384,384]{2,1,0:T(8,128)(2,1)S(1)}, bf16[2,384,384]{2,1,0:T(8,128)(2,1)S(1)}, u32[]{:S(2)}, u32[]{:S(2)}) collective-permute-start(bf16[2,384,384]{2,1,0:T(8,128)(2,1)S(1)} %get-tuple-element.50), channel_id=1, source_target_pairs={{0,2},{1,3},{2,0},{3,1},{4,6},{5,7},{6,4},{7,5},{8,10},{9,11},{10,... | collective-permute-start | bytes 1769480 | tf_op jit(solution)/shard_map/ppermute | solution.py:44
  34.5 15.0 %collective-permute-start.6 = (bf16[2,384,384]{2,1,0:T(8,128)(2,1)S(1)}, bf16[2,384,384]{2,1,0:T(8,128)(2,1)S(1)}, u32[]{:S(2)}, u32[]{:S(2)}) collective-permute-start(bf16[2,384,384]{2,1,0:T(8,128)(2,1)S(1)} %get-tuple-element.51), channel_id=1, source_target_pairs={{0,1},{1,0},{2,3},{3,2},{4,5},{5,4},{6,7},{7,6},{8,9},{9,8},{10,11... | collective-permute-start | bytes 1769480 | tf_op jit(solution)/shard_map/ppermute | solution.py:44
  35.2 18.4 %collective-permute-start.8 = (bf16[2,768,384]{2,1,0:T(8,128)(2,1)S(1)}, bf16[2,768,384]{2,1,0:T(8,128)(2,1)S(1)}, u32[]{:S(2)}, u32[]{:S(2)}) collective-permute-start(bf16[2,768,384]{2,1,0:T(8,128)(2,1)S(1)} %collective-permute-done.5.refs_4_), channel_id=1, source_target_pairs={{0,8},{8,0},{16,24},{24,16},{1,9},{9,1},{17,25},{25,17},{2,10},{10... | collective-permute-start | bytes 3538952 | tf_op jit(solution)/shard_map/ppermute | solution.py:44
  35.2 15.7 %collective-permute-start.11 = (bf16[768,384]{1,0:T(8,128)(2,1)S(1)}, bf16[768,384]{1,0:T(8,128)(2,1)S(1)}, u32[]{:S(2)}, u32[]{:S(2)}) collective-permute-start(bf16[768,384]{1,0:T(8,128)(2,1)S(1)} %get-tuple-element.33), channel_id=1, source_target_pairs={{0,16},{8,24},{16,0},{24,8},{1,17},{9,25},{17,1},{25,9},{2,18},{10... | collective-permute-start | bytes 1769480 | tf_op jit(solution)/shard_map/ppermute | solution.py:44
  48.1 4.5 %collective-permute-start.10 = (bf16[2,384,384]{2,1,0:T(8,128)(2,1)S(1)}, bf16[2,384,384]{2,1,0:T(8,128)(2,1)S(1)}, u32[]{:S(2)}, u32[]{:S(2)}) collective-permute-start(bf16[2,384,384]{2,1,0:T(8,128)(2,1)S(1)} %collective-permute-done.7.refs_6_), channel_id=1, source_target_pairs={{0,8},{8,0},{16,24},{24,16},{1,9},{9,1},{17,25},{25,17},{2,10},{10... | collective-permute-start | bytes 1769480 | tf_op jit(solution)/shard_map/ppermute | solution.py:44
  49.5 3.6 %collective-permute-start.9 = (bf16[2,384,384]{2,1,0:T(8,128)(2,1)S(1)}, bf16[2,384,384]{2,1,0:T(8,128)(2,1)S(1)}, u32[]{:S(2)}, u32[]{:S(2)}) collective-permute-start(bf16[2,384,384]{2,1,0:T(8,128)(2,1)S(1)} %collective-permute-done.6.refs_5_), channel_id=1, source_target_pairs={{0,8},{8,0},{16,24},{24,16},{1,9},{9,1},{17,25},{25,17},{2,10},{10... | collective-permute-start | bytes 1769480 | tf_op jit(solution)/shard_map/ppermute | solution.py:44
  51.0 10.8 %collective-permute-start.20 = (bf16[2,256,384]{2,1,0:T(8,128)(2,1)S(1)}, bf16[2,256,384]{2,1,0:T(8,128)(2,1)S(1)}, u32[]{:S(2)}, u32[]{:S(2)}) collective-permute-start(bf16[2,256,384]{2,1,0:T(8,128)(2,1)S(1)} %get-tuple-element.38), channel_id=1, source_target_pairs={{0,16},{8,24},{16,0},{24,8},{1,17},{9,25},{17,1},{25,9},{2,18},{10... | collective-permute-start | bytes 1179656 | tf_op jit(solution)/shard_map/ppermute | solution.py:44
  52.6 10.7 %collective-permute-start.13 = (bf16[384,384]{1,0:T(8,128)(2,1)S(1)}, bf16[384,384]{1,0:T(8,128)(2,1)S(1)}, u32[]{:S(2)}, u32[]{:S(2)}) collective-permute-start(bf16[384,384]{1,0:T(8,128)(2,1)S(1)} %get-tuple-element.54), channel_id=1, source_target_pairs={{0,2},{1,3},{2,0},{3,1},{4,6},{5,7},{6,4},{7,5},{8,10},{9,11},{10,... | collective-permute-start | bytes 884744 | tf_op jit(solution)/shard_map/ppermute | solution.py:44
  53.1 10.2 %collective-permute-start.12 = (bf16[384,384]{1,0:T(8,128)(2,1)S(1)}, bf16[384,384]{1,0:T(8,128)(2,1)S(1)}, u32[]{:S(2)}, u32[]{:S(2)}) collective-permute-start(bf16[384,384]{1,0:T(8,128)(2,1)S(1)} %get-tuple-element.55), channel_id=1, source_target_pairs={{0,1},{1,0},{2,3},{3,2},{4,5},{5,4},{6,7},{7,6},{8,9},{9,8},{10,11... | collective-permute-start | bytes 884744 | tf_op jit(solution)/shard_map/ppermute | solution.py:44
  53.6 10.2 %collective-permute-start.14 = (bf16[768,384]{1,0:T(8,128)(2,1)S(1)}, bf16[768,384]{1,0:T(8,128)(2,1)S(1)}, u32[]{:S(2)}, u32[]{:S(2)}) collective-permute-start(bf16[768,384]{1,0:T(8,128)(2,1)S(1)} %collective-permute-done.11.refs_10_), channel_id=1, source_target_pairs={{0,8},{8,0},{16,24},{24,16},{1,9},{9,1},{17,25},{25,17},{2,10},{10... | collective-permute-start | bytes 1769480 | tf_op jit(solution)/shard_map/ppermute | solution.py:44
  61.8 11.6 %collective-permute-start.26 = (bf16[256,768]{1,0:T(8,128)(2,1)S(1)}, bf16[256,768]{1,0:T(8,128)(2,1)S(1)}, u32[]{:S(2)}, u32[]{:S(2)}) collective-permute-start(bf16[256,768]{1,0:T(8,128)(2,1)S(1)} %attention_0.1.far_ref.refs_0_), channel_id=1, source_target_pairs={{0,16},{8,24},{16,0},{24,8},{1,17},{9,25},{17,1},{25,9},{2,18},{10... | collective-permute-start | bytes 1179656 | tf_op jit(solution)/shard_map/ppermute | solution.py:44
  63.3 1.6 %collective-permute-start.15 = (bf16[384,384]{1,0:T(8,128)(2,1)S(1)}, bf16[384,384]{1,0:T(8,128)(2,1)S(1)}, u32[]{:S(2)}, u32[]{:S(2)}) collective-permute-start(bf16[384,384]{1,0:T(8,128)(2,1)S(1)} %collective-permute-done.12.refs_11_), channel_id=1, source_target_pairs={{0,8},{8,0},{16,24},{24,16},{1,9},{9,1},{17,25},{25,17},{2,10},{10... | collective-permute-start | bytes 884744 | tf_op jit(solution)/shard_map/ppermute | solution.py:44
  63.3 2.0 %collective-permute-start.16 = (bf16[384,384]{1,0:T(8,128)(2,1)S(1)}, bf16[384,384]{1,0:T(8,128)(2,1)S(1)}, u32[]{:S(2)}, u32[]{:S(2)}) collective-permute-start(bf16[384,384]{1,0:T(8,128)(2,1)S(1)} %collective-permute-done.13.refs_12_), channel_id=1, source_target_pairs={{0,8},{8,0},{16,24},{24,16},{1,9},{9,1},{17,25},{25,17},{2,10},{10... | collective-permute-start | bytes 884744 | tf_op jit(solution)/shard_map/ppermute | solution.py:44
  63.8 11.0 %collective-permute-start.25 = (bf16[256,768]{1,0:T(8,128)(2,1)S(1)}, bf16[256,768]{1,0:T(8,128)(2,1)S(1)}, u32[]{:S(2)}, u32[]{:S(2)}) collective-permute-start(bf16[256,768]{1,0:T(8,128)(2,1)S(1)} %attention_0.1.far_ref.refs_0_), channel_id=1, source_target_pairs={{0,8},{8,0},{16,24},{24,16},{1,9},{9,1},{17,25},{25,17},{2,10},{10... | collective-permute-start | bytes 1179656 | tf_op jit(solution)/shard_map/ppermute | solution.py:44
  73.2 1.8 %collective-permute-start.21 = (bf16[2,256,384]{2,1,0:T(8,128)(2,1)S(1)}, bf16[2,256,384]{2,1,0:T(8,128)(2,1)S(1)}, u32[]{:S(2)}, u32[]{:S(2)}) collective-permute-start(bf16[2,256,384]{2,1,0:T(8,128)(2,1)S(1)} %collective-permute-done.20.refs_6_), channel_id=1, source_target_pairs={{0,8},{8,0},{16,24},{24,16},{1,9},{9,1},{17,25},{25,17},{2,10},{10... | collective-permute-start | bytes 1179656 | tf_op jit(solution)/shard_map/ppermute | solution.py:44
  73.4 2.2 %collective-permute-start.27 = (bf16[256,768]{1,0:T(8,128)(2,1)S(1)}, bf16[256,768]{1,0:T(8,128)(2,1)S(1)}, u32[]{:S(2)}, u32[]{:S(2)}) collective-permute-start(bf16[256,768]{1,0:T(8,128)(2,1)S(1)} %collective-permute-done.26.refs_2_), channel_id=1, source_target_pairs={{0,8},{8,0},{16,24},{24,16},{1,9},{9,1},{17,25},{25,17},{2,10},{10... | collective-permute-start | bytes 1179656 | tf_op jit(solution)/shard_map/ppermute | solution.py:44
  73.8 11.1 %collective-permute-start.18 = (bf16[256,768]{1,0:T(8,128)(2,1)S(1)}, bf16[256,768]{1,0:T(8,128)(2,1)S(1)}, u32[]{:S(2)}, u32[]{:S(2)}) collective-permute-start(bf16[256,768]{1,0:T(8,128)(2,1)S(1)} %attention_1.1.near_ref.refs_0_), channel_id=1, source_target_pairs={{0,16},{8,24},{16,0},{24,8},{1,17},{9,25},{17,1},{25,9},{2,18},{10... | collective-permute-start | bytes 1179656 | tf_op jit(solution)/shard_map/ppermute | solution.py:44
  76.7 8.3 %collective-permute-start.28 = (bf16[192,384]{1,0:T(8,128)(2,1)S(1)}, bf16[192,384]{1,0:T(8,128)(2,1)S(1)}, u32[]{:S(2)}, u32[]{:S(2)}) collective-permute-start(bf16[192,384]{1,0:T(8,128)(2,1)S(1)} %get-tuple-element.47), channel_id=1, source_target_pairs={{0,3},{1,2},{2,1},{3,0},{4,7},{5,6},{6,5},{7,4},{8,11},{9,10},{10,... | collective-permute-start | bytes 442376 | tf_op jit(solution)/shard_map/ppermute | solution.py:44
  78.8 7.5 %collective-permute-start.29 = (bf16[192,384]{1,0:T(8,128)(2,1)S(1)}, bf16[192,384]{1,0:T(8,128)(2,1)S(1)}, u32[]{:S(2)}, u32[]{:S(2)}) collective-permute-start(bf16[192,384]{1,0:T(8,128)(2,1)S(1)} %get-tuple-element.48), channel_id=1, source_target_pairs={{0,2},{1,3},{2,0},{3,1},{4,6},{5,7},{6,4},{7,5},{8,10},{9,11},{10,... | collective-permute-start | bytes 442376 | tf_op jit(solution)/shard_map/ppermute | solution.py:44
  79.2 7.5 %collective-permute-start.30 = (bf16[192,384]{1,0:T(8,128)(2,1)S(1)}, bf16[192,384]{1,0:T(8,128)(2,1)S(1)}, u32[]{:S(2)}, u32[]{:S(2)}) collective-permute-start(bf16[192,384]{1,0:T(8,128)(2,1)S(1)} %get-tuple-element.49), channel_id=1, source_target_pairs={{0,1},{1,0},{2,3},{3,2},{4,5},{5,4},{6,7},{7,6},{8,9},{9,8},{10,11... | collective-permute-start | bytes 442376 | tf_op jit(solution)/shard_map/ppermute | solution.py:44
  80.2 9.5 %collective-permute-start.17 = (bf16[256,768]{1,0:T(8,128)(2,1)S(1)}, bf16[256,768]{1,0:T(8,128)(2,1)S(1)}, u32[]{:S(2)}, u32[]{:S(2)}) collective-permute-start(bf16[256,768]{1,0:T(8,128)(2,1)S(1)} %attention_1.1.near_ref.refs_0_), channel_id=1, source_target_pairs={{0,8},{8,0},{16,24},{24,16},{1,9},{9,1},{17,25},{25,17},{2,10},{10... | collective-permute-start | bytes 1179656 | tf_op jit(solution)/shard_map/ppermute | solution.py:44
  84.9 4.8 %collective-permute-start.19 = (bf16[256,768]{1,0:T(8,128)(2,1)S(1)}, bf16[256,768]{1,0:T(8,128)(2,1)S(1)}, u32[]{:S(2)}, u32[]{:S(2)}) collective-permute-start(bf16[256,768]{1,0:T(8,128)(2,1)S(1)} %collective-permute-done.18.refs_2_), channel_id=1, source_target_pairs={{0,8},{8,0},{16,24},{24,16},{1,9},{9,1},{17,25},{25,17},{2,10},{10... | collective-permute-start | bytes 1179656 | tf_op jit(solution)/shard_map/ppermute | solution.py:44
  86.7 12.4 %collective-permute-start.31 = (bf16[192,384]{1,0:T(8,128)(2,1)S(1)}, bf16[192,384]{1,0:T(8,128)(2,1)S(1)}, u32[]{:S(2)}, u32[]{:S(2)}) collective-permute-start(bf16[192,384]{1,0:T(8,128)(2,1)S(1)} %add_convert_fusion), channel_id=1, source_target_pairs={{0,4},{1,5},{2,6},{3,7},{4,0},{5,1},{6,2},{7,3},{8,12},{9,13},{10,... | collective-permute-start | bytes 442376 | tf_op jit(solution)/shard_map/ppermute | solution.py:44
  90.8 9.2 %collective-permute-start.22 = (bf16[192,384]{1,0:T(8,128)(2,1)S(1)}, bf16[192,384]{1,0:T(8,128)(2,1)S(1)}, u32[]{:S(2)}, u32[]{:S(2)}) collective-permute-start(bf16[192,384]{1,0:T(8,128)(2,1)S(1)} %get-tuple-element.41), channel_id=1, source_target_pairs={{0,3},{1,2},{2,1},{3,0},{4,7},{5,6},{6,5},{7,4},{8,11},{9,10},{10,... | collective-permute-start | bytes 442376 | tf_op jit(solution)/shard_map/ppermute | solution.py:44
  92.6 9.1 %collective-permute-start.23 = (bf16[192,384]{1,0:T(8,128)(2,1)S(1)}, bf16[192,384]{1,0:T(8,128)(2,1)S(1)}, u32[]{:S(2)}, u32[]{:S(2)}) collective-permute-start(bf16[192,384]{1,0:T(8,128)(2,1)S(1)} %get-tuple-element.42), channel_id=1, source_target_pairs={{0,2},{1,3},{2,0},{3,1},{4,6},{5,7},{6,4},{7,5},{8,10},{9,11},{10,... | collective-permute-start | bytes 442376 | tf_op jit(solution)/shard_map/ppermute | solution.py:44
  93.0 8.7 %collective-permute-start.24 = (bf16[192,384]{1,0:T(8,128)(2,1)S(1)}, bf16[192,384]{1,0:T(8,128)(2,1)S(1)}, u32[]{:S(2)}, u32[]{:S(2)}) collective-permute-start(bf16[192,384]{1,0:T(8,128)(2,1)S(1)} %get-tuple-element.43), channel_id=1, source_target_pairs={{0,1},{1,0},{2,3},{3,2},{4,5},{5,4},{6,7},{7,6},{8,9},{9,8},{10,11... | collective-permute-start | bytes 442376 | tf_op jit(solution)/shard_map/ppermute | solution.py:44
  (4 other events, 57.7 us)

commit v3 on v2

--- a/solution.py
+++ b/solution.py
@@ -286,10 +286,9 @@
 
     for at in range(6):
         fetch(at)
-    ready = []
     for at in range(3):
         wait(at)
-        ready.append(project(at, rows if at == 0 else 0))
+    ready = [project(at, rows if at == 0 else 0) for at in range(3)]
     for at in range(3, 6):
         wait(at)
     attend_group(0, *ready)

time: 103 us -> 102 us (level)
  transfers between devices with their start and end apart: 32 -> 32, of which waited for: 16 -> 17; matrix products, arithmetic and copies ran while one was open for 0% -> 0% of each run, Pallas kernels for 30% -> 30%
where the time goes in v3:
time: 102 us
  waiting for transfers between devices  35.5 us (35%)
  starting transfers between devices  34.5 us (34%)
  Pallas kernels  30.2 us (30%)
    ppermute x29, waiting for transfers between devices, crossed(): return lax.ppermute(block, axis, [(i, i ^ bits) for i in range(count)])  26.8 us
    ppermute x29, starting transfers between devices, crossed(): return lax.ppermute(block, axis, [(i, i ^ bits) for i in range(count)])  24.4 us
    pallas_call x2, Pallas kernels, attend(): pl.pallas_call(kernel, out_shape=jax.ShapeDtypeStruct((rows, 2 * COLS), j...  15.5 us
    ppermute x3, starting transfers between devices, shifted(): return lax.ppermute(block, axis, route)  10.1 us
    ppermute x3, waiting for transfers between devices, shifted(): return lax.ppermute(block, axis, route)  8.73 us
    pallas_call x1, Pallas kernels, project_out(): pl.pallas_call(mixed_kernel, grid=(width // cols,), out_shape=jax.ShapeDt...  4.76 us
    pallas_call x1, Pallas kernels, conv_silu(): pl.pallas_call(conv_kernel, out_shape=jax.ShapeDtypeStruct((2 * rows, wid...  4.07 us
    pallas_call x2, Pallas kernels, sliced(): pl.pallas_call(kernel, out_shape=out_shape, in_specs=[anywhere] * len(blo...  2.71 us
  transfers between devices with their start and end apart: 32, of which 17 were waited for; matrix products, arithmetic and copies ran while one was open for 0% of the time, Pallas kernels for 30%

profile of v3, /device:TPU:0, one launch (start us, length us, event | category | flops | bytes accessed | tf_op | source)
XLA Modules:
  0.0 102.1 jit_solution(5909704637288430047)
XLA Ops:
  1.2 1.3 %first_slice.1._ = bf16[2,768,384]{2,1,0:T(8,128)(2,1)S(1)} custom-call(bf16[1536,1152]{1,0:T(8,128)(2,1)} %refs_2_.3), custom_call_target="tpu_custom_call" | custom-call | flops 1000000 | bytes 10000 | tf_op jit(solution)/shard_map/first_slice/pallas_call | solution.py:178
  2.5 2.7 %collective-permute-start.5 = (bf16[2,768,384]{2,1,0:T(8,128)(2,1)S(1)}, bf16[2,768,384]{2,1,0:T(8,128)(2,1)S(1)}, u32[]{:S(2)}, u32[]{:S(2)}) collective-permute-start(bf16[2,768,384]{2,1,0:T(8,128)(2,1)S(1)} %first_slice.1._), channel_id=1, source_target_pairs={{0,16},{8,24},{16,0},{24,8},{1,17},{9,25},{17,1},{25,9},{2,18},{10... | collective-permute-start | bytes 3538952 | tf_op jit(solution)/shard_map/ppermute | solution.py:44
  5.2 3.4 %collective-permute-start.1 = (bf16[256,1536]{1,0:T(8,128)(2,1)S(1)}, bf16[256,1536]{1,0:T(8,128)(2,1)S(1)}, u32[]{:S(2)}, u32[]{:S(2)}) collective-permute-start(bf16[256,1536]{1,0:T(8,128)(2,1)S(1)} %copy-done), channel_id=1, source_target_pairs={{0,1},{1,2},{2,3},{3,4},{4,5},{5,6},{6,7},{8,9},{9,10},{10,11},{11... | collective-permute-start | bytes 2359304 | tf_op jit(solution)/shard_map/ppermute | solution.py:39
  8.6 1.4 %later_slices.1 = (bf16[768,384]{1,0:T(8,128)(2,1)S(1)}, bf16[256,384]{1,0:T(8,128)(2,1)S(1)}, bf16[256,384]{1,0:T(8,128)(2,1)S(1)}, bf16[2,256,384]{2,1,0:T(8,128)(2,1)S(1)}) custom-call(bf16[1536,1152]{1,0:T(8,128)(2,1)} %refs_2_.3, bf16[256,1536]{1,0:T(8,128)(2,1)} %cot_ref.1, bf16[2,768,384]{2,1,0:T(8,128)(2,1)S(1)} %first_slice.1._), custom_call_target="tpu_custom_call" | custom-call | flops 1000000 | bytes 10000 | tf_op jit(solution)/shard_map/later_slices/pallas_call | solution.py:178
  10.1 1.3 %collective-permute-start.3 = (bf16[16,1536]{1,0:T(8,128)(2,1)S(1)}, bf16[16,1536]{1,0:T(8,128)(2,1)S(1)}, u32[]{:S(2)}, u32[]{:S(2)}) collective-permute-start(bf16[16,1536]{1,0:T(8,128)(2,1)S(1)} %get-tuple-element.52), channel_id=1, source_target_pairs={{1,0},{2,1},{3,2},{4,3},{5,4},{6,5},{7,6},{9,8},{10,9},{11,10},{12... | collective-permute-start | bytes 147464 | tf_op jit(solution)/shard_map/ppermute | solution.py:39
  11.5 5.4 %collective-permute-start = (bf16[16,1536]{1,0:T(8,128)(2,1)S(1)}, bf16[16,1536]{1,0:T(8,128)(2,1)S(1)}, u32[]{:S(2)}, u32[]{:S(2)}) collective-permute-start(bf16[16,1536]{1,0:T(8,128)(2,1)S(1)} %get-tuple-element.53), channel_id=1, source_target_pairs={{0,2},{1,3},{2,4},{3,5},{4,6},{5,7},{8,10},{9,11},{10,12},{11,13},... | collective-permute-start | bytes 147464 | tf_op jit(solution)/shard_map/ppermute | solution.py:39
  17.0 1.0 %masks.1 = (f32[512,128]{1,0:T(8,128)S(1)}, f32[256,512]{1,0:T(8,128)S(1)}) custom-call(s32[1,8]{1,0:T(1,128)S(1)} %copy-done.3, s32[1,2048]{1,0:T(1,128)S(1)} %copy-done.2), custom_call_target="tpu_custom_call" | custom-call | flops 1000000 | bytes 10000 | tf_op jit(solution)/shard_map/masks/pallas_call | solution.py:83
  18.7 8.1 %collective-permute-done.1.prev_ref = bf16[256,1536]{1,0:T(8,128)(2,1)S(1)} collective-permute-done((bf16[256,1536]{1,0:T(8,128)(2,1)S(1)}, bf16[256,1536]{1,0:T(8,128)(2,1)S(1)}, u32[]{:S(2)}, u32[]{:S(2)}) %collective-permute-start.1) | collective-permute-done | bytes 786464 | tf_op jit(solution)/shard_map/ppermute | solution.py:39
  26.7 4.1 %conv_silu.1.refs_0_ = bf16[512,1536]{1,0:T(8,128)(2,1)S(1)} custom-call(bf16[16,1536]{1,0:T(8,128)(2,1)S(1)} %collective-permute-done.far_ref, bf16[256,1536]{1,0:T(8,128)(2,1)S(1)} %collective-permute-done.1.prev_ref, bf16[256,1536]{1,0:T(8,128)(2,1)S(1)} %copy-done, bf16[16,1536]{1,0:T(8,128)(2,1)S(1)} %collective-permute-done.3.next_ref, ...), custom_call_target="tpu_custom_call" | custom-call | flops 1000000 | bytes 10000 | tf_op jit(solution)/shard_map/conv_silu/pallas_call | solution.py:132
  30.8 0.9 collective-permute-done.5.refs_4_
  31.9 2.6 %collective-permute-start.7 = (bf16[2,384,384]{2,1,0:T(8,128)(2,1)S(1)}, bf16[2,384,384]{2,1,0:T(8,128)(2,1)S(1)}, u32[]{:S(2)}, u32[]{:S(2)}) collective-permute-start(bf16[2,384,384]{2,1,0:T(8,128)(2,1)S(1)} %get-tuple-element.50), channel_id=1, source_target_pairs={{0,2},{1,3},{2,0},{3,1},{4,6},{5,7},{6,4},{7,5},{8,10},{9,11},{10,... | collective-permute-start | bytes 1769480 | tf_op jit(solution)/shard_map/ppermute | solution.py:44
  35.2 1.5 %collective-permute-start.11 = (bf16[768,384]{1,0:T(8,128)(2,1)S(1)}, bf16[768,384]{1,0:T(8,128)(2,1)S(1)}, u32[]{:S(2)}, u32[]{:S(2)}) collective-permute-start(bf16[768,384]{1,0:T(8,128)(2,1)S(1)} %get-tuple-element.33), channel_id=1, source_target_pairs={{0,16},{8,24},{16,0},{24,8},{1,17},{9,25},{17,1},{25,9},{2,18},{10... | collective-permute-start | bytes 1769480 | tf_op jit(solution)/shard_map/ppermute | solution.py:44
  36.8 11.3 %collective-permute-done.7.refs_6_ = bf16[2,384,384]{2,1,0:T(8,128)(2,1)S(1)} collective-permute-done((bf16[2,384,384]{2,1,0:T(8,128)(2,1)S(1)}, bf16[2,384,384]{2,1,0:T(8,128)(2,1)S(1)}, u32[]{:S(2)}, u32[]{:S(2)}) %collective-permute-start.7) | collective-permute-done | bytes 589856 | tf_op jit(solution)/shard_map/ppermute | solution.py:44
  48.1 1.5 %collective-permute-done.6.refs_5_ = bf16[2,384,384]{2,1,0:T(8,128)(2,1)S(1)} collective-permute-done((bf16[2,384,384]{2,1,0:T(8,128)(2,1)S(1)}, bf16[2,384,384]{2,1,0:T(8,128)(2,1)S(1)}, u32[]{:S(2)}, u32[]{:S(2)}) %collective-permute-start.6) | collective-permute-done | bytes 589856 | tf_op jit(solution)/shard_map/ppermute | solution.py:44
  49.5 1.4 %collective-permute-done.11.refs_10_ = bf16[768,384]{1,0:T(8,128)(2,1)S(1)} collective-permute-done((bf16[768,384]{1,0:T(8,128)(2,1)S(1)}, bf16[768,384]{1,0:T(8,128)(2,1)S(1)}, u32[]{:S(2)}, u32[]{:S(2)}) %collective-permute-start.11) | collective-permute-done | bytes 589856 | tf_op jit(solution)/shard_map/ppermute | solution.py:44
  51.0 1.5 %collective-permute-start.20 = (bf16[2,256,384]{2,1,0:T(8,128)(2,1)S(1)}, bf16[2,256,384]{2,1,0:T(8,128)(2,1)S(1)}, u32[]{:S(2)}, u32[]{:S(2)}) collective-permute-start(bf16[2,256,384]{2,1,0:T(8,128)(2,1)S(1)} %get-tuple-element.38), channel_id=1, source_target_pairs={{0,16},{8,24},{16,0},{24,8},{1,17},{9,25},{17,1},{25,9},{2,18},{10... | collective-permute-start | bytes 1179656 | tf_op jit(solution)/shard_map/ppermute | solution.py:44
  53.6 7.8 %attention_0.1.far_ref.refs_0_ = bf16[256,768]{1,0:T(8,128)(2,1)S(1)} custom-call(bf16[512,1536]{1,0:T(8,128)(2,1)S(1)} %conv_silu.1.refs_0_, f32[256,512]{1,0:T(8,128)S(1)} %get-tuple-element.30.refs_1_, bf16[1536,1152]{1,0:T(8,128)(2,1)} %refs_2_.3, bf16[1536,1152]{1,0:T(8,128)(2,1)S(1)} %collective-permute-done.4.refs_3_, ...), custom_call_target="tpu_custom_call" | custom-call | flops 1000000 | bytes 10000 | tf_op jit(solution)/shard_map/attention_0/pallas_call | solution.py:306
  61.7 1.5 %collective-permute-start.26 = (bf16[256,768]{1,0:T(8,128)(2,1)S(1)}, bf16[256,768]{1,0:T(8,128)(2,1)S(1)}, u32[]{:S(2)}, u32[]{:S(2)}) collective-permute-start(bf16[256,768]{1,0:T(8,128)(2,1)S(1)} %attention_0.1.far_ref.refs_0_), channel_id=1, source_target_pairs={{0,16},{8,24},{16,0},{24,8},{1,17},{9,25},{17,1},{25,9},{2,18},{10... | collective-permute-start | bytes 1179656 | tf_op jit(solution)/shard_map/ppermute | solution.py:44
  63.8 1.0 collective-permute-done.15.refs_14_
  65.3 7.6 %attention_1.1.near_ref.refs_0_ = bf16[256,768]{1,0:T(8,128)(2,1)S(1)} custom-call(bf16[512,1536]{1,0:T(8,128)(2,1)S(1)} %conv_silu.1.refs_0_, f32[256,512]{1,0:T(8,128)S(1)} %get-tuple-element.30.refs_1_, bf16[1536,1152]{1,0:T(8,128)(2,1)} %refs_2_.3, bf16[1536,1152]{1,0:T(8,128)(2,1)S(1)} %collective-permute-done.4.refs_3_, ...), custom_call_target="tpu_custom_call" | custom-call | flops 1000000 | bytes 10000 | tf_op jit(solution)/shard_map/attention_1/pallas_call | solution.py:306
  73.5 1.0 %collective-permute-start.18 = (bf16[256,768]{1,0:T(8,128)(2,1)S(1)}, bf16[256,768]{1,0:T(8,128)(2,1)S(1)}, u32[]{:S(2)}, u32[]{:S(2)}) collective-permute-start(bf16[256,768]{1,0:T(8,128)(2,1)S(1)} %attention_1.1.near_ref.refs_0_), channel_id=1, source_target_pairs={{0,16},{8,24},{16,0},{24,8},{1,17},{9,25},{17,1},{25,9},{2,18},{10... | collective-permute-start | bytes 1179656 | tf_op jit(solution)/shard_map/ppermute | solution.py:44
  75.3 1.1 %far.1 = (f32[192,384]{1,0:T(8,128)S(1)}, bf16[192,384]{1,0:T(8,128)(2,1)S(1)}, bf16[192,384]{1,0:T(8,128)(2,1)S(1)}, bf16[192,384]{1,0:T(8,128)(2,1)S(1)}) custom-call(bf16[256,768]{1,0:T(8,128)(2,1)S(1)} %attention_0.1.far_ref.refs_0_, bf16[256,768]{1,0:T(8,128)(2,1)S(1)} %collective-permute-done.25.refs_1_, ...), custom_call_target="tpu_custom_call" | custom-call | flops 1000000 | bytes 10000 | tf_op jit(solution)/shard_map/far/pallas_call | solution.py:371
  76.3 2.1 %collective-permute-start.28 = (bf16[192,384]{1,0:T(8,128)(2,1)S(1)}, bf16[192,384]{1,0:T(8,128)(2,1)S(1)}, u32[]{:S(2)}, u32[]{:S(2)}) collective-permute-start(bf16[192,384]{1,0:T(8,128)(2,1)S(1)} %get-tuple-element.47), channel_id=1, source_target_pairs={{0,3},{1,2},{2,1},{3,0},{4,7},{5,6},{6,5},{7,4},{8,11},{9,10},{10,... | collective-permute-start | bytes 442376 | tf_op jit(solution)/shard_map/ppermute | solution.py:44
  78.9 1.0 %collective-permute-start.30 = (bf16[192,384]{1,0:T(8,128)(2,1)S(1)}, bf16[192,384]{1,0:T(8,128)(2,1)S(1)}, u32[]{:S(2)}, u32[]{:S(2)}) collective-permute-start(bf16[192,384]{1,0:T(8,128)(2,1)S(1)} %get-tuple-element.49), channel_id=1, source_target_pairs={{0,1},{1,0},{2,3},{3,2},{4,5},{5,4},{6,7},{7,6},{8,9},{9,8},{10,11... | collective-permute-start | bytes 442376 | tf_op jit(solution)/shard_map/ppermute | solution.py:44
  79.9 4.9 %collective-permute-done.18.refs_2_ = bf16[256,768]{1,0:T(8,128)(2,1)S(1)} collective-permute-done((bf16[256,768]{1,0:T(8,128)(2,1)S(1)}, bf16[256,768]{1,0:T(8,128)(2,1)S(1)}, u32[]{:S(2)}, u32[]{:S(2)}) %collective-permute-start.18) | collective-permute-done | bytes 393248 | tf_op jit(solution)/shard_map/ppermute | solution.py:44
  84.8 1.1 %collective-permute-done.29 = bf16[192,384]{1,0:T(8,128)(2,1)S(1)} collective-permute-done((bf16[192,384]{1,0:T(8,128)(2,1)S(1)}, bf16[192,384]{1,0:T(8,128)(2,1)S(1)}, u32[]{:S(2)}, u32[]{:S(2)}) %collective-permute-start.29) | collective-permute-done | bytes 147488 | tf_op jit(solution)/shard_map/ppermute | solution.py:44
  86.6 2.8 %collective-permute-start.31 = (bf16[192,384]{1,0:T(8,128)(2,1)S(1)}, bf16[192,384]{1,0:T(8,128)(2,1)S(1)}, u32[]{:S(2)}, u32[]{:S(2)}) collective-permute-start(bf16[192,384]{1,0:T(8,128)(2,1)S(1)} %add_convert_fusion), channel_id=1, source_target_pairs={{0,4},{1,5},{2,6},{3,7},{4,0},{5,1},{6,2},{7,3},{8,12},{9,13},{10,... | collective-permute-start | bytes 442376 | tf_op jit(solution)/shard_map/ppermute | solution.py:44
  89.4 1.1 %near.1 = (f32[192,384]{1,0:T(8,128)S(1)}, bf16[192,384]{1,0:T(8,128)(2,1)S(1)}, bf16[192,384]{1,0:T(8,128)(2,1)S(1)}, bf16[192,384]{1,0:T(8,128)(2,1)S(1)}) custom-call(bf16[256,768]{1,0:T(8,128)(2,1)S(1)} %attention_1.1.near_ref.refs_0_, bf16[256,768]{1,0:T(8,128)(2,1)S(1)} %collective-permute-done.17.refs_1_, ...), custom_call_target="tpu_custom_call" | custom-call | flops 1000000 | bytes 10000 | tf_op jit(solution)/shard_map/near/pallas_call | solution.py:371
  90.5 1.8 %collective-permute-start.22 = (bf16[192,384]{1,0:T(8,128)(2,1)S(1)}, bf16[192,384]{1,0:T(8,128)(2,1)S(1)}, u32[]{:S(2)}, u32[]{:S(2)}) collective-permute-start(bf16[192,384]{1,0:T(8,128)(2,1)S(1)} %get-tuple-element.41), channel_id=1, source_target_pairs={{0,3},{1,2},{2,1},{3,0},{4,7},{5,6},{6,5},{7,4},{8,11},{9,10},{10,... | collective-permute-start | bytes 442376 | tf_op jit(solution)/shard_map/ppermute | solution.py:44
  92.7 1.4 %collective-permute-start.24 = (bf16[192,384]{1,0:T(8,128)(2,1)S(1)}, bf16[192,384]{1,0:T(8,128)(2,1)S(1)}, u32[]{:S(2)}, u32[]{:S(2)}) collective-permute-start(bf16[192,384]{1,0:T(8,128)(2,1)S(1)} %get-tuple-element.43), channel_id=1, source_target_pairs={{0,1},{1,0},{2,3},{3,2},{4,5},{5,4},{6,7},{7,6},{8,9},{9,8},{10,11... | collective-permute-start | bytes 442376 | tf_op jit(solution)/shard_map/ppermute | solution.py:44
  94.0 4.8 %mixed.1 = bf16[256,1536]{1,0:T(8,128)(2,1)} custom-call(bf16[256,768]{1,0:T(8,128)(2,1)S(1)} %attention_0.1.far_ref.refs_0_, bf16[256,768]{1,0:T(8,128)(2,1)S(1)} %attention_1.1.near_ref.refs_0_, bf16[1536,1536]{1,0:T(8,128)(2,1)} %w_ref.5), custom_call_target="tpu_custom_call" | custom-call | flops 1000000 | bytes 10000 | tf_op jit(solution)/shard_map/mixed/pallas_call | solution.py:336
  99.7 1.7 %collective-permute-done.23 = bf16[192,384]{1,0:T(8,128)(2,1)S(1)} collective-permute-done((bf16[192,384]{1,0:T(8,128)(2,1)S(1)}, bf16[192,384]{1,0:T(8,128)(2,1)S(1)}, u32[]{:S(2)}, u32[]{:S(2)}) %collective-permute-start.23) | collective-permute-done | bytes 147488 | tf_op jit(solution)/shard_map/ppermute | solution.py:44
  (54 shorter events, 9.1 us)
Async XLA Ops:
  0.6 53.0 %collective-permute-start.4 = (bf16[1536,1152]{1,0:T(8,128)(2,1)}, bf16[1536,1152]{1,0:T(8,128)(2,1)S(1)}, u32[]{:S(2)}, u32[]{:S(2)}) collective-permute-start(bf16[1536,1152]{1,0:T(8,128)(2,1)} %refs_2_.3), channel_id=1, source_target_pairs={{0,8},{8,0},{16,24},{24,16},{1,9},{9,1},{17,25},{25,17},{2,10},{10... | collective-permute-start | bytes 10616840 | tf_op jit(solution)/shard_map/ppermute | solution.py:44
  2.5 29.2 %collective-permute-start.5 = (bf16[2,768,384]{2,1,0:T(8,128)(2,1)S(1)}, bf16[2,768,384]{2,1,0:T(8,128)(2,1)S(1)}, u32[]{:S(2)}, u32[]{:S(2)}) collective-permute-start(bf16[2,768,384]{2,1,0:T(8,128)(2,1)S(1)} %first_slice.1._), channel_id=1, source_target_pairs={{0,16},{8,24},{16,0},{24,8},{1,17},{9,25},{17,1},{25,9},{2,18},{10... | collective-permute-start | bytes 3538952 | tf_op jit(solution)/shard_map/ppermute | solution.py:44
  5.2 21.5 %collective-permute-start.1 = (bf16[256,1536]{1,0:T(8,128)(2,1)S(1)}, bf16[256,1536]{1,0:T(8,128)(2,1)S(1)}, u32[]{:S(2)}, u32[]{:S(2)}) collective-permute-start(bf16[256,1536]{1,0:T(8,128)(2,1)S(1)} %copy-done), channel_id=1, source_target_pairs={{0,1},{1,2},{2,3},{3,4},{4,5},{5,6},{6,7},{8,9},{9,10},{10,11},{11... | collective-permute-start | bytes 2359304 | tf_op jit(solution)/shard_map/ppermute | solution.py:39
  10.0 1.5 %collective-permute-start.2 = (bf16[256,384]{1,0:T(8,128)(2,1)S(1)}, bf16[256,384]{1,0:T(8,128)(2,1)S(1)}, u32[]{:S(2)}, u32[]{:S(2)}) collective-permute-start(bf16[256,384]{1,0:T(8,128)(2,1)S(1)} %get-tuple-element.26), channel_id=1, source_target_pairs={{0,8},{8,0},{16,24},{24,16},{1,9},{9,1},{17,25},{25,17},{2,10},{10... | collective-permute-start | bytes 589832 | tf_op jit(solution)/shard_map/ppermute | solution.py:44
  10.1 7.9 %collective-permute-start.3 = (bf16[16,1536]{1,0:T(8,128)(2,1)S(1)}, bf16[16,1536]{1,0:T(8,128)(2,1)S(1)}, u32[]{:S(2)}, u32[]{:S(2)}) collective-permute-start(bf16[16,1536]{1,0:T(8,128)(2,1)S(1)} %get-tuple-element.52), channel_id=1, source_target_pairs={{1,0},{2,1},{3,2},{4,3},{5,4},{6,5},{7,6},{9,8},{10,9},{11,10},{12... | collective-permute-start | bytes 147464 | tf_op jit(solution)/shard_map/ppermute | solution.py:39
  11.5 7.1 %collective-permute-start = (bf16[16,1536]{1,0:T(8,128)(2,1)S(1)}, bf16[16,1536]{1,0:T(8,128)(2,1)S(1)}, u32[]{:S(2)}, u32[]{:S(2)}) collective-permute-start(bf16[16,1536]{1,0:T(8,128)(2,1)S(1)} %get-tuple-element.53), channel_id=1, source_target_pairs={{0,2},{1,3},{2,4},{3,5},{4,6},{5,7},{8,10},{9,11},{10,12},{11,13},... | collective-permute-start | bytes 147464 | tf_op jit(solution)/shard_map/ppermute | solution.py:39
  31.9 16.2 %collective-permute-start.7 = (bf16[2,384,384]{2,1,0:T(8,128)(2,1)S(1)}, bf16[2,384,384]{2,1,0:T(8,128)(2,1)S(1)}, u32[]{:S(2)}, u32[]{:S(2)}) collective-permute-start(bf16[2,384,384]{2,1,0:T(8,128)(2,1)S(1)} %get-tuple-element.50), channel_id=1, source_target_pairs={{0,2},{1,3},{2,0},{3,1},{4,6},{5,7},{6,4},{7,5},{8,10},{9,11},{10,... | collective-permute-start | bytes 1769480 | tf_op jit(solution)/shard_map/ppermute | solution.py:44
  34.5 15.0 %collective-permute-start.6 = (bf16[2,384,384]{2,1,0:T(8,128)(2,1)S(1)}, bf16[2,384,384]{2,1,0:T(8,128)(2,1)S(1)}, u32[]{:S(2)}, u32[]{:S(2)}) collective-permute-start(bf16[2,384,384]{2,1,0:T(8,128)(2,1)S(1)} %get-tuple-element.51), channel_id=1, source_target_pairs={{0,1},{1,0},{2,3},{3,2},{4,5},{5,4},{6,7},{7,6},{8,9},{9,8},{10,11... | collective-permute-start | bytes 1769480 | tf_op jit(solution)/shard_map/ppermute | solution.py:44
  35.2 18.4 %collective-permute-start.8 = (bf16[2,768,384]{2,1,0:T(8,128)(2,1)S(1)}, bf16[2,768,384]{2,1,0:T(8,128)(2,1)S(1)}, u32[]{:S(2)}, u32[]{:S(2)}) collective-permute-start(bf16[2,768,384]{2,1,0:T(8,128)(2,1)S(1)} %collective-permute-done.5.refs_4_), channel_id=1, source_target_pairs={{0,8},{8,0},{16,24},{24,16},{1,9},{9,1},{17,25},{25,17},{2,10},{10... | collective-permute-start | bytes 3538952 | tf_op jit(solution)/shard_map/ppermute | solution.py:44
  35.2 15.7 %collective-permute-start.11 = (bf16[768,384]{1,0:T(8,128)(2,1)S(1)}, bf16[768,384]{1,0:T(8,128)(2,1)S(1)}, u32[]{:S(2)}, u32[]{:S(2)}) collective-permute-start(bf16[768,384]{1,0:T(8,128)(2,1)S(1)} %get-tuple-element.33), channel_id=1, source_target_pairs={{0,16},{8,24},{16,0},{24,8},{1,17},{9,25},{17,1},{25,9},{2,18},{10... | collective-permute-start | bytes 1769480 | tf_op jit(solution)/shard_map/ppermute | solution.py:44
  48.1 4.5 %collective-permute-start.10 = (bf16[2,384,384]{2,1,0:T(8,128)(2,1)S(1)}, bf16[2,384,384]{2,1,0:T(8,128)(2,1)S(1)}, u32[]{:S(2)}, u32[]{:S(2)}) collective-permute-start(bf16[2,384,384]{2,1,0:T(8,128)(2,1)S(1)} %collective-permute-done.7.refs_6_), channel_id=1, source_target_pairs={{0,8},{8,0},{16,24},{24,16},{1,9},{9,1},{17,25},{25,17},{2,10},{10... | collective-permute-start | bytes 1769480 | tf_op jit(solution)/shard_map/ppermute | solution.py:44
  49.5 3.6 %collective-permute-start.9 = (bf16[2,384,384]{2,1,0:T(8,128)(2,1)S(1)}, bf16[2,384,384]{2,1,0:T(8,128)(2,1)S(1)}, u32[]{:S(2)}, u32[]{:S(2)}) collective-permute-start(bf16[2,384,384]{2,1,0:T(8,128)(2,1)S(1)} %collective-permute-done.6.refs_5_), channel_id=1, source_target_pairs={{0,8},{8,0},{16,24},{24,16},{1,9},{9,1},{17,25},{25,17},{2,10},{10... | collective-permute-start | bytes 1769480 | tf_op jit(solution)/shard_map/ppermute | solution.py:44
  51.0 10.7 %collective-permute-start.20 = (bf16[2,256,384]{2,1,0:T(8,128)(2,1)S(1)}, bf16[2,256,384]{2,1,0:T(8,128)(2,1)S(1)}, u32[]{:S(2)}, u32[]{:S(2)}) collective-permute-start(bf16[2,256,384]{2,1,0:T(8,128)(2,1)S(1)} %get-tuple-element.38), channel_id=1, source_target_pairs={{0,16},{8,24},{16,0},{24,8},{1,17},{9,25},{17,1},{25,9},{2,18},{10... | collective-permute-start | bytes 1179656 | tf_op jit(solution)/shard_map/ppermute | solution.py:44
  52.6 10.7 %collective-permute-start.13 = (bf16[384,384]{1,0:T(8,128)(2,1)S(1)}, bf16[384,384]{1,0:T(8,128)(2,1)S(1)}, u32[]{:S(2)}, u32[]{:S(2)}) collective-permute-start(bf16[384,384]{1,0:T(8,128)(2,1)S(1)} %get-tuple-element.54), channel_id=1, source_target_pairs={{0,2},{1,3},{2,0},{3,1},{4,6},{5,7},{6,4},{7,5},{8,10},{9,11},{10,... | collective-permute-start | bytes 884744 | tf_op jit(solution)/shard_map/ppermute | solution.py:44
  53.1 10.2 %collective-permute-start.12 = (bf16[384,384]{1,0:T(8,128)(2,1)S(1)}, bf16[384,384]{1,0:T(8,128)(2,1)S(1)}, u32[]{:S(2)}, u32[]{:S(2)}) collective-permute-start(bf16[384,384]{1,0:T(8,128)(2,1)S(1)} %get-tuple-element.55), channel_id=1, source_target_pairs={{0,1},{1,0},{2,3},{3,2},{4,5},{5,4},{6,7},{7,6},{8,9},{9,8},{10,11... | collective-permute-start | bytes 884744 | tf_op jit(solution)/shard_map/ppermute | solution.py:44
  53.6 10.2 %collective-permute-start.14 = (bf16[768,384]{1,0:T(8,128)(2,1)S(1)}, bf16[768,384]{1,0:T(8,128)(2,1)S(1)}, u32[]{:S(2)}, u32[]{:S(2)}) collective-permute-start(bf16[768,384]{1,0:T(8,128)(2,1)S(1)} %collective-permute-done.11.refs_10_), channel_id=1, source_target_pairs={{0,8},{8,0},{16,24},{24,16},{1,9},{9,1},{17,25},{25,17},{2,10},{10... | collective-permute-start | bytes 1769480 | tf_op jit(solution)/shard_map/ppermute | solution.py:44
  61.7 11.5 %collective-permute-start.26 = (bf16[256,768]{1,0:T(8,128)(2,1)S(1)}, bf16[256,768]{1,0:T(8,128)(2,1)S(1)}, u32[]{:S(2)}, u32[]{:S(2)}) collective-permute-start(bf16[256,768]{1,0:T(8,128)(2,1)S(1)} %attention_0.1.far_ref.refs_0_), channel_id=1, source_target_pairs={{0,16},{8,24},{16,0},{24,8},{1,17},{9,25},{17,1},{25,9},{2,18},{10... | collective-permute-start | bytes 1179656 | tf_op jit(solution)/shard_map/ppermute | solution.py:44
  63.3 1.6 %collective-permute-start.15 = (bf16[384,384]{1,0:T(8,128)(2,1)S(1)}, bf16[384,384]{1,0:T(8,128)(2,1)S(1)}, u32[]{:S(2)}, u32[]{:S(2)}) collective-permute-start(bf16[384,384]{1,0:T(8,128)(2,1)S(1)} %collective-permute-done.12.refs_11_), channel_id=1, source_target_pairs={{0,8},{8,0},{16,24},{24,16},{1,9},{9,1},{17,25},{25,17},{2,10},{10... | collective-permute-start | bytes 884744 | tf_op jit(solution)/shard_map/ppermute | solution.py:44
  63.3 2.0 %collective-permute-start.16 = (bf16[384,384]{1,0:T(8,128)(2,1)S(1)}, bf16[384,384]{1,0:T(8,128)(2,1)S(1)}, u32[]{:S(2)}, u32[]{:S(2)}) collective-permute-start(bf16[384,384]{1,0:T(8,128)(2,1)S(1)} %collective-permute-done.13.refs_12_), channel_id=1, source_target_pairs={{0,8},{8,0},{16,24},{24,16},{1,9},{9,1},{17,25},{25,17},{2,10},{10... | collective-permute-start | bytes 884744 | tf_op jit(solution)/shard_map/ppermute | solution.py:44
  63.8 10.8 %collective-permute-start.25 = (bf16[256,768]{1,0:T(8,128)(2,1)S(1)}, bf16[256,768]{1,0:T(8,128)(2,1)S(1)}, u32[]{:S(2)}, u32[]{:S(2)}) collective-permute-start(bf16[256,768]{1,0:T(8,128)(2,1)S(1)} %attention_0.1.far_ref.refs_0_), channel_id=1, source_target_pairs={{0,8},{8,0},{16,24},{24,16},{1,9},{9,1},{17,25},{25,17},{2,10},{10... | collective-permute-start | bytes 1179656 | tf_op jit(solution)/shard_map/ppermute | solution.py:44
  72.9 1.8 %collective-permute-start.21 = (bf16[2,256,384]{2,1,0:T(8,128)(2,1)S(1)}, bf16[2,256,384]{2,1,0:T(8,128)(2,1)S(1)}, u32[]{:S(2)}, u32[]{:S(2)}) collective-permute-start(bf16[2,256,384]{2,1,0:T(8,128)(2,1)S(1)} %collective-permute-done.20.refs_6_), channel_id=1, source_target_pairs={{0,8},{8,0},{16,24},{24,16},{1,9},{9,1},{17,25},{25,17},{2,10},{10... | collective-permute-start | bytes 1179656 | tf_op jit(solution)/shard_map/ppermute | solution.py:44
  73.3 2.0 %collective-permute-start.27 = (bf16[256,768]{1,0:T(8,128)(2,1)S(1)}, bf16[256,768]{1,0:T(8,128)(2,1)S(1)}, u32[]{:S(2)}, u32[]{:S(2)}) collective-permute-start(bf16[256,768]{1,0:T(8,128)(2,1)S(1)} %collective-permute-done.26.refs_2_), channel_id=1, source_target_pairs={{0,8},{8,0},{16,24},{24,16},{1,9},{9,1},{17,25},{25,17},{2,10},{10... | collective-permute-start | bytes 1179656 | tf_op jit(solution)/shard_map/ppermute | solution.py:44
  73.5 11.3 %collective-permute-start.18 = (bf16[256,768]{1,0:T(8,128)(2,1)S(1)}, bf16[256,768]{1,0:T(8,128)(2,1)S(1)}, u32[]{:S(2)}, u32[]{:S(2)}) collective-permute-start(bf16[256,768]{1,0:T(8,128)(2,1)S(1)} %attention_1.1.near_ref.refs_0_), channel_id=1, source_target_pairs={{0,16},{8,24},{16,0},{24,8},{1,17},{9,25},{17,1},{25,9},{2,18},{10... | collective-permute-start | bytes 1179656 | tf_op jit(solution)/shard_map/ppermute | solution.py:44
  76.3 8.4 %collective-permute-start.28 = (bf16[192,384]{1,0:T(8,128)(2,1)S(1)}, bf16[192,384]{1,0:T(8,128)(2,1)S(1)}, u32[]{:S(2)}, u32[]{:S(2)}) collective-permute-start(bf16[192,384]{1,0:T(8,128)(2,1)S(1)} %get-tuple-element.47), channel_id=1, source_target_pairs={{0,3},{1,2},{2,1},{3,0},{4,7},{5,6},{6,5},{7,4},{8,11},{9,10},{10,... | collective-permute-start | bytes 442376 | tf_op jit(solution)/shard_map/ppermute | solution.py:44
  78.5 7.4 %collective-permute-start.29 = (bf16[192,384]{1,0:T(8,128)(2,1)S(1)}, bf16[192,384]{1,0:T(8,128)(2,1)S(1)}, u32[]{:S(2)}, u32[]{:S(2)}) collective-permute-start(bf16[192,384]{1,0:T(8,128)(2,1)S(1)} %get-tuple-element.48), channel_id=1, source_target_pairs={{0,2},{1,3},{2,0},{3,1},{4,6},{5,7},{6,4},{7,5},{8,10},{9,11},{10,... | collective-permute-start | bytes 442376 | tf_op jit(solution)/shard_map/ppermute | solution.py:44
  78.9 7.6 %collective-permute-start.30 = (bf16[192,384]{1,0:T(8,128)(2,1)S(1)}, bf16[192,384]{1,0:T(8,128)(2,1)S(1)}, u32[]{:S(2)}, u32[]{:S(2)}) collective-permute-start(bf16[192,384]{1,0:T(8,128)(2,1)S(1)} %get-tuple-element.49), channel_id=1, source_target_pairs={{0,1},{1,0},{2,3},{3,2},{4,5},{5,4},{6,7},{7,6},{8,9},{9,8},{10,11... | collective-permute-start | bytes 442376 | tf_op jit(solution)/shard_map/ppermute | solution.py:44
  79.9 9.5 %collective-permute-start.17 = (bf16[256,768]{1,0:T(8,128)(2,1)S(1)}, bf16[256,768]{1,0:T(8,128)(2,1)S(1)}, u32[]{:S(2)}, u32[]{:S(2)}) collective-permute-start(bf16[256,768]{1,0:T(8,128)(2,1)S(1)} %attention_1.1.near_ref.refs_0_), channel_id=1, source_target_pairs={{0,8},{8,0},{16,24},{24,16},{1,9},{9,1},{17,25},{25,17},{2,10},{10... | collective-permute-start | bytes 1179656 | tf_op jit(solution)/shard_map/ppermute | solution.py:44
  84.8 4.6 %collective-permute-start.19 = (bf16[256,768]{1,0:T(8,128)(2,1)S(1)}, bf16[256,768]{1,0:T(8,128)(2,1)S(1)}, u32[]{:S(2)}, u32[]{:S(2)}) collective-permute-start(bf16[256,768]{1,0:T(8,128)(2,1)S(1)} %collective-permute-done.18.refs_2_), channel_id=1, source_target_pairs={{0,8},{8,0},{16,24},{24,16},{1,9},{9,1},{17,25},{25,17},{2,10},{10... | collective-permute-start | bytes 1179656 | tf_op jit(solution)/shard_map/ppermute | solution.py:44
  86.6 12.2 %collective-permute-start.31 = (bf16[192,384]{1,0:T(8,128)(2,1)S(1)}, bf16[192,384]{1,0:T(8,128)(2,1)S(1)}, u32[]{:S(2)}, u32[]{:S(2)}) collective-permute-start(bf16[192,384]{1,0:T(8,128)(2,1)S(1)} %add_convert_fusion), channel_id=1, source_target_pairs={{0,4},{1,5},{2,6},{3,7},{4,0},{5,1},{6,2},{7,3},{8,12},{9,13},{10,... | collective-permute-start | bytes 442376 | tf_op jit(solution)/shard_map/ppermute | solution.py:44
  90.5 9.2 %collective-permute-start.22 = (bf16[192,384]{1,0:T(8,128)(2,1)S(1)}, bf16[192,384]{1,0:T(8,128)(2,1)S(1)}, u32[]{:S(2)}, u32[]{:S(2)}) collective-permute-start(bf16[192,384]{1,0:T(8,128)(2,1)S(1)} %get-tuple-element.41), channel_id=1, source_target_pairs={{0,3},{1,2},{2,1},{3,0},{4,7},{5,6},{6,5},{7,4},{8,11},{9,10},{10,... | collective-permute-start | bytes 442376 | tf_op jit(solution)/shard_map/ppermute | solution.py:44
  92.3 9.0 %collective-permute-start.23 = (bf16[192,384]{1,0:T(8,128)(2,1)S(1)}, bf16[192,384]{1,0:T(8,128)(2,1)S(1)}, u32[]{:S(2)}, u32[]{:S(2)}) collective-permute-start(bf16[192,384]{1,0:T(8,128)(2,1)S(1)} %get-tuple-element.42), channel_id=1, source_target_pairs={{0,2},{1,3},{2,0},{3,1},{4,6},{5,7},{6,4},{7,5},{8,10},{9,11},{10,... | collective-permute-start | bytes 442376 | tf_op jit(solution)/shard_map/ppermute | solution.py:44
  92.7 8.7 %collective-permute-start.24 = (bf16[192,384]{1,0:T(8,128)(2,1)S(1)}, bf16[192,384]{1,0:T(8,128)(2,1)S(1)}, u32[]{:S(2)}, u32[]{:S(2)}) collective-permute-start(bf16[192,384]{1,0:T(8,128)(2,1)S(1)} %get-tuple-element.43), channel_id=1, source_target_pairs={{0,1},{1,0},{2,3},{3,2},{4,5},{5,4},{6,7},{7,6},{8,9},{9,8},{10,11... | collective-permute-start | bytes 442376 | tf_op jit(solution)/shard_map/ppermute | solution.py:44
  (4 other events, 57.7 us)

commit v4 on v3

--- a/solution.py
+++ b/solution.py
@@ -286,12 +286,9 @@
 
     for at in range(6):
         fetch(at)
-    for at in range(3):
+    for at in range(6):
         wait(at)
-    ready = [project(at, rows if at == 0 else 0) for at in range(3)]
-    for at in range(3, 6):
-        wait(at)
-    attend_group(0, *ready)
+    attend_group(0, *(project(at, rows if at == 0 else 0) for at in range(3)))
     attend_group(1, *(project(at, rows if at == 3 else 0) for at in range(3, 6)))
 
 

time: 102 us -> 103 us (level)
  transfers between devices with their start and end apart: 32 -> 32, of which waited for: 17 -> 16; matrix products, arithmetic and copies ran while one was open for 0% -> 0% of each run, Pallas kernels for 30% -> 30%
where the time goes in v4:
time: 103 us
  waiting for transfers between devices  35.7 us (35%)
  starting transfers between devices  35 us (34%)
  Pallas kernels  30.4 us (30%)
    ppermute x29, waiting for transfers between devices, crossed(): return lax.ppermute(block, axis, [(i, i ^ bits) for i in range(count)])  26.9 us
    ppermute x29, starting transfers between devices, crossed(): return lax.ppermute(block, axis, [(i, i ^ bits) for i in range(count)])  24.8 us
    pallas_call x2, Pallas kernels, attend(): pl.pallas_call(kernel, out_shape=jax.ShapeDtypeStruct((rows, 2 * COLS), j...  15.7 us
    ppermute x3, starting transfers between devices, shifted(): return lax.ppermute(block, axis, route)  10.1 us
    ppermute x3, waiting for transfers between devices, shifted(): return lax.ppermute(block, axis, route)  8.73 us
    pallas_call x1, Pallas kernels, project_out(): pl.pallas_call(mixed_kernel, grid=(width // cols,), out_shape=jax.ShapeDt...  4.76 us
    pallas_call x1, Pallas kernels, conv_silu(): pl.pallas_call(conv_kernel, out_shape=jax.ShapeDtypeStruct((2 * rows, wid...  4.07 us
    pallas_call x2, Pallas kernels, sliced(): pl.pallas_call(kernel, out_shape=out_shape, in_specs=[anywhere] * len(blo...  2.71 us
  transfers between devices with their start and end apart: 32, of which 16 were waited for; matrix products, arithmetic and copies ran while one was open for 0% of the time, Pallas kernels for 30%

profile of v4, /device:TPU:0, one launch (start us, length us, event | category | flops | bytes accessed | tf_op | source)
XLA Modules:
  0.0 103.0 jit_solution(12958966455817661692)
XLA Ops:
  1.2 1.3 %first_slice.1._ = bf16[2,768,384]{2,1,0:T(8,128)(2,1)S(1)} custom-call(bf16[1536,1152]{1,0:T(8,128)(2,1)} %refs_2_.3), custom_call_target="tpu_custom_call" | custom-call | flops 1000000 | bytes 10000 | tf_op jit(solution)/shard_map/first_slice/pallas_call | solution.py:178
  2.5 2.7 %collective-permute-start.5 = (bf16[2,768,384]{2,1,0:T(8,128)(2,1)S(1)}, bf16[2,768,384]{2,1,0:T(8,128)(2,1)S(1)}, u32[]{:S(2)}, u32[]{:S(2)}) collective-permute-start(bf16[2,768,384]{2,1,0:T(8,128)(2,1)S(1)} %first_slice.1._), channel_id=1, source_target_pairs={{0,16},{8,24},{16,0},{24,8},{1,17},{9,25},{17,1},{25,9},{2,18},{10... | collective-permute-start | bytes 3538952 | tf_op jit(solution)/shard_map/ppermute | solution.py:44
  5.2 3.4 %collective-permute-start.1 = (bf16[256,1536]{1,0:T(8,128)(2,1)S(1)}, bf16[256,1536]{1,0:T(8,128)(2,1)S(1)}, u32[]{:S(2)}, u32[]{:S(2)}) collective-permute-start(bf16[256,1536]{1,0:T(8,128)(2,1)S(1)} %copy-done), channel_id=1, source_target_pairs={{0,1},{1,2},{2,3},{3,4},{4,5},{5,6},{6,7},{8,9},{9,10},{10,11},{11... | collective-permute-start | bytes 2359304 | tf_op jit(solution)/shard_map/ppermute | solution.py:39
  8.6 1.4 %later_slices.1 = (bf16[768,384]{1,0:T(8,128)(2,1)S(1)}, bf16[256,384]{1,0:T(8,128)(2,1)S(1)}, bf16[256,384]{1,0:T(8,128)(2,1)S(1)}, bf16[2,256,384]{2,1,0:T(8,128)(2,1)S(1)}) custom-call(bf16[1536,1152]{1,0:T(8,128)(2,1)} %refs_2_.3, bf16[256,1536]{1,0:T(8,128)(2,1)} %cot_ref.1, bf16[2,768,384]{2,1,0:T(8,128)(2,1)S(1)} %first_slice.1._), custom_call_target="tpu_custom_call" | custom-call | flops 1000000 | bytes 10000 | tf_op jit(solution)/shard_map/later_slices/pallas_call | solution.py:178
  10.1 1.3 %collective-permute-start.3 = (bf16[16,1536]{1,0:T(8,128)(2,1)S(1)}, bf16[16,1536]{1,0:T(8,128)(2,1)S(1)}, u32[]{:S(2)}, u32[]{:S(2)}) collective-permute-start(bf16[16,1536]{1,0:T(8,128)(2,1)S(1)} %get-tuple-element.52), channel_id=1, source_target_pairs={{1,0},{2,1},{3,2},{4,3},{5,4},{6,5},{7,6},{9,8},{10,9},{11,10},{12... | collective-permute-start | bytes 147464 | tf_op jit(solution)/shard_map/ppermute | solution.py:39
  11.5 5.4 %collective-permute-start = (bf16[16,1536]{1,0:T(8,128)(2,1)S(1)}, bf16[16,1536]{1,0:T(8,128)(2,1)S(1)}, u32[]{:S(2)}, u32[]{:S(2)}) collective-permute-start(bf16[16,1536]{1,0:T(8,128)(2,1)S(1)} %get-tuple-element.53), channel_id=1, source_target_pairs={{0,2},{1,3},{2,4},{3,5},{4,6},{5,7},{8,10},{9,11},{10,12},{11,13},... | collective-permute-start | bytes 147464 | tf_op jit(solution)/shard_map/ppermute | solution.py:39
  17.0 1.0 %masks.1 = (f32[512,128]{1,0:T(8,128)S(1)}, f32[256,512]{1,0:T(8,128)S(1)}) custom-call(s32[1,8]{1,0:T(1,128)S(1)} %copy-done.3, s32[1,2048]{1,0:T(1,128)S(1)} %copy-done.2), custom_call_target="tpu_custom_call" | custom-call | flops 1000000 | bytes 10000 | tf_op jit(solution)/shard_map/masks/pallas_call | solution.py:83
  18.7 8.1 %collective-permute-done.1.prev_ref = bf16[256,1536]{1,0:T(8,128)(2,1)S(1)} collective-permute-done((bf16[256,1536]{1,0:T(8,128)(2,1)S(1)}, bf16[256,1536]{1,0:T(8,128)(2,1)S(1)}, u32[]{:S(2)}, u32[]{:S(2)}) %collective-permute-start.1) | collective-permute-done | bytes 786464 | tf_op jit(solution)/shard_map/ppermute | solution.py:39
  26.7 4.1 %conv_silu.1.refs_0_ = bf16[512,1536]{1,0:T(8,128)(2,1)S(1)} custom-call(bf16[16,1536]{1,0:T(8,128)(2,1)S(1)} %collective-permute-done.far_ref, bf16[256,1536]{1,0:T(8,128)(2,1)S(1)} %collective-permute-done.1.prev_ref, bf16[256,1536]{1,0:T(8,128)(2,1)S(1)} %copy-done, bf16[16,1536]{1,0:T(8,128)(2,1)S(1)} %collective-permute-done.3.next_ref, ...), custom_call_target="tpu_custom_call" | custom-call | flops 1000000 | bytes 10000 | tf_op jit(solution)/shard_map/conv_silu/pallas_call | solution.py:132
  31.9 2.6 %collective-permute-start.7 = (bf16[2,384,384]{2,1,0:T(8,128)(2,1)S(1)}, bf16[2,384,384]{2,1,0:T(8,128)(2,1)S(1)}, u32[]{:S(2)}, u32[]{:S(2)}) collective-permute-start(bf16[2,384,384]{2,1,0:T(8,128)(2,1)S(1)} %get-tuple-element.50), channel_id=1, source_target_pairs={{0,2},{1,3},{2,0},{3,1},{4,6},{5,7},{6,4},{7,5},{8,10},{9,11},{10,... | collective-permute-start | bytes 1769480 | tf_op jit(solution)/shard_map/ppermute | solution.py:44
  35.2 1.5 %collective-permute-start.11 = (bf16[768,384]{1,0:T(8,128)(2,1)S(1)}, bf16[768,384]{1,0:T(8,128)(2,1)S(1)}, u32[]{:S(2)}, u32[]{:S(2)}) collective-permute-start(bf16[768,384]{1,0:T(8,128)(2,1)S(1)} %get-tuple-element.33), channel_id=1, source_target_pairs={{0,16},{8,24},{16,0},{24,8},{1,17},{9,25},{17,1},{25,9},{2,18},{10... | collective-permute-start | bytes 1769480 | tf_op jit(solution)/shard_map/ppermute | solution.py:44
  36.8 11.3 %collective-permute-done.7.refs_6_ = bf16[2,384,384]{2,1,0:T(8,128)(2,1)S(1)} collective-permute-done((bf16[2,384,384]{2,1,0:T(8,128)(2,1)S(1)}, bf16[2,384,384]{2,1,0:T(8,128)(2,1)S(1)}, u32[]{:S(2)}, u32[]{:S(2)}) %collective-permute-start.7) | collective-permute-done | bytes 589856 | tf_op jit(solution)/shard_map/ppermute | solution.py:44
  48.1 1.5 %collective-permute-done.6.refs_5_ = bf16[2,384,384]{2,1,0:T(8,128)(2,1)S(1)} collective-permute-done((bf16[2,384,384]{2,1,0:T(8,128)(2,1)S(1)}, bf16[2,384,384]{2,1,0:T(8,128)(2,1)S(1)}, u32[]{:S(2)}, u32[]{:S(2)}) %collective-permute-start.6) | collective-permute-done | bytes 589856 | tf_op jit(solution)/shard_map/ppermute | solution.py:44
  49.5 1.4 %collective-permute-done.11.refs_10_ = bf16[768,384]{1,0:T(8,128)(2,1)S(1)} collective-permute-done((bf16[768,384]{1,0:T(8,128)(2,1)S(1)}, bf16[768,384]{1,0:T(8,128)(2,1)S(1)}, u32[]{:S(2)}, u32[]{:S(2)}) %collective-permute-start.11) | collective-permute-done | bytes 589856 | tf_op jit(solution)/shard_map/ppermute | solution.py:44
  51.0 1.5 %collective-permute-start.20 = (bf16[2,256,384]{2,1,0:T(8,128)(2,1)S(1)}, bf16[2,256,384]{2,1,0:T(8,128)(2,1)S(1)}, u32[]{:S(2)}, u32[]{:S(2)}) collective-permute-start(bf16[2,256,384]{2,1,0:T(8,128)(2,1)S(1)} %get-tuple-element.38), channel_id=1, source_target_pairs={{0,16},{8,24},{16,0},{24,8},{1,17},{9,25},{17,1},{25,9},{2,18},{10... | collective-permute-start | bytes 1179656 | tf_op jit(solution)/shard_map/ppermute | solution.py:44
  53.6 7.7 %attention_0.1.far_ref.refs_0_ = bf16[256,768]{1,0:T(8,128)(2,1)S(1)} custom-call(bf16[512,1536]{1,0:T(8,128)(2,1)S(1)} %conv_silu.1.refs_0_, f32[256,512]{1,0:T(8,128)S(1)} %get-tuple-element.30.refs_1_, bf16[1536,1152]{1,0:T(8,128)(2,1)} %refs_2_.3, bf16[1536,1152]{1,0:T(8,128)(2,1)S(1)} %collective-permute-done.4.refs_3_, ...), custom_call_target="tpu_custom_call" | custom-call | flops 1000000 | bytes 10000 | tf_op jit(solution)/shard_map/attention_0/pallas_call | solution.py:303
  61.7 1.5 %collective-permute-start.26 = (bf16[256,768]{1,0:T(8,128)(2,1)S(1)}, bf16[256,768]{1,0:T(8,128)(2,1)S(1)}, u32[]{:S(2)}, u32[]{:S(2)}) collective-permute-start(bf16[256,768]{1,0:T(8,128)(2,1)S(1)} %attention_0.1.far_ref.refs_0_), channel_id=1, source_target_pairs={{0,16},{8,24},{16,0},{24,8},{1,17},{9,25},{17,1},{25,9},{2,18},{10... | collective-permute-start | bytes 1179656 | tf_op jit(solution)/shard_map/ppermute | solution.py:44
  63.8 1.0 collective-permute-done.15.refs_14_
  65.3 8.0 %attention_1.1.near_ref.refs_0_ = bf16[256,768]{1,0:T(8,128)(2,1)S(1)} custom-call(bf16[512,1536]{1,0:T(8,128)(2,1)S(1)} %conv_silu.1.refs_0_, f32[256,512]{1,0:T(8,128)S(1)} %get-tuple-element.30.refs_1_, bf16[1536,1152]{1,0:T(8,128)(2,1)} %refs_2_.3, bf16[1536,1152]{1,0:T(8,128)(2,1)S(1)} %collective-permute-done.4.refs_3_, ...), custom_call_target="tpu_custom_call" | custom-call | flops 1000000 | bytes 10000 | tf_op jit(solution)/shard_map/attention_1/pallas_call | solution.py:303
  73.9 1.2 %collective-permute-start.18 = (bf16[256,768]{1,0:T(8,128)(2,1)S(1)}, bf16[256,768]{1,0:T(8,128)(2,1)S(1)}, u32[]{:S(2)}, u32[]{:S(2)}) collective-permute-start(bf16[256,768]{1,0:T(8,128)(2,1)S(1)} %attention_1.1.near_ref.refs_0_), channel_id=1, source_target_pairs={{0,16},{8,24},{16,0},{24,8},{1,17},{9,25},{17,1},{25,9},{2,18},{10... | collective-permute-start | bytes 1179656 | tf_op jit(solution)/shard_map/ppermute | solution.py:44
  75.6 1.1 %far.1 = (f32[192,384]{1,0:T(8,128)S(1)}, bf16[192,384]{1,0:T(8,128)(2,1)S(1)}, bf16[192,384]{1,0:T(8,128)(2,1)S(1)}, bf16[192,384]{1,0:T(8,128)(2,1)S(1)}) custom-call(bf16[256,768]{1,0:T(8,128)(2,1)S(1)} %attention_0.1.far_ref.refs_0_, bf16[256,768]{1,0:T(8,128)(2,1)S(1)} %collective-permute-done.25.refs_1_, ...), custom_call_target="tpu_custom_call" | custom-call | flops 1000000 | bytes 10000 | tf_op jit(solution)/shard_map/far/pallas_call | solution.py:368
  76.7 2.1 %collective-permute-start.28 = (bf16[192,384]{1,0:T(8,128)(2,1)S(1)}, bf16[192,384]{1,0:T(8,128)(2,1)S(1)}, u32[]{:S(2)}, u32[]{:S(2)}) collective-permute-start(bf16[192,384]{1,0:T(8,128)(2,1)S(1)} %get-tuple-element.47), channel_id=1, source_target_pairs={{0,3},{1,2},{2,1},{3,0},{4,7},{5,6},{6,5},{7,4},{8,11},{9,10},{10,... | collective-permute-start | bytes 442376 | tf_op jit(solution)/shard_map/ppermute | solution.py:44
  79.2 1.0 %collective-permute-start.30 = (bf16[192,384]{1,0:T(8,128)(2,1)S(1)}, bf16[192,384]{1,0:T(8,128)(2,1)S(1)}, u32[]{:S(2)}, u32[]{:S(2)}) collective-permute-start(bf16[192,384]{1,0:T(8,128)(2,1)S(1)} %get-tuple-element.49), channel_id=1, source_target_pairs={{0,1},{1,0},{2,3},{3,2},{4,5},{5,4},{6,7},{7,6},{8,9},{9,8},{10,11... | collective-permute-start | bytes 442376 | tf_op jit(solution)/shard_map/ppermute | solution.py:44
  80.3 4.9 %collective-permute-done.18.refs_2_ = bf16[256,768]{1,0:T(8,128)(2,1)S(1)} collective-permute-done((bf16[256,768]{1,0:T(8,128)(2,1)S(1)}, bf16[256,768]{1,0:T(8,128)(2,1)S(1)}, u32[]{:S(2)}, u32[]{:S(2)}) %collective-permute-start.18) | collective-permute-done | bytes 393248 | tf_op jit(solution)/shard_map/ppermute | solution.py:44
  85.2 1.2 %collective-permute-done.29 = bf16[192,384]{1,0:T(8,128)(2,1)S(1)} collective-permute-done((bf16[192,384]{1,0:T(8,128)(2,1)S(1)}, bf16[192,384]{1,0:T(8,128)(2,1)S(1)}, u32[]{:S(2)}, u32[]{:S(2)}) %collective-permute-start.29) | collective-permute-done | bytes 147488 | tf_op jit(solution)/shard_map/ppermute | solution.py:44
  87.0 3.1 %collective-permute-start.31 = (bf16[192,384]{1,0:T(8,128)(2,1)S(1)}, bf16[192,384]{1,0:T(8,128)(2,1)S(1)}, u32[]{:S(2)}, u32[]{:S(2)}) collective-permute-start(bf16[192,384]{1,0:T(8,128)(2,1)S(1)} %add_convert_fusion), channel_id=1, source_target_pairs={{0,4},{1,5},{2,6},{3,7},{4,0},{5,1},{6,2},{7,3},{8,12},{9,13},{10,... | collective-permute-start | bytes 442376 | tf_op jit(solution)/shard_map/ppermute | solution.py:44
  90.1 1.1 %near.1 = (f32[192,384]{1,0:T(8,128)S(1)}, bf16[192,384]{1,0:T(8,128)(2,1)S(1)}, bf16[192,384]{1,0:T(8,128)(2,1)S(1)}, bf16[192,384]{1,0:T(8,128)(2,1)S(1)}) custom-call(bf16[256,768]{1,0:T(8,128)(2,1)S(1)} %attention_1.1.near_ref.refs_0_, bf16[256,768]{1,0:T(8,128)(2,1)S(1)} %collective-permute-done.17.refs_1_, ...), custom_call_target="tpu_custom_call" | custom-call | flops 1000000 | bytes 10000 | tf_op jit(solution)/shard_map/near/pallas_call | solution.py:368
  91.2 1.9 %collective-permute-start.22 = (bf16[192,384]{1,0:T(8,128)(2,1)S(1)}, bf16[192,384]{1,0:T(8,128)(2,1)S(1)}, u32[]{:S(2)}, u32[]{:S(2)}) collective-permute-start(bf16[192,384]{1,0:T(8,128)(2,1)S(1)} %get-tuple-element.41), channel_id=1, source_target_pairs={{0,3},{1,2},{2,1},{3,0},{4,7},{5,6},{6,5},{7,4},{8,11},{9,10},{10,... | collective-permute-start | bytes 442376 | tf_op jit(solution)/shard_map/ppermute | solution.py:44
  93.5 1.3 %collective-permute-start.24 = (bf16[192,384]{1,0:T(8,128)(2,1)S(1)}, bf16[192,384]{1,0:T(8,128)(2,1)S(1)}, u32[]{:S(2)}, u32[]{:S(2)}) collective-permute-start(bf16[192,384]{1,0:T(8,128)(2,1)S(1)} %get-tuple-element.43), channel_id=1, source_target_pairs={{0,1},{1,0},{2,3},{3,2},{4,5},{5,4},{6,7},{7,6},{8,9},{9,8},{10,11... | collective-permute-start | bytes 442376 | tf_op jit(solution)/shard_map/ppermute | solution.py:44
  94.8 4.8 %mixed.1 = bf16[256,1536]{1,0:T(8,128)(2,1)} custom-call(bf16[256,768]{1,0:T(8,128)(2,1)S(1)} %attention_0.1.far_ref.refs_0_, bf16[256,768]{1,0:T(8,128)(2,1)S(1)} %attention_1.1.near_ref.refs_0_, bf16[1536,1536]{1,0:T(8,128)(2,1)} %w_ref.5), custom_call_target="tpu_custom_call" | custom-call | flops 1000000 | bytes 10000 | tf_op jit(solution)/shard_map/mixed/pallas_call | solution.py:333
  99.5 1.0 collective-permute-done.22
  100.5 1.6 %collective-permute-done.23 = bf16[192,384]{1,0:T(8,128)(2,1)S(1)} collective-permute-done((bf16[192,384]{1,0:T(8,128)(2,1)S(1)}, bf16[192,384]{1,0:T(8,128)(2,1)S(1)}, u32[]{:S(2)}, u32[]{:S(2)}) %collective-permute-start.23) | collective-permute-done | bytes 147488 | tf_op jit(solution)/shard_map/ppermute | solution.py:44
  (54 shorter events, 9.1 us)
Async XLA Ops:
  0.6 53.0 %collective-permute-start.4 = (bf16[1536,1152]{1,0:T(8,128)(2,1)}, bf16[1536,1152]{1,0:T(8,128)(2,1)S(1)}, u32[]{:S(2)}, u32[]{:S(2)}) collective-permute-start(bf16[1536,1152]{1,0:T(8,128)(2,1)} %refs_2_.3), channel_id=1, source_target_pairs={{0,8},{8,0},{16,24},{24,16},{1,9},{9,1},{17,25},{25,17},{2,10},{10... | collective-permute-start | bytes 10616840 | tf_op jit(solution)/shard_map/ppermute | solution.py:44
  2.5 29.2 %collective-permute-start.5 = (bf16[2,768,384]{2,1,0:T(8,128)(2,1)S(1)}, bf16[2,768,384]{2,1,0:T(8,128)(2,1)S(1)}, u32[]{:S(2)}, u32[]{:S(2)}) collective-permute-start(bf16[2,768,384]{2,1,0:T(8,128)(2,1)S(1)} %first_slice.1._), channel_id=1, source_target_pairs={{0,16},{8,24},{16,0},{24,8},{1,17},{9,25},{17,1},{25,9},{2,18},{10... | collective-permute-start | bytes 3538952 | tf_op jit(solution)/shard_map/ppermute | solution.py:44
  5.2 21.5 %collective-permute-start.1 = (bf16[256,1536]{1,0:T(8,128)(2,1)S(1)}, bf16[256,1536]{1,0:T(8,128)(2,1)S(1)}, u32[]{:S(2)}, u32[]{:S(2)}) collective-permute-start(bf16[256,1536]{1,0:T(8,128)(2,1)S(1)} %copy-done), channel_id=1, source_target_pairs={{0,1},{1,2},{2,3},{3,4},{4,5},{5,6},{6,7},{8,9},{9,10},{10,11},{11... | collective-permute-start | bytes 2359304 | tf_op jit(solution)/shard_map/ppermute | solution.py:39
  10.0 1.5 %collective-permute-start.2 = (bf16[256,384]{1,0:T(8,128)(2,1)S(1)}, bf16[256,384]{1,0:T(8,128)(2,1)S(1)}, u32[]{:S(2)}, u32[]{:S(2)}) collective-permute-start(bf16[256,384]{1,0:T(8,128)(2,1)S(1)} %get-tuple-element.26), channel_id=1, source_target_pairs={{0,8},{8,0},{16,24},{24,16},{1,9},{9,1},{17,25},{25,17},{2,10},{10... | collective-permute-start | bytes 589832 | tf_op jit(solution)/shard_map/ppermute | solution.py:44
  10.1 7.9 %collective-permute-start.3 = (bf16[16,1536]{1,0:T(8,128)(2,1)S(1)}, bf16[16,1536]{1,0:T(8,128)(2,1)S(1)}, u32[]{:S(2)}, u32[]{:S(2)}) collective-permute-start(bf16[16,1536]{1,0:T(8,128)(2,1)S(1)} %get-tuple-element.52), channel_id=1, source_target_pairs={{1,0},{2,1},{3,2},{4,3},{5,4},{6,5},{7,6},{9,8},{10,9},{11,10},{12... | collective-permute-start | bytes 147464 | tf_op jit(solution)/shard_map/ppermute | solution.py:39
  11.5 7.1 %collective-permute-start = (bf16[16,1536]{1,0:T(8,128)(2,1)S(1)}, bf16[16,1536]{1,0:T(8,128)(2,1)S(1)}, u32[]{:S(2)}, u32[]{:S(2)}) collective-permute-start(bf16[16,1536]{1,0:T(8,128)(2,1)S(1)} %get-tuple-element.53), channel_id=1, source_target_pairs={{0,2},{1,3},{2,4},{3,5},{4,6},{5,7},{8,10},{9,11},{10,12},{11,13},... | collective-permute-start | bytes 147464 | tf_op jit(solution)/shard_map/ppermute | solution.py:39
  31.9 16.2 %collective-permute-start.7 = (bf16[2,384,384]{2,1,0:T(8,128)(2,1)S(1)}, bf16[2,384,384]{2,1,0:T(8,128)(2,1)S(1)}, u32[]{:S(2)}, u32[]{:S(2)}) collective-permute-start(bf16[2,384,384]{2,1,0:T(8,128)(2,1)S(1)} %get-tuple-element.50), channel_id=1, source_target_pairs={{0,2},{1,3},{2,0},{3,1},{4,6},{5,7},{6,4},{7,5},{8,10},{9,11},{10,... | collective-permute-start | bytes 1769480 | tf_op jit(solution)/shard_map/ppermute | solution.py:44
  34.5 15.0 %collective-permute-start.6 = (bf16[2,384,384]{2,1,0:T(8,128)(2,1)S(1)}, bf16[2,384,384]{2,1,0:T(8,128)(2,1)S(1)}, u32[]{:S(2)}, u32[]{:S(2)}) collective-permute-start(bf16[2,384,384]{2,1,0:T(8,128)(2,1)S(1)} %get-tuple-element.51), channel_id=1, source_target_pairs={{0,1},{1,0},{2,3},{3,2},{4,5},{5,4},{6,7},{7,6},{8,9},{9,8},{10,11... | collective-permute-start | bytes 1769480 | tf_op jit(solution)/shard_map/ppermute | solution.py:44
  35.2 18.4 %collective-permute-start.8 = (bf16[2,768,384]{2,1,0:T(8,128)(2,1)S(1)}, bf16[2,768,384]{2,1,0:T(8,128)(2,1)S(1)}, u32[]{:S(2)}, u32[]{:S(2)}) collective-permute-start(bf16[2,768,384]{2,1,0:T(8,128)(2,1)S(1)} %collective-permute-done.5.refs_4_), channel_id=1, source_target_pairs={{0,8},{8,0},{16,24},{24,16},{1,9},{9,1},{17,25},{25,17},{2,10},{10... | collective-permute-start | bytes 3538952 | tf_op jit(solution)/shard_map/ppermute | solution.py:44
  35.2 15.7 %collective-permute-start.11 = (bf16[768,384]{1,0:T(8,128)(2,1)S(1)}, bf16[768,384]{1,0:T(8,128)(2,1)S(1)}, u32[]{:S(2)}, u32[]{:S(2)}) collective-permute-start(bf16[768,384]{1,0:T(8,128)(2,1)S(1)} %get-tuple-element.33), channel_id=1, source_target_pairs={{0,16},{8,24},{16,0},{24,8},{1,17},{9,25},{17,1},{25,9},{2,18},{10... | collective-permute-start | bytes 1769480 | tf_op jit(solution)/shard_map/ppermute | solution.py:44
  48.1 4.5 %collective-permute-start.10 = (bf16[2,384,384]{2,1,0:T(8,128)(2,1)S(1)}, bf16[2,384,384]{2,1,0:T(8,128)(2,1)S(1)}, u32[]{:S(2)}, u32[]{:S(2)}) collective-permute-start(bf16[2,384,384]{2,1,0:T(8,128)(2,1)S(1)} %collective-permute-done.7.refs_6_), channel_id=1, source_target_pairs={{0,8},{8,0},{16,24},{24,16},{1,9},{9,1},{17,25},{25,17},{2,10},{10... | collective-permute-start | bytes 1769480 | tf_op jit(solution)/shard_map/ppermute | solution.py:44
  49.5 3.6 %collective-permute-start.9 = (bf16[2,384,384]{2,1,0:T(8,128)(2,1)S(1)}, bf16[2,384,384]{2,1,0:T(8,128)(2,1)S(1)}, u32[]{:S(2)}, u32[]{:S(2)}) collective-permute-start(bf16[2,384,384]{2,1,0:T(8,128)(2,1)S(1)} %collective-permute-done.6.refs_5_), channel_id=1, source_target_pairs={{0,8},{8,0},{16,24},{24,16},{1,9},{9,1},{17,25},{25,17},{2,10},{10... | collective-permute-start | bytes 1769480 | tf_op jit(solution)/shard_map/ppermute | solution.py:44
  51.0 10.7 %collective-permute-start.20 = (bf16[2,256,384]{2,1,0:T(8,128)(2,1)S(1)}, bf16[2,256,384]{2,1,0:T(8,128)(2,1)S(1)}, u32[]{:S(2)}, u32[]{:S(2)}) collective-permute-start(bf16[2,256,384]{2,1,0:T(8,128)(2,1)S(1)} %get-tuple-element.38), channel_id=1, source_target_pairs={{0,16},{8,24},{16,0},{24,8},{1,17},{9,25},{17,1},{25,9},{2,18},{10... | collective-permute-start | bytes 1179656 | tf_op jit(solution)/shard_map/ppermute | solution.py:44
  52.6 10.7 %collective-permute-start.13 = (bf16[384,384]{1,0:T(8,128)(2,1)S(1)}, bf16[384,384]{1,0:T(8,128)(2,1)S(1)}, u32[]{:S(2)}, u32[]{:S(2)}) collective-permute-start(bf16[384,384]{1,0:T(8,128)(2,1)S(1)} %get-tuple-element.54), channel_id=1, source_target_pairs={{0,2},{1,3},{2,0},{3,1},{4,6},{5,7},{6,4},{7,5},{8,10},{9,11},{10,... | collective-permute-start | bytes 884744 | tf_op jit(solution)/shard_map/ppermute | solution.py:44
  53.1 10.2 %collective-permute-start.12 = (bf16[384,384]{1,0:T(8,128)(2,1)S(1)}, bf16[384,384]{1,0:T(8,128)(2,1)S(1)}, u32[]{:S(2)}, u32[]{:S(2)}) collective-permute-start(bf16[384,384]{1,0:T(8,128)(2,1)S(1)} %get-tuple-element.55), channel_id=1, source_target_pairs={{0,1},{1,0},{2,3},{3,2},{4,5},{5,4},{6,7},{7,6},{8,9},{9,8},{10,11... | collective-permute-start | bytes 884744 | tf_op jit(solution)/shard_map/ppermute | solution.py:44
  53.6 10.2 %collective-permute-start.14 = (bf16[768,384]{1,0:T(8,128)(2,1)S(1)}, bf16[768,384]{1,0:T(8,128)(2,1)S(1)}, u32[]{:S(2)}, u32[]{:S(2)}) collective-permute-start(bf16[768,384]{1,0:T(8,128)(2,1)S(1)} %collective-permute-done.11.refs_10_), channel_id=1, source_target_pairs={{0,8},{8,0},{16,24},{24,16},{1,9},{9,1},{17,25},{25,17},{2,10},{10... | collective-permute-start | bytes 1769480 | tf_op jit(solution)/shard_map/ppermute | solution.py:44
  61.7 12.0 %collective-permute-start.26 = (bf16[256,768]{1,0:T(8,128)(2,1)S(1)}, bf16[256,768]{1,0:T(8,128)(2,1)S(1)}, u32[]{:S(2)}, u32[]{:S(2)}) collective-permute-start(bf16[256,768]{1,0:T(8,128)(2,1)S(1)} %attention_0.1.far_ref.refs_0_), channel_id=1, source_target_pairs={{0,16},{8,24},{16,0},{24,8},{1,17},{9,25},{17,1},{25,9},{2,18},{10... | collective-permute-start | bytes 1179656 | tf_op jit(solution)/shard_map/ppermute | solution.py:44
  63.3 1.6 %collective-permute-start.15 = (bf16[384,384]{1,0:T(8,128)(2,1)S(1)}, bf16[384,384]{1,0:T(8,128)(2,1)S(1)}, u32[]{:S(2)}, u32[]{:S(2)}) collective-permute-start(bf16[384,384]{1,0:T(8,128)(2,1)S(1)} %collective-permute-done.12.refs_11_), channel_id=1, source_target_pairs={{0,8},{8,0},{16,24},{24,16},{1,9},{9,1},{17,25},{25,17},{2,10},{10... | collective-permute-start | bytes 884744 | tf_op jit(solution)/shard_map/ppermute | solution.py:44
  63.3 2.0 %collective-permute-start.16 = (bf16[384,384]{1,0:T(8,128)(2,1)S(1)}, bf16[384,384]{1,0:T(8,128)(2,1)S(1)}, u32[]{:S(2)}, u32[]{:S(2)}) collective-permute-start(bf16[384,384]{1,0:T(8,128)(2,1)S(1)} %collective-permute-done.13.refs_12_), channel_id=1, source_target_pairs={{0,8},{8,0},{16,24},{24,16},{1,9},{9,1},{17,25},{25,17},{2,10},{10... | collective-permute-start | bytes 884744 | tf_op jit(solution)/shard_map/ppermute | solution.py:44
  63.8 11.3 %collective-permute-start.25 = (bf16[256,768]{1,0:T(8,128)(2,1)S(1)}, bf16[256,768]{1,0:T(8,128)(2,1)S(1)}, u32[]{:S(2)}, u32[]{:S(2)}) collective-permute-start(bf16[256,768]{1,0:T(8,128)(2,1)S(1)} %attention_0.1.far_ref.refs_0_), channel_id=1, source_target_pairs={{0,8},{8,0},{16,24},{24,16},{1,9},{9,1},{17,25},{25,17},{2,10},{10... | collective-permute-start | bytes 1179656 | tf_op jit(solution)/shard_map/ppermute | solution.py:44
  73.3 1.8 %collective-permute-start.21 = (bf16[2,256,384]{2,1,0:T(8,128)(2,1)S(1)}, bf16[2,256,384]{2,1,0:T(8,128)(2,1)S(1)}, u32[]{:S(2)}, u32[]{:S(2)}) collective-permute-start(bf16[2,256,384]{2,1,0:T(8,128)(2,1)S(1)} %collective-permute-done.20.refs_6_), channel_id=1, source_target_pairs={{0,8},{8,0},{16,24},{24,16},{1,9},{9,1},{17,25},{25,17},{2,10},{10... | collective-permute-start | bytes 1179656 | tf_op jit(solution)/shard_map/ppermute | solution.py:44
  73.7 1.9 %collective-permute-start.27 = (bf16[256,768]{1,0:T(8,128)(2,1)S(1)}, bf16[256,768]{1,0:T(8,128)(2,1)S(1)}, u32[]{:S(2)}, u32[]{:S(2)}) collective-permute-start(bf16[256,768]{1,0:T(8,128)(2,1)S(1)} %collective-permute-done.26.refs_2_), channel_id=1, source_target_pairs={{0,8},{8,0},{16,24},{24,16},{1,9},{9,1},{17,25},{25,17},{2,10},{10... | collective-permute-start | bytes 1179656 | tf_op jit(solution)/shard_map/ppermute | solution.py:44
  73.9 11.4 %collective-permute-start.18 = (bf16[256,768]{1,0:T(8,128)(2,1)S(1)}, bf16[256,768]{1,0:T(8,128)(2,1)S(1)}, u32[]{:S(2)}, u32[]{:S(2)}) collective-permute-start(bf16[256,768]{1,0:T(8,128)(2,1)S(1)} %attention_1.1.near_ref.refs_0_), channel_id=1, source_target_pairs={{0,16},{8,24},{16,0},{24,8},{1,17},{9,25},{17,1},{25,9},{2,18},{10... | collective-permute-start | bytes 1179656 | tf_op jit(solution)/shard_map/ppermute | solution.py:44
  76.7 8.5 %collective-permute-start.28 = (bf16[192,384]{1,0:T(8,128)(2,1)S(1)}, bf16[192,384]{1,0:T(8,128)(2,1)S(1)}, u32[]{:S(2)}, u32[]{:S(2)}) collective-permute-start(bf16[192,384]{1,0:T(8,128)(2,1)S(1)} %get-tuple-element.47), channel_id=1, source_target_pairs={{0,3},{1,2},{2,1},{3,0},{4,7},{5,6},{6,5},{7,4},{8,11},{9,10},{10,... | collective-permute-start | bytes 442376 | tf_op jit(solution)/shard_map/ppermute | solution.py:44
  78.8 7.6 %collective-permute-start.29 = (bf16[192,384]{1,0:T(8,128)(2,1)S(1)}, bf16[192,384]{1,0:T(8,128)(2,1)S(1)}, u32[]{:S(2)}, u32[]{:S(2)}) collective-permute-start(bf16[192,384]{1,0:T(8,128)(2,1)S(1)} %get-tuple-element.48), channel_id=1, source_target_pairs={{0,2},{1,3},{2,0},{3,1},{4,6},{5,7},{6,4},{7,5},{8,10},{9,11},{10,... | collective-permute-start | bytes 442376 | tf_op jit(solution)/shard_map/ppermute | solution.py:44
  79.2 7.7 %collective-permute-start.30 = (bf16[192,384]{1,0:T(8,128)(2,1)S(1)}, bf16[192,384]{1,0:T(8,128)(2,1)S(1)}, u32[]{:S(2)}, u32[]{:S(2)}) collective-permute-start(bf16[192,384]{1,0:T(8,128)(2,1)S(1)} %get-tuple-element.49), channel_id=1, source_target_pairs={{0,1},{1,0},{2,3},{3,2},{4,5},{5,4},{6,7},{7,6},{8,9},{9,8},{10,11... | collective-permute-start | bytes 442376 | tf_op jit(solution)/shard_map/ppermute | solution.py:44
  80.3 9.9 %collective-permute-start.17 = (bf16[256,768]{1,0:T(8,128)(2,1)S(1)}, bf16[256,768]{1,0:T(8,128)(2,1)S(1)}, u32[]{:S(2)}, u32[]{:S(2)}) collective-permute-start(bf16[256,768]{1,0:T(8,128)(2,1)S(1)} %attention_1.1.near_ref.refs_0_), channel_id=1, source_target_pairs={{0,8},{8,0},{16,24},{24,16},{1,9},{9,1},{17,25},{25,17},{2,10},{10... | collective-permute-start | bytes 1179656 | tf_op jit(solution)/shard_map/ppermute | solution.py:44
  85.2 4.9 %collective-permute-start.19 = (bf16[256,768]{1,0:T(8,128)(2,1)S(1)}, bf16[256,768]{1,0:T(8,128)(2,1)S(1)}, u32[]{:S(2)}, u32[]{:S(2)}) collective-permute-start(bf16[256,768]{1,0:T(8,128)(2,1)S(1)} %collective-permute-done.18.refs_2_), channel_id=1, source_target_pairs={{0,8},{8,0},{16,24},{24,16},{1,9},{9,1},{17,25},{25,17},{2,10},{10... | collective-permute-start | bytes 1179656 | tf_op jit(solution)/shard_map/ppermute | solution.py:44
  87.0 12.5 %collective-permute-start.31 = (bf16[192,384]{1,0:T(8,128)(2,1)S(1)}, bf16[192,384]{1,0:T(8,128)(2,1)S(1)}, u32[]{:S(2)}, u32[]{:S(2)}) collective-permute-start(bf16[192,384]{1,0:T(8,128)(2,1)S(1)} %add_convert_fusion), channel_id=1, source_target_pairs={{0,4},{1,5},{2,6},{3,7},{4,0},{5,1},{6,2},{7,3},{8,12},{9,13},{10,... | collective-permute-start | bytes 442376 | tf_op jit(solution)/shard_map/ppermute | solution.py:44
  91.2 9.3 %collective-permute-start.22 = (bf16[192,384]{1,0:T(8,128)(2,1)S(1)}, bf16[192,384]{1,0:T(8,128)(2,1)S(1)}, u32[]{:S(2)}, u32[]{:S(2)}) collective-permute-start(bf16[192,384]{1,0:T(8,128)(2,1)S(1)} %get-tuple-element.41), channel_id=1, source_target_pairs={{0,3},{1,2},{2,1},{3,0},{4,7},{5,6},{6,5},{7,4},{8,11},{9,10},{10,... | collective-permute-start | bytes 442376 | tf_op jit(solution)/shard_map/ppermute | solution.py:44
  93.1 9.0 %collective-permute-start.23 = (bf16[192,384]{1,0:T(8,128)(2,1)S(1)}, bf16[192,384]{1,0:T(8,128)(2,1)S(1)}, u32[]{:S(2)}, u32[]{:S(2)}) collective-permute-start(bf16[192,384]{1,0:T(8,128)(2,1)S(1)} %get-tuple-element.42), channel_id=1, source_target_pairs={{0,2},{1,3},{2,0},{3,1},{4,6},{5,7},{6,4},{7,5},{8,10},{9,11},{10,... | collective-permute-start | bytes 442376 | tf_op jit(solution)/shard_map/ppermute | solution.py:44
  93.5 8.7 %collective-permute-start.24 = (bf16[192,384]{1,0:T(8,128)(2,1)S(1)}, bf16[192,384]{1,0:T(8,128)(2,1)S(1)}, u32[]{:S(2)}, u32[]{:S(2)}) collective-permute-start(bf16[192,384]{1,0:T(8,128)(2,1)S(1)} %get-tuple-element.43), channel_id=1, source_target_pairs={{0,1},{1,0},{2,3},{3,2},{4,5},{5,4},{6,7},{7,6},{8,9},{9,8},{10,11... | collective-permute-start | bytes 442376 | tf_op jit(solution)/shard_map/ppermute | solution.py:44
  (4 other events, 57.7 us)
